TPU v7x, 32 devices: a whole 2x2x4 slice. The times are simulated.
32 devices in a mesh: ctx: 8 (over z, x), tp: 4 (over y, core).
Axes of the slice: x: 2, y: 2, z: 4, core: 2. Of those that a mesh axis runs over, the one named last changes fastest.
Arguments:
- tokens: bfloat16 [2, 2048, 2048], P(None, 'ctx'), may hold values from -6 to 6
- pair_index: int32 [2, 8], replicated, may hold values from 0 to 7, each once within a row
- norm_gain: bfloat16 [2048], P('ctx'), may hold values from 0.5 to 1.5
- norm_shift: bfloat16 [2048], P('ctx'), may hold values from -3 to 3
- w_attention_in: bfloat16 [3, 2048, 2048], P(None, 'ctx', 'tp'), may hold values from -0.1875 to 0.1875
- w_attention_out: bfloat16 [2048, 2048], P('tp', 'ctx'), may hold values from -0.5 to 0.5
- w_expand: bfloat16 [2048, 8192], P('ctx', 'tp'), may hold values from -0.125 to 0.125
- w_contract: bfloat16 [8192, 2048], P('tp', 'ctx'), may hold values from -0.09375 to 0.09375
- cotangent: bfloat16 [2, 2048, 2048], P(None, 'ctx'), may hold values from -6 to 6
Outputs:
- output: bfloat16 [2, 2048, 2048], P(None, 'ctx')
- input_grad: float32 [2, 2048, 2048], P(None, 'ctx')
- gain_grad: float32 [2048], P('ctx')
- shift_grad: float32 [2048], P('ctx')
- attention_in_grad: float32 [3, 2048, 2048], P(None, 'ctx', 'tp')
- attention_out_grad: float32 [2048, 2048], P('tp', 'ctx')
- expand_grad: float32 [2048, 8192], P('ctx', 'tp')
- contract_grad: float32 [8192, 2048], P('tp', 'ctx')
Inputs may be any that keep to these rules, and one draw needn't show every extreme that they name: Each row is a permutation: context index c holds blocks pair_index[s, c] and 2 P - 1 - pair_index[s, c] of sequence s, each of 128 tokens, with P = 8.
All inputs are finite; a program needn't handle non-finite values.
Results may differ from a plain program's by a relative error of at most 0.023.
Values may be sent and summed in bfloat16 or wider, within the bound.
A program may use at most 320 MiB of HBM per device.

v0:
```python
import jax
import jax.numpy as jnp
from jax import lax
from jax.sharding import PartitionSpec as P

HEAD_DIM = 64
ROT = 32


epsilon = 1e-05


def position_table(pair_index, shard_rows):
    pair_count = pair_index.shape[1]
    half_rows = shard_rows // 2
    token_index = jnp.arange(shard_rows * pair_count, dtype=jnp.int32)
    owning = token_index // shard_rows
    within = token_index % shard_rows
    picked = (owning[:, None] == jnp.arange(pair_count, dtype=jnp.int32)[None, :]).astype(jnp.int32)
    chosen = jnp.sum(picked[None, :, :] * pair_index[:, None, :], axis=2)
    first_half = chosen * half_rows + within[None, :]
    second = (2 * pair_count - 1 - chosen) * half_rows + within[None, :] - half_rows
    return jnp.where(within[None, :] < half_rows, first_half, second)


def rotate(tensor, positions):
    half_rot = ROT // 2
    frequency = 10000.0 ** (-2.0 * jnp.arange(half_rot, dtype=jnp.float32) / ROT)
    angles = positions.astype(jnp.float32)[..., None] * frequency
    cosine = jnp.cos(angles)[..., None, :]
    sine_part = jnp.sin(angles)[..., None, :]
    leading = tensor[..., :half_rot]
    trailing = tensor[..., half_rot:ROT]
    return jnp.concatenate(
        [
            leading * cosine - trailing * sine_part,
            trailing * cosine + leading * sine_part,
            tensor[..., ROT:],
        ],
        axis=-1,
    )


def gelu_tanh(values_in):
    return (
        0.5
        * values_in
        * (
            1.0
            + jnp.tanh(
                0.7978845608028654 * (values_in + 0.044715 * values_in * values_in * values_in)
            )
        )
    )


def layer_norm(inputs, gain_full, shift_full):
    centred = inputs - jnp.mean(inputs, axis=-1, keepdims=True)
    spread = jnp.mean(centred * centred, axis=-1, keepdims=True)
    return centred * lax.rsqrt(spread + epsilon) * gain_full + shift_full


def block_probs(queries, keys_block, log_total, query_pos, key_pos):
    raw_scores = jnp.einsum(
        "sqhe,skhe->shqk", queries, keys_block, preferred_element_type=jnp.float32
    )
    allowed = key_pos[:, None, None, :] <= query_pos[:, None, :, None]
    return jnp.where(allowed, jnp.exp(raw_scores * HEAD_DIM ** (-0.5) - log_total[..., None]), 0.0)


def score_grads(
    queries, keys_block, values_block, log_total, row_delta, out_grad, query_pos, key_pos
):
    probs_full = block_probs(queries, keys_block, log_total, query_pos, key_pos)
    prob_grad = jnp.einsum(
        "sqhe,skhe->shqk", out_grad, values_block, preferred_element_type=jnp.float32
    )
    score_grad = (probs_full * (prob_grad - row_delta[..., None]) * HEAD_DIM ** (-0.5)).astype(
        jnp.bfloat16
    )
    return (probs_full.astype(jnp.bfloat16), score_grad)


def key_slice(keys_all, offset, key_rows, head_count):
    seq_count = keys_all.shape[0]
    return lax.dynamic_slice_in_dim(keys_all, offset, key_rows, 1).reshape(
        seq_count, key_rows, head_count, HEAD_DIM
    )


def log_totals(queries, keys_all, query_pos, pos_table, key_rows):
    seq_count, query_rows, head_count, head_size = queries.shape
    turn_count = keys_all.shape[1] // key_rows

    def log_one_turn(turn_index, state_in):
        running_max, running_sum = state_in
        offset = turn_index * key_rows
        keys_block = key_slice(keys_all, offset, key_rows, head_count)
        key_pos = lax.dynamic_slice_in_dim(pos_table, offset, key_rows, 1)
        raw_scores = jnp.einsum(
            "sqhe,skhe->shqk", queries, keys_block, preferred_element_type=jnp.float32
        ) * HEAD_DIM ** (-0.5)
        allowed = key_pos[:, None, None, :] <= query_pos[:, None, :, None]
        masked = jnp.where(allowed, raw_scores, -1e30)
        new_max = jnp.maximum(running_max, jnp.max(masked, axis=-1))
        kept_terms = jnp.where(allowed, jnp.exp(masked - new_max[..., None]), 0.0)
        return (
            new_max,
            running_sum * jnp.exp(running_max - new_max) + jnp.sum(kept_terms, axis=-1),
        )

    initial = (
        jnp.full((seq_count, head_count, query_rows), -1e30, jnp.float32),
        jnp.zeros((seq_count, head_count, query_rows), jnp.float32),
    )
    final_max, final_sum = lax.fori_loop(0, turn_count, log_one_turn, initial)
    return final_max + jnp.log(final_sum)


def attend_values(queries, keys_all, values_all, log_total, query_pos, pos_table, key_rows):
    head_count = queries.shape[2]
    turn_count = keys_all.shape[1] // key_rows

    def attend_one_turn(turn_index, running):
        offset = turn_index * key_rows
        keys_block = key_slice(keys_all, offset, key_rows, head_count)
        values_block = key_slice(values_all, offset, key_rows, head_count)
        key_pos = lax.dynamic_slice_in_dim(pos_table, offset, key_rows, 1)
        weights_low = block_probs(queries, keys_block, log_total, query_pos, key_pos).astype(
            jnp.bfloat16
        )
        return running + jnp.einsum(
            "shqk,skhe->sqhe", weights_low, values_block, preferred_element_type=jnp.float32
        )

    return lax.fori_loop(0, turn_count, attend_one_turn, jnp.zeros(queries.shape, jnp.float32))


def full_grads(
    queries, keys_all, values_all, log_total, row_delta, out_grad, query_pos, pos_table, key_rows
):
    seq_count, query_rows, head_count, head_size = queries.shape
    turn_count = keys_all.shape[1] // key_rows

    def full_one_turn(turn_index, state_in):
        query_grad, key_terms, value_terms = state_in
        offset = turn_index * key_rows
        keys_block = key_slice(keys_all, offset, key_rows, head_count)
        values_block = key_slice(values_all, offset, key_rows, head_count)
        key_pos = lax.dynamic_slice_in_dim(pos_table, offset, key_rows, 1)
        weights_low, score_grad = score_grads(
            queries, keys_block, values_block, log_total, row_delta, out_grad, query_pos, key_pos
        )
        query_grad = query_grad + jnp.einsum(
            "shqk,skhe->sqhe", score_grad, keys_block, preferred_element_type=jnp.float32
        )
        key_part = jnp.einsum(
            "shqk,sqhe->skhe", score_grad, queries, preferred_element_type=jnp.float32
        ).reshape(seq_count, key_rows, head_count * head_size)
        value_part = jnp.einsum(
            "shqk,sqhe->skhe", weights_low, out_grad, preferred_element_type=jnp.float32
        ).reshape(seq_count, key_rows, head_count * head_size)
        key_terms = lax.dynamic_update_slice_in_dim(key_terms, key_part, offset, 1)
        value_terms = lax.dynamic_update_slice_in_dim(value_terms, value_part, offset, 1)
        return (query_grad, key_terms, value_terms)

    initial = (
        jnp.zeros(queries.shape, jnp.float32),
        jnp.zeros(keys_all.shape, jnp.float32),
        jnp.zeros(values_all.shape, jnp.float32),
    )
    return lax.fori_loop(0, turn_count, full_one_turn, initial)


def local(
    tokens,
    pair_index,
    norm_gain,
    norm_shift,
    w_attention_in,
    w_attention_out,
    w_expand,
    w_contract,
    cotangent,
):
    seq_count, shard_rows, model_width = tokens.shape
    gain_full, shift_full, attention_in, attention_out, expand_full, contract_full = (
        lax.all_gather(norm_gain, "ctx", axis=0, tiled=True),
        lax.all_gather(norm_shift, "ctx", axis=0, tiled=True),
        lax.all_gather(w_attention_in, "ctx", axis=1, tiled=True),
        lax.all_gather(w_attention_out, "ctx", axis=1, tiled=True),
        lax.all_gather(w_expand, "ctx", axis=0, tiled=True),
        lax.all_gather(w_contract, "ctx", axis=1, tiled=True),
    )
    local_width = attention_in.shape[2]
    head_count = local_width // HEAD_DIM
    flat_rows = seq_count * shard_rows
    pos_table = position_table(pair_index, shard_rows)
    total_rows = pos_table.shape[1]
    own_pos = lax.dynamic_slice_in_dim(pos_table, lax.axis_index("ctx") * shard_rows, shard_rows, 1)
    key_rows = min(total_rows, 1024)
    inputs = tokens.astype(jnp.float32)
    normed_full, norm_pull = jax.vjp(
        layer_norm, inputs, gain_full.astype(jnp.float32), shift_full.astype(jnp.float32)
    )
    normed = normed_full.astype(jnp.bfloat16).reshape(flat_rows, model_width)
    projected = jnp.einsum("td,kde->kte", normed, attention_in, preferred_element_type=jnp.float32)
    split_heads = projected.reshape(3, seq_count, shard_rows, head_count, HEAD_DIM)
    rotated, rotate_pull = jax.vjp(lambda pair_part: rotate(pair_part, own_pos), split_heads[:2])
    queries = rotated[0].astype(jnp.bfloat16)
    own_keys = rotated[1].astype(jnp.bfloat16)
    own_values = split_heads[2].astype(jnp.bfloat16)
    keys_all, values_all = (
        lax.all_gather(
            own_keys.reshape(seq_count, shard_rows, local_width), "ctx", axis=1, tiled=True
        ),
        lax.all_gather(
            own_values.reshape(seq_count, shard_rows, local_width), "ctx", axis=1, tiled=True
        ),
    )
    log_total = log_totals(queries, keys_all, own_pos, pos_table, key_rows)
    attended = attend_values(queries, keys_all, values_all, log_total, own_pos, pos_table, key_rows)
    mixed = attended.reshape(flat_rows, local_width).astype(jnp.bfloat16)
    hidden_pre = jnp.dot(normed, expand_full, preferred_element_type=jnp.float32)
    activated_full, gelu_pull = jax.vjp(gelu_tanh, hidden_pre)
    activated = activated_full.astype(jnp.bfloat16)
    branch = jnp.dot(mixed, attention_out, preferred_element_type=jnp.float32) + jnp.dot(
        activated, contract_full, preferred_element_type=jnp.float32
    )
    branch = lax.psum(branch.astype(jnp.bfloat16), "tp").astype(jnp.float32)
    output = (inputs + branch.reshape(seq_count, shard_rows, model_width)).astype(jnp.bfloat16)
    upstream = cotangent.reshape(flat_rows, model_width)
    contract_grad = jnp.einsum("tf,td->fd", activated, upstream, preferred_element_type=jnp.float32)
    (gelu_grad,) = gelu_pull(
        jnp.einsum("td,fd->tf", upstream, contract_full, preferred_element_type=jnp.float32)
    )
    hidden_grad = gelu_grad.astype(jnp.bfloat16)
    expand_grad = jnp.einsum("td,tf->df", normed, hidden_grad, preferred_element_type=jnp.float32)
    mixed_grad = jnp.einsum(
        "td,ed->te", upstream, attention_out, preferred_element_type=jnp.float32
    ).astype(jnp.bfloat16)
    attention_out_grad = jnp.einsum(
        "te,td->ed", mixed, upstream, preferred_element_type=jnp.float32
    )
    out_grad = mixed_grad.reshape(seq_count, shard_rows, head_count, HEAD_DIM)
    row_delta = jnp.sum(out_grad.astype(jnp.float32) * attended, axis=-1).transpose(0, 2, 1)
    query_grad, key_terms, value_terms = full_grads(
        queries, keys_all, values_all, log_total, row_delta, out_grad, own_pos, pos_table, key_rows
    )
    key_grad, value_grad = (
        lax.psum_scatter(
            key_terms.astype(jnp.bfloat16), "ctx", scatter_dimension=1, tiled=True
        ).astype(jnp.float32),
        lax.psum_scatter(
            value_terms.astype(jnp.bfloat16), "ctx", scatter_dimension=1, tiled=True
        ).astype(jnp.float32),
    )
    key_grad = key_grad.reshape(seq_count, shard_rows, head_count, HEAD_DIM)
    value_grad = value_grad.reshape(seq_count, shard_rows, head_count, HEAD_DIM)
    (rotated_grad,) = rotate_pull(jnp.stack([query_grad, key_grad]))
    projected_grad = (
        jnp.concatenate([rotated_grad, value_grad[None]], axis=0)
        .reshape(3, flat_rows, local_width)
        .astype(jnp.bfloat16)
    )
    attention_in_grad = jnp.einsum(
        "td,kte->kde", normed, projected_grad, preferred_element_type=jnp.float32
    )
    normed_grad = jnp.einsum(
        "kte,kde->td", projected_grad, attention_in, preferred_element_type=jnp.float32
    )
    normed_grad = normed_grad + jnp.einsum(
        "tf,df->td", hidden_grad, expand_full, preferred_element_type=jnp.float32
    )
    normed_grad = lax.psum(normed_grad.astype(jnp.bfloat16), "tp").astype(jnp.float32)
    input_part, gain_grad, shift_grad = norm_pull(
        normed_grad.reshape(seq_count, shard_rows, model_width)
    )
    input_grad = input_part + cotangent.astype(jnp.float32)
    reduced = (
        lax.psum_scatter(
            gain_grad.astype(jnp.bfloat16), "ctx", scatter_dimension=0, tiled=True
        ).astype(jnp.float32),
        lax.psum_scatter(
            shift_grad.astype(jnp.bfloat16), "ctx", scatter_dimension=0, tiled=True
        ).astype(jnp.float32),
        lax.psum_scatter(
            attention_in_grad.astype(jnp.bfloat16), "ctx", scatter_dimension=1, tiled=True
        ).astype(jnp.float32),
        lax.psum_scatter(
            attention_out_grad.astype(jnp.bfloat16), "ctx", scatter_dimension=1, tiled=True
        ).astype(jnp.float32),
        lax.psum_scatter(
            expand_grad.astype(jnp.bfloat16), "ctx", scatter_dimension=0, tiled=True
        ).astype(jnp.float32),
        lax.psum_scatter(
            contract_grad.astype(jnp.bfloat16), "ctx", scatter_dimension=1, tiled=True
        ).astype(jnp.float32),
    )
    return (
        output,
        input_grad,
        reduced[0],
        reduced[1],
        reduced[2],
        reduced[3],
        reduced[4],
        reduced[5],
    )


def solution(mesh):
    in_specs = (
        P(None, "ctx", None),
        P(),
        P("ctx"),
        P("ctx"),
        P(None, "ctx", "tp"),
        P("tp", "ctx"),
        P("ctx", "tp"),
        P("tp", "ctx"),
        P(None, "ctx", None),
    )
    out_specs = (
        P(None, "ctx", None),
        P(None, "ctx", None),
        P("ctx"),
        P("ctx"),
        P(None, "ctx", "tp"),
        P("tp", "ctx"),
        P("ctx", "tp"),
        P("tp", "ctx"),
    )
    return jax.shard_map(local, mesh=mesh, in_specs=in_specs, out_specs=out_specs, check_vma=False)
```

profile of v0, /device:TPU:0, one launch (start us, length us, event | category | flops | bytes accessed | tf_op | source)
XLA Modules:
  0.0 1343.8 jit_solution(11901705000451130712)
XLA Ops:
  10.3 22.4 %all-gather = bf16[8,1,256]{2,1,0:T(2,128)(2,1)S(1)} all-gather(bf16[1,1,256]{2,1,0:T(2,128)(2,1)S(1)} %reshape.232), channel_id=1, replica_groups=mesh['ctx'=8,'tp'=4] {'ctx'}, dimensions={0}, use_global_device_ids=true | all-gather | bytes 4608 | tf_op jit(solution)/shard_map/all_gather | solution.py:188
  33.4 16.5 %all-gather.1 = bf16[8,1,256]{2,1,0:T(2,128)(2,1)S(1)} all-gather(bf16[1,1,256]{2,1,0:T(2,128)(2,1)S(1)} %reshape.234), channel_id=1, replica_groups=mesh['ctx'=8,'tp'=4] {'ctx'}, dimensions={0}, use_global_device_ids=true | all-gather | bytes 4608 | tf_op jit(solution)/shard_map/all_gather | solution.py:189
  49.9 1.9 convert_reduce_fusion
  53.7 2.1 fusion.32
  55.9 56.2 %all-gather.9.cloned.1.call-done = bf16[3,2048,512]{2,1,0:T(8,128)(2,1)} async-done(((bf16[3,256,512]{2,1,0:T(8,128)(2,1)}), bf16[3,2048,512]{2,1,0:T(8,128)(2,1)}) %all-gather.9.cloned.1.call-update) | async-done | bytes 6291472 | tf_op jit(solution)/shard_map/all_gather | solution.py:190
  112.1 6.2 convolution_bitcast_fusion.1
  121.5 1.9 copy.77
  123.4 2.4 slice.30
  136.2 27.3 %all-gather.15.cloned.1.call-done = bf16[512,2048]{1,0:T(8,128)(2,1)} async-done(((bf16[512,256]{1,0:T(8,128)(2,1)}), bf16[512,2048]{1,0:T(8,128)(2,1)}) %all-gather.15.cloned.1.call-update) | async-done | bytes 2097168 | tf_op jit(solution)/shard_map/all_gather | solution.py:191
  163.4 3.5 convolution_convert_fusion.3
  168.3 70.9 %all-gather.13.cloned.1.call-done = bf16[2,2048,512]{1,2,0:T(8,128)(2,1)} async-done(((bf16[2,256,512]{1,2,0:T(8,128)(2,1)}), bf16[2,2048,512]{1,2,0:T(8,128)(2,1)}) %all-gather.13.cloned.1.call-update) | async-done | bytes 4194320 | tf_op jit(solution)/shard_map/all_gather | solution.py:214
  239.3 35.4 %while.48 = (s32[]{:T(128)}, f32[2,8,256]{2,1,0:T(8,128)S(1)}, f32[2,8,256]{2,1,0:T(8,128)S(1)}, s32[2,2048]{1,0:T(2,128)S(1)}, s32[2,256]{1,0:T(2,128)S(1)}, /*...) while((s32[]{:T(128)}, f32[2,8,256]{2,1,0:T(8,128)S(1)}, ...), condition=%wide.region_6.7_spmd.clone, body=%wide.region_3.6_spmd.clone.sunk | while | flops 570970112 | bytes 42182828 | solution.py:116
  241.5 7.5 fusion.124
  249.0 7.9 select_reduce_fusion.2
  259.3 7.3 fusion.124
  266.7 7.9 select_reduce_fusion.2
  274.7 40.3 %all-gather.11.cloned.1.call-done = bf16[2,2048,512]{1,2,0:T(8,128)(2,1)} async-done(((bf16[2,256,512]{1,2,0:T(8,128)(2,1)}), bf16[2,2048,512]{1,2,0:T(8,128)(2,1)}) %all-gather.11.cloned.1.call-update) | async-done | bytes 4194320 | tf_op jit(solution)/shard_map/all_gather | solution.py:217
  315.0 24.6 %while.49 = (s32[]{:T(128)}, f32[2,256,8,64]{1,3,2,0:T(8,128)}, bf16[2,2048,512]{1,2,0:T(8,128)(2,1)}, s32[2,2048]{1,0:T(2,128)S(1)}, s32[2,256]{1,0:T(2,128)S(1...) while((s32[]{:T(128)}, f32[2,256,8,64]{1,3,2,0:T(8,128)}, ...), condition=%wide.region_8.9_spmd.clone, body=%wide.region_7.8_spmd.clone.sunk | while | flops 1091567616 | bytes 16296117 | solution.py:136
  315.0 4.2 constant_dynamic-slice_fusion.19
  319.6 7.5 fusion.130
  327.1 4.2 constant_dynamic-slice_fusion.19
  331.8 7.7 fusion.130
  339.5 2.6 fusion.46
  342.1 2.5 broadcast.275
  344.7 2.6 broadcast.275.clone
  347.3 92.4 %while.50 = (s32[]{:T(128)}, f32[2,256,8,64]{1,3,2,0:T(8,128)}, bf16[2,2048,512]{1,2,0:T(8,128)(2,1)}, bf16[2,2048,512]{1,2,0:T(8,128)(2,1)}, bf16[2,2048,512]{1...) while((s32[]{:T(128)}, f32[2,256,8,64]{1,3,2,0:T(8,128)}, ...), condition=%wide.region_12.13_spmd.clone, body=%wide.region_11.12_spmd.clone.sunk | while | flops 2731540480 | bytes 161032496 | solution.py:172
  349.5 8.1 fusion.141
  358.7 9.4 fusion.142
  368.0 4.1 fusion.145
  372.1 10.9 fusion.144
  383.0 4.8 constant_dynamic-update-slice_fusion.3
  387.8 5.8 fusion.143
  395.4 8.1 fusion.141
  404.6 9.4 fusion.142
  413.9 4.1 fusion.145
  418.0 10.7 fusion.144
  428.7 4.7 constant_dynamic-update-slice_fusion.3
  433.4 6.1 fusion.143
  440.5 10.7 fusion.62
  451.2 114.5 %all-gather.17.cloned.1.call-done = bf16[2048,2048]{1,0:T(8,128)(2,1)} async-done(((bf16[256,2048]{1,0:T(8,128)(2,1)}), bf16[2048,2048]{1,0:T(8,128)(2,1)}) %all-gather.17.cloned.1.call-update) | async-done | bytes 8388624 | tf_op jit(solution)/shard_map/all_gather | solution.py:192
  565.7 13.5 %fusion.37 = (bf16[512,2048]{1,0:T(8,128)(2,1)}, f32[512,2048]{1,0:T(8,128)}) fusion(f32[512,2048]{1,0:T(8,128)} %fusion.62, bf16[512,2048]{1,0:T(8,128)(2,1)S(1)} %bitcast.205, bf16[2048,2048]{1,0:T(8,128)(2,1)} %all-gather.17.cloned.1.call-done), kind=kOutput, calls=%fused_computation.64 | convolution fusion | flops 4320133120 | bytes 20971520 | tf_op jit(solution)/shard_map/dot_general | solution.py:224
  579.9 2.6 convolution_convert_fusion.2
  582.5 10.9 fusion.63
  593.4 8.0 fusion.57
  602.3 2.7 add_convert_fusion
  605.0 50.8 %reduce-scatter.7.cloned.1.call-done = bf16[2,256,512]{1,2,0:T(8,128)(2,1)} async-done(((bf16[2,2048,512]{1,2,0:T(8,128)(2,1)}), bf16[2,256,512]{1,2,0:T(8,128)(2,1)}) %reduce-scatter.7.cloned.1.call-update) | async-done | bytes 524304 | tf_op jit(solution)/shard_map/reduce_scatter | solution.py:251
  660.9 87.2 %reduce-scatter.9.cloned.1.call-done = bf16[2,256,512]{1,2,0:T(8,128)(2,1)} async-done(((bf16[2,2048,512]{1,2,0:T(8,128)(2,1)}), bf16[2,256,512]{1,2,0:T(8,128)(2,1)}) %reduce-scatter.9.cloned.1.call-update) | async-done | bytes 524304 | tf_op jit(solution)/shard_map/reduce_scatter | solution.py:254
  750.2 8.1 fusion.43
  759.9 8.4 convolution_convert_fusion.1
  768.6 11.2 convolution_convert_fusion
  779.9 6.5 convert_bitcast_fusion
  788.3 31.4 %reduce-scatter.13.cloned.1.call-done = bf16[512,256]{1,0:T(8,128)(2,1)} async-done(((bf16[512,2048]{1,0:T(8,128)(2,1)}), bf16[512,256]{1,0:T(8,128)(2,1)}) %reduce-scatter.13.cloned.1.call-update) | async-done | bytes 262160 | tf_op jit(solution)/shard_map/reduce_scatter | solution.py:290
  821.5 85.8 %all-reduce.9.cloned.1.call-done = (bf16[2,256,2048]{2,1,0:T(8,128)(2,1)}, bf16[512,2048]{1,0:T(8,128)(2,1)}) async-done(((bf16[2,256,2048]{2,1,0:T(8,128)(2,1)}, bf16[512,2048]{1,0:T(8,128)(2,1)}), (bf16[2,256,2048]{2,1,0:T(8,128)(2,1)}, bf16[512,2048]{1,0:T(8,128)(2,1)})) %all-reduce.9.cloned.1.call-update) | async-done | bytes 4194320 | tf_op jit(solution)/shard_map/psum | solution.py:230
  907.3 2.0 reduce_sum.111
  909.3 2.7 fusion.39
  912.0 2.1 fusion.33
  914.2 22.7 %all-reduce.5 = (bf16[2048]{0:T(1024)(128)(2,1)S(1)}, bf16[2048]{0:T(1024)(128)(2,1)S(1)}) all-reduce(bf16[2048]{0:T(1024)(128)(2,1)S(1)} %get-tuple-element.702, bf16[2048]{0:T(1024)(128)(2,1)S(1)} %reduce_sum.111), channel_id=4, replica_groups=mesh['ctx'=8,'tp'=4] {'ctx'}, use_global_device_ids=true, to_apply=%region_19.20.clone | all-reduce | flops 4096 | bytes 16384
  937.5 5.8 convert_add_fusion.1
  943.3 117.7 %reduce-scatter.15.cloned.1.call-done = bf16[256,2048]{1,0:T(8,128)(2,1)} async-done(((bf16[2048,2048]{1,0:T(8,128)(2,1)}), bf16[256,2048]{1,0:T(8,128)(2,1)}) %reduce-scatter.15.cloned.1.call-update) | async-done | bytes 1048592 | tf_op jit(solution)/shard_map/reduce_scatter | solution.py:293
  1061.0 2.8 convert_element_type.166
  1063.7 149.1 %reduce-scatter.17.cloned.1.call-done = bf16[2048,256]{1,0:T(8,128)(2,1)} async-done(((bf16[2048,2048]{1,0:T(8,128)(2,1)}), bf16[2048,256]{1,0:T(8,128)(2,1)}) %reduce-scatter.17.cloned.1.call-update) | async-done | bytes 1048592 | tf_op jit(solution)/shard_map/reduce_scatter | solution.py:296
  1212.9 2.7 convert_element_type.168
  1215.6 118.7 %reduce-scatter.11.cloned.1.call-done = bf16[3,256,512]{1,2,0:T(8,128)(2,1)} async-done(((bf16[3,2048,512]{1,2,0:T(8,128)(2,1)}), bf16[3,256,512]{1,2,0:T(8,128)(2,1)}) %reduce-scatter.11.cloned.1.call-update) | async-done | bytes 786448 | tf_op jit(solution)/shard_map/reduce_scatter | solution.py:287
  1334.3 2.6 copy.92
  (166 shorter events, 46.5 us)
Async XLA Ops:
  7.2 44.7 %copy-start.3 = (bf16[2,256,2048]{2,1,0:T(8,128)(2,1)S(1)}, bf16[2,256,2048]{2,1,0:T(8,128)(2,1)}, u32[]{:S(2)}) copy-start(bf16[2,256,2048]{2,1,0:T(8,128)(2,1)} %param.15) | copy-start | bytes 6291460
  7.2 104.9 %all-gather.9.cloned.1.call-start = ((), (), s32[]{:S(2)}) async-start(), calls=%async_computation.6 | async-start | bytes 7077888 | tf_op jit(solution)/shard_map/all_gather | solution.py:190
  7.9 155.5 %all-gather.15.cloned.1.call-start = ((), (), s32[]{:S(2)}) async-start(), calls=%async_computation.9 | async-start | bytes 2359296 | tf_op jit(solution)/shard_map/all_gather | solution.py:191
  8.7 230.6 %all-gather.13.cloned.1.call-start = ((), (), s32[]{:S(2)}) async-start(), calls=%async_computation.8 | async-start | bytes 4718592 | tf_op jit(solution)/shard_map/all_gather | solution.py:214
  32.7 23.2 %copy-start.19 = (f32[8,1,256]{2,1,0:T(1,128)}, f32[8,1,256]{2,1,0:T(1,128)S(1)}, u32[]{:S(2)}) copy-start(f32[8,1,256]{2,1,0:T(1,128)S(1)} %convert_element_type.169) | copy-start | bytes 24580
  51.9 66.4 %copy-start.21 = (f32[2,256]{1,0:T(2,128)}, f32[2,256]{1,0:T(2,128)S(1)}, u32[]{:S(2)}) copy-start(f32[2,256]{1,0:T(2,128)S(1)} %broadcast_multiply_fusion) | copy-start | bytes 6148
  52.6 0.6 copy-start.25
  53.2 65.1 %copy-start.23 = (f32[2,256]{1,0:T(2,128)}, f32[2,256]{1,0:T(2,128)S(1)}, u32[]{:S(2)}) copy-start(f32[2,256]{1,0:T(2,128)S(1)} %fusion.54) | copy-start | bytes 6148
  53.7 73.7 %copy-start.13 = (f32[2,256,16]{1,0,2:T(2,128)}, f32[2,256,16]{1,0,2:T(2,128)S(1)}, u32[]{:S(2)}) copy-start(f32[2,256,16]{1,0,2:T(2,128)S(1)} %get-tuple-element.779) | copy-start | bytes 98308
  53.7 73.7 %copy-start.15 = (f32[2,256,16]{1,0,2:T(2,128)}, f32[2,256,16]{1,0,2:T(2,128)S(1)}, u32[]{:S(2)}) copy-start(f32[2,256,16]{1,0,2:T(2,128)S(1)} %get-tuple-element.780) | copy-start | bytes 98308
  118.3 1.7 copy-start.8
  132.3 182.7 %all-gather.11.cloned.1.call-start = ((), (), s32[]{:S(2)}) async-start(), calls=%async_computation.7 | async-start | bytes 4718592 | tf_op jit(solution)/shard_map/all_gather | solution.py:217
  134.7 305.8 %all-gather.19.cloned.1.call-start = ((), (), s32[]{:S(2)}) async-start(), calls=%async_computation.11 | async-start | bytes 9437184 | tf_op jit(solution)/shard_map/all_gather | solution.py:193
  135.3 430.4 %all-gather.17.cloned.1.call-start = ((), (), s32[]{:S(2)}) async-start(), calls=%async_computation.10 | async-start | bytes 9437184 | tf_op jit(solution)/shard_map/all_gather | solution.py:192
  135.8 519.9 %reduce-scatter.7.cloned.1.call-start = ((), (), s32[]{:S(2)}) async-start(), calls=%async_computation.12 | async-start | bytes 4718592 | tf_op jit(solution)/shard_map/reduce_scatter | solution.py:251
  167.3 72.0 %copy-start.6 = (bf16[2,256,8,64]{1,0,3,2:T(2,128)(2,1)}, bf16[2,256,8,64]{1,0,3,2:T(2,128)(2,1)S(1)}, u32[]{:S(2)}) copy-start(bf16[2,256,8,64]{1,0,3,2:T(2,128)(2,1)S(1)} %reshape.226) | copy-start | bytes 1572868
  349.5 8.6 copy-start.1
  357.6 1.0 copy-start.17
  368.0 4.1 copy-start
  395.4 8.6 copy-start.1
  403.5 1.0 copy-start.17
  413.9 4.1 copy-start
  439.7 308.5 %reduce-scatter.9.cloned.1.call-start = ((), (), s32[]{:S(2)}) async-start(), calls=%async_computation.13 | async-start | bytes 4718592 | tf_op jit(solution)/shard_map/reduce_scatter | solution.py:254
  440.4 125.2 %copy-start.9 = (bf16[2,256,2048]{2,1,0:T(8,128)(2,1)S(1)}, bf16[2,256,2048]{2,1,0:T(8,128)(2,1)}, u32[]{:S(2)}) copy-start(bf16[2,256,2048]{2,1,0:T(8,128)(2,1)} %fusion.32) | copy-start | bytes 6291460
  440.4 379.3 %reduce-scatter.13.cloned.1.call-start = ((), (), s32[]{:S(2)}) async-start(), calls=%async_computation.15 | async-start | bytes 2359296 | tf_op jit(solution)/shard_map/reduce_scatter | solution.py:290
  565.6 13.5 %copy-start.7 = (f32[2,256,8,64]{1,3,2,0:T(8,128)S(1)}, f32[2,256,8,64]{1,3,2,0:T(8,128)}, u32[]{:S(2)}) copy-start(f32[2,256,8,64]{1,3,2,0:T(8,128)} %get-tuple-element.475) | copy-start | bytes 3145732
  565.6 14.2 %copy-start.11 = (bf16[2,256,2048]{2,1,0:T(8,128)(2,1)S(1)}, bf16[2,256,2048]{2,1,0:T(8,128)(2,1)}, u32[]{:S(2)}) copy-start(bf16[2,256,2048]{2,1,0:T(8,128)(2,1)} %param.23) | copy-start | bytes 6291460
  582.5 324.9 %all-reduce.9.cloned.1.call-start = ((), (), s32[]{:S(2)}) async-start(), calls=%async_computation.18 | async-start | bytes 8388608 | tf_op jit(solution)/shard_map/psum | solution.py:230
  582.5 10.9 copy-start.28
  593.4 8.1 copy-start.2
  593.4 8.9 copy-start.12
  605.0 52.9 %copy-start.14 = (f32[2,256,16]{1,0,2:T(2,128)S(1)}, f32[2,256,16]{1,0,2:T(2,128)}, u32[]{:S(2)}) copy-start(f32[2,256,16]{1,0,2:T(2,128)} %copy-done.13) | copy-start | bytes 98308
  605.0 52.9 %copy-start.16 = (f32[2,256,16]{1,0,2:T(2,128)S(1)}, f32[2,256,16]{1,0,2:T(2,128)}, u32[]{:S(2)}) copy-start(f32[2,256,16]{1,0,2:T(2,128)} %copy-done.15) | copy-start | bytes 98308
  749.4 0.8 copy-start.18
  758.3 1.6 copy-start.10
  758.3 302.6 %reduce-scatter.15.cloned.1.call-start = ((), (), s32[]{:S(2)}) async-start(), calls=%async_computation.16 | async-start | bytes 9437184 | tf_op jit(solution)/shard_map/reduce_scatter | solution.py:293
  768.3 444.6 %reduce-scatter.17.cloned.1.call-start = ((), (), s32[]{:S(2)}) async-start(), calls=%async_computation.17 | async-start | bytes 9437184 | tf_op jit(solution)/shard_map/reduce_scatter | solution.py:296
  779.9 554.4 %reduce-scatter.11.cloned.1.call-start = ((), (), s32[]{:S(2)}) async-start(), calls=%async_computation.14 | async-start | bytes 7077888 | tf_op jit(solution)/shard_map/reduce_scatter | solution.py:287
  786.4 0.7 copy-start.27
  786.4 122.9 %copy-start.4 = (bf16[2,256,2048]{2,1,0:T(8,128)(2,1)S(1)}, bf16[2,256,2048]{2,1,0:T(8,128)(2,1)}, u32[]{:S(2)}) copy-start(bf16[2,256,2048]{2,1,0:T(8,128)(2,1)} %param.15) | copy-start | bytes 6291460
  786.4 122.9 %copy-start.20 = (f32[8,1,256]{2,1,0:T(1,128)S(1)}, f32[8,1,256]{2,1,0:T(1,128)}, u32[]{:S(2)}) copy-start(f32[8,1,256]{2,1,0:T(1,128)} %copy-done.19) | copy-start | bytes 24580
  786.4 122.9 %copy-start.22 = (f32[2,256]{1,0:T(2,128)S(1)}, f32[2,256]{1,0:T(2,128)}, u32[]{:S(2)}) copy-start(f32[2,256]{1,0:T(2,128)} %copy-done.21) | copy-start | bytes 6148
  786.4 125.6 %copy-start.26 = (f32[2,256]{1,0:T(2,128)S(1)}, f32[2,256]{1,0:T(2,128)}, u32[]{:S(2)}) copy-start(f32[2,256]{1,0:T(2,128)} %copy-done.25) | copy-start | bytes 6148
  786.4 125.6 %copy-start.24 = (f32[2,256]{1,0:T(2,128)S(1)}, f32[2,256]{1,0:T(2,128)}, u32[]{:S(2)}) copy-start(f32[2,256]{1,0:T(2,128)} %copy-done.23) | copy-start | bytes 6148
  909.3 2.8 copy-start.5
Sparse Core Ops, SparseCore 0:
  10.2 101.8 all-gather.8
  114.1 49.2 all-gather.14
  166.0 73.1 all-gather.12
  241.7 73.1 all-gather.10
  316.9 123.5 all-gather.18
  442.5 123.1 all-gather.16
  569.3 86.4 reduce-scatter.6
  659.8 88.2 reduce-scatter.8
  751.7 68.0 reduce-scatter.12
  822.6 84.6 all-reduce.8
  911.4 149.5 reduce-scatter.14
  1064.4 148.3 reduce-scatter.16
  1216.9 117.3 reduce-scatter.10
where the time goes:
time: 1350 us; the launch traced here: 1340 us
  waiting for transfers between devices  953 us (71%)
  matrix products  199 us (15%)
  blocking collectives  61.6 us (5%)
  local copies, waits for them, and re-layouts  59.1 us (4%)
  other arithmetic  53.4 us (4%)
  between operations  15.6 us (1%)
    reduce_scatter x1, waiting for transfers between devices, local(): lax.psum_scatter(contract_grad.astype(jnp.bfloat16), 'ctx', scatter_dimen...  149 us
    reduce_scatter x1, waiting for transfers between devices, local(): lax.psum_scatter(attention_in_grad.astype(jnp.bfloat16), 'ctx', scatter_d...  119 us
    reduce_scatter x1, waiting for transfers between devices, local(): lax.psum_scatter(expand_grad.astype(jnp.bfloat16), 'ctx', scatter_dimensi...  118 us
    all_gather x1, waiting for transfers between devices, local(): lax.all_gather(w_expand, 'ctx', axis=0, tiled=True)  114 us
    reduce_scatter x1, waiting for transfers between devices, local(): lax.psum_scatter(value_terms.astype(jnp.bfloat16), 'ctx', scatter_dimensi...  87.2 us
    psum x1, waiting for transfers between devices, local(): branch = lax.psum(branch.astype(jnp.bfloat16), 'tp').astype(jnp.float32)  85.8 us
    all_gather x1, waiting for transfers between devices, local(): lax.all_gather(own_keys.reshape(seq_count, shard_rows, local_width), 'ctx...  70.9 us
    all_gather x1, waiting for transfers between devices, local(): lax.all_gather(w_attention_in, 'ctx', axis=1, tiled=True)  56.2 us
  transfers between devices with their start and end apart: 13, of which 12 were waited for; matrix products, arithmetic and copies ran while one was open for 23% of the time, Pallas kernels for 0%

commit v1 on v0

--- a/solution.py
+++ b/solution.py
@@ -1,6 +1,11 @@
+import functools
+import itertools
+
 import jax
 import jax.numpy as jnp
 from jax import lax
+from jax.experimental import pallas as pl
+from jax.experimental.pallas import tpu as pltpu
 from jax.sharding import PartitionSpec as P
 
 HEAD_DIM = 64
@@ -172,7 +177,7 @@
     return lax.fori_loop(0, turn_count, full_one_turn, initial)
 
 
-def local(
+def general_local(
     tokens,
     pair_index,
     norm_gain,
@@ -309,6 +314,786 @@
     )
 
 
+MESH = pl.DeviceIdType.MESH
+MB = 1 << 20
+EPS = 1e-05
+
+
+def place():
+    c = lax.axis_index("ctx")
+    t = lax.axis_index("tp")
+    return c // 2, c % 2, t // 2, t % 2
+
+
+def device(z, x, y, k):
+    return (z * 2 + x, y * 2 + k)
+
+
+def remote(src, dst, send_sem, recv_sem, target):
+    return pltpu.make_async_remote_copy(
+        src_ref=src, dst_ref=dst, send_sem=send_sem, recv_sem=recv_sem,
+        device_id=target, device_id_type=MESH,
+    )
+
+
+def meet(peers):
+    barrier = pltpu.get_barrier_semaphore()
+    for peer in peers:
+        pl.semaphore_signal(barrier, inc=1, device_id=peer, device_id_type=MESH)
+    pl.semaphore_wait(barrier, len(peers))
+
+
+class TokenGather:
+    def __init__(self, whole, sems):
+        self.whole = whole
+        self.xs, self.xr, self.zs, self.zr, self.ys, self.yr, self.cs, self.cr, self.loc = sems
+        self.z, self.x, self.y, self.k = place()
+        self.q = 2 * self.y + self.k
+
+    def chunk(self, zz, s, q):
+        xx = self.x if s == 0 else 1 - self.x
+        return self.whole.at[zz, xx, pl.ds(64 * q, 64), :]
+
+    def send_x(self, src):
+        z, x, y, k = self.z, self.x, self.y, self.k
+        return remote(src, self.whole.at[z, x, pl.ds(64 * self.q, 64), :], self.xs, self.xr, device(z, 1 - x, y, k))
+
+    def send_up(self, zz, s, src):
+        return remote(src, self.chunk(zz, s, self.q), self.zs.at[zz, s, 0], self.zr.at[zz, s],
+                      device(jnp.minimum(self.z + 1, 3), self.x, self.y, self.k))
+
+    def send_down(self, zz, s, src):
+        return remote(src, self.chunk(zz, s, self.q), self.zs.at[zz, s, 1], self.zr.at[zz, s],
+                      device(jnp.maximum(self.z - 1, 0), self.x, self.y, self.k))
+
+    def send_y(self, zz, s):
+        c = self.chunk(zz, s, self.q)
+        return remote(c, c, self.ys.at[zz, s], self.yr.at[zz, s], device(self.z, self.x, 1 - self.y, self.k))
+
+    def send_core(self, zz, s, j):
+        yy = self.y if j == 0 else 1 - self.y
+        c = self.chunk(zz, s, 2 * yy + self.k)
+        return remote(c, c, self.cs.at[zz, s, j], self.cr.at[zz, s, j], device(self.z, self.x, self.y, 1 - self.k))
+
+    def start(self, own_quarter, other_quarter, own_slot):
+        z = self.z
+        self.send_x(other_quarter).start()
+
+        @pl.when(z < 3)
+        def _():
+            self.send_up(z, 0, own_quarter).start()
+
+        @pl.when(z > 0)
+        def _():
+            self.send_down(z, 0, own_quarter).start()
+
+        pltpu.make_async_copy(own_slot, self.whole.at[z, self.x], self.loc).start()
+
+    def after_x(self):
+        z = self.z
+        c = self.chunk(z, 1, self.q)
+        remote(c, c, self.xs, self.xr, device(z, 1 - self.x, self.y, self.k)).wait_recv()
+
+        @pl.when(z < 3)
+        def _():
+            self.send_up(z, 1, c).start()
+
+        @pl.when(z > 0)
+        def _():
+            self.send_down(z, 1, c).start()
+
+        self.send_y(z, 1).start()
+        self.send_core(z, 1, 0).start()
+
+    def hop(self, d, s):
+        z = self.z
+
+        @pl.when(z >= d)
+        def _():
+            zz = z - d
+            c = self.chunk(zz, s, self.q)
+            self.send_down(zz, s, c).wait_recv()
+
+            @pl.when(z < 3)
+            def _():
+                self.send_up(zz, s, c).start()
+
+            self.send_y(zz, s).start()
+            self.send_core(zz, s, 0).start()
+
+        @pl.when(z + d <= 3)
+        def _():
+            zz = z + d
+            c = self.chunk(zz, s, self.q)
+            self.send_up(zz, s, c).wait_recv()
+
+            @pl.when(z > 0)
+            def _():
+                self.send_down(zz, s, c).start()
+
+            self.send_y(zz, s).start()
+            self.send_core(zz, s, 0).start()
+
+    def y_in(self, zz, s):
+        c = self.chunk(zz, s, 2 * (1 - self.y) + self.k)
+        remote(c, c, self.ys.at[zz, s], self.yr.at[zz, s], device(self.z, self.x, 1 - self.y, self.k)).wait_recv()
+        self.send_core(zz, s, 1).start()
+
+    def y_hop(self, d, s):
+        z = self.z
+        if d == 0:
+            self.y_in(z, s)
+            return
+
+        @pl.when(z >= d)
+        def _():
+            self.y_in(z - d, s)
+
+        @pl.when(z + d <= 3)
+        def _():
+            self.y_in(z + d, s)
+
+    def finish(self, own_quarter, other_quarter, own_slot):
+        z = self.z
+        self.send_x(other_quarter).wait_send()
+        pltpu.make_async_copy(own_slot, self.whole.at[z, self.x], self.loc).wait()
+        for zz in range(4):
+            for s in range(2):
+                def rest():
+                    self.send_y(zz, s).wait_send()
+                    for j in range(2):
+                        yy = self.y if j == 0 else 1 - self.y
+                        c = self.chunk(zz, s, 2 * yy + 1 - self.k)
+                        r = remote(c, c, self.cs.at[zz, s, j], self.cr.at[zz, s, j], device(self.z, self.x, self.y, 1 - self.k))
+                        r.wait()
+                if s == 0:
+                    pl.when(z != zz)(rest)
+                else:
+                    rest()
+                c = self.chunk(zz, s, self.q)
+
+                @pl.when((z < 3) & (zz <= z))
+                def _():
+                    self.send_up(zz, s, c).wait_send()
+
+                @pl.when((z > 0) & (zz >= z))
+                def _():
+                    self.send_down(zz, s, c).wait_send()
+
+
+def token_sems():
+    D = pltpu.SemaphoreType.DMA
+    return [D, D, D((4, 2, 2)), D((4, 2)), D((4, 2)), D((4, 2)), D((4, 2, 2)), D((4, 2, 2)), D]
+
+
+class WeightGather:
+    def __init__(self, pairs, sems):
+        self.pairs = pairs
+        self.zs, self.zr, self.xs, self.xr, self.loc = sems
+        self.z, self.x, self.y, self.k = place()
+
+    def z_send(self, d, w):
+        src, dst = self.pairs[w]
+        z = self.z
+        to = (z + d) % 4
+        return remote(src(to), dst(z, self.x), self.zs.at[d, w], self.zr.at[d, w], device(to, self.x, self.y, self.k))
+
+    def z_recv(self, d, w):
+        src, dst = self.pairs[w]
+        frm = (self.z - d + 4) % 4
+        return remote(dst(frm, self.x), dst(frm, self.x), self.zs.at[d, w], self.zr.at[d, w], device(frm, self.x, self.y, self.k))
+
+    def x_send(self, d, w):
+        src, dst = self.pairs[w]
+        frm = (self.z - d + 4) % 4
+        s = src(self.z) if d == 0 else dst(frm, self.x)
+        return remote(s, dst(frm, self.x), self.xs.at[d, w], self.xr.at[d, w], device(self.z, 1 - self.x, self.y, self.k))
+
+    def x_recv(self, d, w):
+        src, dst = self.pairs[w]
+        frm = (self.z - d + 4) % 4
+        r = dst(frm, 1 - self.x)
+        return remote(r, r, self.xs.at[d, w], self.xr.at[d, w], device(self.z, 1 - self.x, self.y, self.k))
+
+    def local(self, w):
+        src, dst = self.pairs[w]
+        return pltpu.make_async_copy(src(self.z), dst(self.z, self.x), self.loc.at[w])
+
+    def start(self, ws, ds=(2, 3, 1)):
+        for w in ws:
+            for d in ds:
+                self.z_send(d, w).start()
+            self.x_send(0, w).start()
+            self.local(w).start()
+
+    def forward(self, w, d):
+        self.z_recv(d, w).wait_recv()
+        self.x_send(d, w).start()
+
+    def finish(self, w):
+        self.local(w).wait()
+        for d in range(4):
+            if d:
+                self.z_send(d, w).wait_send()
+            self.x_send(d, w).wait_send()
+            self.x_recv(d, w).wait_recv()
+
+
+def weight_sems(n):
+    D = pltpu.SemaphoreType.DMA
+    return [D((4, n)), D((4, n)), D((4, n)), D((4, n)), D((n,))]
+
+
+def norm_rows(rows, gain, shift):
+    v = rows.astype(jnp.float32)
+    centred = v - jnp.mean(v, axis=-1, keepdims=True)
+    spread = jnp.mean(centred * centred, axis=-1, keepdims=True)
+    return (centred * lax.rsqrt(spread + EPS) * gain + shift).astype(jnp.bfloat16)
+
+
+def gather_kernel(tok, gs, cot, win, wout, wexp, wcon,
+                  xn_all, ct_all, win_all, wout_all, wexp_all, wcon_all, gs_all,
+                  xn, gsem_s, gsem_r, *sems):
+    z, x, y, k = place()
+    c = z * 2 + x
+    q = 2 * y + k
+    nt, nw = len(token_sems()), len(weight_sems(4))
+    tx = TokenGather(xn_all, sems[:nt])
+    tc = TokenGather(ct_all, sems[nt:2 * nt])
+    col = lambda n, i: pl.ds(pl.multiple_of(n * i, n), n)
+    pairs = [
+        (lambda zz: win.at[:, :, col(128, zz)], lambda zz, xx: win_all.at[:, zz, xx]),
+        (lambda zz: wexp.at[:, col(512, zz)], lambda zz, xx: wexp_all.at[zz, xx]),
+        (lambda zz: wcon.at[col(512, zz), :], lambda zz, xx: wcon_all.at[:, col(256, zz * 2 + xx)]),
+        (lambda zz: wout.at[col(128, zz), :], lambda zz, xx: wout_all.at[:, col(256, zz * 2 + xx)]),
+    ]
+    wg = WeightGather(pairs, sems[2 * nt:])
+    others = [((c + i) % 8, lax.axis_index("tp")) for i in range(1, 8)]
+    meet(others + [device(z, x, 1 - y, k), device(z, x, y, 1 - k)])
+    gcopies = [remote(gs, gs_all.at[c], gsem_s.at[i], gsem_r.at[i], others[i]) for i in range(7)]
+    for g in gcopies:
+        g.start()
+    gs_all[c] = gs[...]
+    cot_own, cot_other = cot.at[x, pl.ds(64 * q, 64)], cot.at[1 - x, pl.ds(64 * q, 64)]
+    wg.start((0, 1))
+    for i in range(7):
+        frm = gs_all.at[(c - i - 1 + 8) % 8]
+        remote(frm, frm, gsem_s.at[i], gsem_r.at[i], others[i]).wait_recv()
+    gain = jnp.concatenate([gs_all[i, 0:1, :] for i in range(8)], axis=1)
+    shift = jnp.concatenate([gs_all[i, 1:2, :] for i in range(8)], axis=1)
+
+    @pl.loop(0, 4)
+    def _(i):
+        xn[pl.ds(256 + 16 * i, 16)] = norm_rows(tok[1 - x, pl.ds(64 * q + 16 * i, 16)], gain, shift)
+
+    @pl.loop(0, 16)
+    def _(i):
+        xn[pl.ds(16 * i, 16)] = norm_rows(tok[x, pl.ds(16 * i, 16)], gain, shift)
+
+    xsrc = (xn.at[pl.ds(64 * q, 64)], xn.at[pl.ds(256, 64)], xn.at[pl.ds(0, 256)])
+    csrc = (cot_own, cot_other, cot.at[x])
+    tx.start(*xsrc)
+    tc.start(*csrc)
+    wg.start((2, 3))
+    tx.after_x()
+    tc.after_x()
+    for d in range(1, 4):
+        for t in (tx, tc):
+            for s in range(2):
+                t.hop(d, s)
+        for w in range(4):
+            wg.forward(w, d)
+        for t in (tx, tc):
+            if d == 1:
+                t.y_hop(0, 1)
+            else:
+                for s in range(2):
+                    t.y_hop(d - 1, s)
+    for t in (tx, tc):
+        for s in range(2):
+            t.y_hop(3, s)
+    tx.finish(*xsrc)
+    tc.finish(*csrc)
+    for w in range(4):
+        wg.finish(w)
+    for g in gcopies:
+        g.wait_send()
+
+
+def gather_call(tokens, gs, cot, win, wout, wexp, wcon):
+    bf = jnp.bfloat16
+    S = jax.ShapeDtypeStruct
+    ANY = pl.BlockSpec(memory_space=pl.ANY)
+    VM = pl.BlockSpec(memory_space=pltpu.VMEM)
+    D = pltpu.SemaphoreType.DMA
+    return pl.pallas_call(
+        gather_kernel,
+        out_shape=[S((4, 2, 256, 2048), bf), S((4, 2, 256, 2048), bf), S((3, 4, 2, 256, 128), bf),
+                   S((128, 2048), bf), S((4, 2, 256, 512), bf), S((512, 2048), bf), S((8, 8, 256), jnp.float32)],
+        in_specs=[VM, VM] + [ANY] * 5,
+        out_specs=[ANY] * 6 + [VM],
+        scratch_shapes=[pltpu.VMEM((320, 2048), bf), D((7,)), D((7,))]
+        + token_sems() * 2 + weight_sems(4),
+        compiler_params=pltpu.CompilerParams(collective_id=0, has_side_effects=True, vmem_limit_bytes=48 * MB),
+        name="gather",
+    )(tokens, gs, cot, win, wout, wexp, wcon)
+
+
+def add_into(dst, src):
+    shape = dst.shape
+    lead = shape[:-2]
+    rows = shape[-2]
+    for idx in itertools.product(*(range(n) for n in lead)):
+        @pl.loop(0, rows // 16)
+        def _(i):
+            at = idx + (pl.ds(pl.multiple_of(16 * i, 16), 16), slice(None))
+            dst[at] = (dst[at].astype(jnp.float32) + src[at].astype(jnp.float32)).astype(jnp.bfloat16)
+
+
+class TokenReduce:
+    def __init__(self, part, out, bufs, sems):
+        self.part, self.out = part, out
+        self.A, self.r1, self.r2, self.rz, self.rf = bufs
+        (self.ld, self.cs, self.cr, self.ys, self.yr, self.zs, self.zr, self.xs, self.xr,
+         self.fl, self.fys, self.fyr, self.fcs, self.fcr) = sems
+        self.z, self.x, self.y, self.k = place()
+        self.q = 2 * self.y + self.k
+
+    def order(self, i):
+        z = self.z
+        if i == 0:
+            return 3 * (1 - z // 2)
+        if i == 1:
+            return z // 2 + 2 * (1 - z % 2)
+        if i == 2:
+            return 1 + z % 2
+        return z
+
+    def rows(self, zz, yy, kk):
+        return self.part.at[zz, :, pl.ds(64 * (2 * yy + kk), 64), :]
+
+    def load(self, zz, yy):
+        return pltpu.make_async_copy(self.rows(zz, yy, self.k), self.A.at[zz, yy], self.ld.at[zz, yy])
+
+    def core(self, zz, yy):
+        return remote(self.rows(zz, yy, 1 - self.k), self.r1.at[zz, yy], self.cs.at[zz, yy], self.cr.at[zz, yy],
+                      device(self.z, self.x, self.y, 1 - self.k))
+
+    def yex(self, zz):
+        return remote(self.A.at[zz, 1 - self.y], self.r2.at[zz], self.ys.at[zz], self.yr.at[zz],
+                      device(self.z, self.x, 1 - self.y, self.k))
+
+    def up(self, zz):
+        return remote(self.A.at[zz, self.y], self.rz.at[zz], self.zs.at[zz], self.zr.at[zz],
+                      device(jnp.minimum(self.z + 1, 3), self.x, self.y, self.k))
+
+    def down(self, zz):
+        slot = jnp.where(zz == self.z - 1, 4, zz)
+        return remote(self.A.at[zz, self.y], self.rz.at[slot], self.zs.at[zz], self.zr.at[slot],
+                      device(jnp.maximum(self.z - 1, 0), self.x, self.y, self.k))
+
+    def arrived(self, slot):
+        remote(self.rz.at[slot], self.rz.at[slot], self.zs.at[0], self.zr.at[slot],
+               device(self.z, self.x, self.y, 1 - self.k)).wait_recv()
+
+    def xex(self):
+        return remote(self.A.at[self.z, self.y, 1 - self.x], self.rf, self.xs, self.xr,
+                      device(self.z, 1 - self.x, self.y, self.k))
+
+    def start(self, i):
+        zz = self.order(i)
+        for yy in range(2):
+            self.core(zz, yy).start()
+            self.load(zz, yy).start()
+
+    def after_core(self, i):
+        zz = self.order(i)
+        for yy in range(2):
+            self.load(zz, yy).wait()
+            self.core(zz, yy).wait_recv()
+        add_into(self.A.at[zz], self.r1.at[zz])
+        self.yex(zz).start()
+
+    def after_y(self, i):
+        zz = self.order(i)
+        self.yex(zz).wait_recv()
+        add_into(self.A.at[zz, self.y], self.r2.at[zz])
+
+    def line(self, i):
+        z = self.z
+        zz = self.order(i)
+        mine = self.A.at[zz, self.y]
+        if i < 3:
+            @pl.when(zz > z)
+            def _():
+                @pl.when(z > 0)
+                def _():
+                    self.arrived(zz)
+                    add_into(mine, self.rz.at[zz])
+                self.up(zz).start()
+
+            @pl.when(zz < z)
+            def _():
+                @pl.when(z < 3)
+                def _():
+                    self.arrived(zz)
+                    add_into(mine, self.rz.at[zz])
+                self.down(zz).start()
+        else:
+            @pl.when(z > 0)
+            def _():
+                self.arrived(z)
+                add_into(mine, self.rz.at[z])
+
+            @pl.when(z < 3)
+            def _():
+                self.arrived(4)
+                add_into(mine, self.rz.at[4])
+            self.xex().start()
+
+    def spot(self, s, q):
+        return self.out.at[s, pl.ds(64 * q, 64), :]
+
+    def fin(self, s):
+        return (self.A.at[self.z, self.y, self.x], self.x) if s == 0 else (self.rf, 1 - self.x)
+
+    def fin_copies(self, s):
+        src, seq = self.fin(s)
+        here = self.spot(seq, self.q)
+        return (pltpu.make_async_copy(src, here, self.fl.at[s]),
+                remote(src, here, self.fys.at[s], self.fyr.at[s], device(self.z, self.x, 1 - self.y, self.k)),
+                remote(src, here, self.fcs.at[s, 0], self.fcr.at[s, 0], device(self.z, self.x, self.y, 1 - self.k)))
+
+    def relay(self, s):
+        seq = self.x if s == 0 else 1 - self.x
+        r = self.spot(seq, 2 * (1 - self.y) + self.k)
+        return remote(r, r, self.fcs.at[s, 1], self.fcr.at[s, 1], device(self.z, self.x, self.y, 1 - self.k))
+
+    def spread(self, s):
+        if s == 1:
+            self.xex().wait_recv()
+        for cp in self.fin_copies(s):
+            cp.start()
+
+    def spread_y(self, s):
+        seq = self.x if s == 0 else 1 - self.x
+        r = self.spot(seq, 2 * (1 - self.y) + self.k)
+        remote(r, r, self.fys.at[s], self.fyr.at[s], device(self.z, self.x, 1 - self.y, self.k)).wait_recv()
+        self.relay(s).start()
+
+    def finish(self):
+        z = self.z
+        for zz in range(4):
+            for yy in range(2):
+                self.core(zz, yy).wait_send()
+            self.yex(zz).wait_send()
+
+            @pl.when(z != zz)
+            def _():
+                self.up(zz).wait_send()
+        self.xex().wait_send()
+        for s in range(2):
+            seq = self.x if s == 0 else 1 - self.x
+            a, b, c = self.fin_copies(s)
+            a.wait()
+            b.wait_send()
+            c.wait_send()
+            self.relay(s).wait_send()
+            for j, yy in ((0, self.y), (1, 1 - self.y)):
+                r = self.spot(seq, 2 * yy + 1 - self.k)
+                remote(r, r, self.fcs.at[s, j], self.fcr.at[s, j], device(self.z, self.x, self.y, 1 - self.k)).wait_recv()
+
+
+def reduce_sems():
+    D = pltpu.SemaphoreType.DMA
+    return [D((4, 2)), D((4, 2)), D((4, 2)), D((4,)), D((4,)), D((4,)), D((5,)), D, D,
+            D((2,)), D((2,)), D((2,)), D((2, 2)), D((2, 2))]
+
+
+def reduce_bufs():
+    V = lambda *s: pltpu.VMEM(s, jnp.bfloat16)
+    return [V(4, 2, 2, 64, 2048), V(4, 2, 2, 64, 2048), V(4, 2, 64, 2048), V(5, 2, 64, 2048), V(64, 2048)]
+
+
+class GradReduce:
+    def __init__(self, pairs, own, got, sems):
+        self.pairs, self.own, self.got = pairs, own, got
+        self.ld, self.xs, self.xr, self.zs, self.zr = sems
+        self.z, self.x, self.y, self.k = place()
+
+    def load(self, d, w):
+        zz = (self.z + d) % 4
+        return pltpu.make_async_copy(self.pairs[w][0](zz, self.x), self.own[w].at[d], self.ld.at[d, w])
+
+    def xex(self, d, w):
+        zz = (self.z + d) % 4
+        return remote(self.pairs[w][0](zz, 1 - self.x), self.got[w].at[d], self.xs.at[d, w], self.xr.at[d, w],
+                      device(self.z, 1 - self.x, self.y, self.k))
+
+    def zex(self, d, w):
+        zz = (self.z + d) % 4
+        return remote(self.own[w].at[d], self.pairs[w][1](self.z), self.zs.at[d, w], self.zr.at[d, w],
+                      device(zz, self.x, self.y, self.k))
+
+    def keep(self, w):
+        return pltpu.make_async_copy(self.own[w].at[0], self.pairs[w][1](self.z), self.zs.at[0, w])
+
+    def start(self, d, w):
+        self.xex(d, w).start()
+        self.load(d, w).start()
+
+    def after_x(self, d, w):
+        self.load(d, w).wait()
+        self.xex(d, w).wait_recv()
+        add_into(self.own[w].at[d], self.got[w].at[d])
+        if d:
+            self.zex(d, w).start()
+        else:
+            self.keep(w).start()
+
+    def finish(self, w):
+        self.keep(w).wait()
+        for d in range(4):
+            self.xex(d, w).wait_send()
+            if d:
+                self.zex(d, w).wait_send()
+                frm = (self.z - d + 4) % 4
+                r = self.pairs[w][1](frm)
+                remote(r, r, self.zs.at[d, w], self.zr.at[d, w], device(frm, self.x, self.y, self.k)).wait_recv()
+
+
+BLOCKS = ((3, 256, 128), (256, 512), (512, 256), (128, 256))
+
+
+def grad_bufs():
+    return [pltpu.VMEM((4,) + b, jnp.bfloat16) for b in BLOCKS] * 2
+
+
+def grad_sems():
+    D = pltpu.SemaphoreType.DMA
+    return [D((4, 4)) for _ in range(5)]
+
+
+def reduce_kernel(po, pn, gin, gexp, gcon, gout, o_out, o_ng, o_gin, o_gexp, o_gcon, o_gout, *scratch):
+    z, x, y, k = place()
+    scratch = list(scratch)
+    take = lambda n: [scratch.pop(0) for _ in range(n)]
+    nb, ns = len(reduce_bufs()), len(reduce_sems())
+    to = TokenReduce(po, o_out, take(nb), take(ns))
+    tn = TokenReduce(pn, o_ng, take(nb), take(ns))
+    col = lambda n, i: pl.ds(pl.multiple_of(n * i, n), n)
+    pairs = [
+        (lambda zz, xx: gin.at[:, zz, xx], lambda zz: o_gin.at[:, :, col(128, zz)]),
+        (lambda zz, xx: gexp.at[zz, xx], lambda zz: o_gexp.at[:, col(512, zz)]),
+        (lambda zz, xx: gcon.at[:, col(256, zz * 2 + xx)], lambda zz: o_gcon.at[col(512, zz), :]),
+        (lambda zz, xx: gout.at[:, col(256, zz * 2 + xx)], lambda zz: o_gout.at[col(128, zz), :]),
+    ]
+    g = GradReduce(pairs, take(4), take(4), take(5))
+    meet([device((z + d) % 4, x, y, k) for d in (1, 2, 3)] + [device(z, 1 - x, y, k), device(z, x, 1 - y, k), device(z, x, y, 1 - k)])
+    ts = (to, tn)
+    for i in range(4):
+        for t in ts:
+            t.start(i)
+    for d in (2, 3, 1, 0):
+        for w in range(4):
+            g.start(d, w)
+    for i in range(5):
+        if i < 4:
+            for t in ts:
+                t.after_core(i)
+        if i >= 1:
+            for t in ts:
+                t.after_y(i - 1)
+                t.line(i - 1)
+        if i < 4:
+            for w in range(4):
+                g.after_x((2, 3, 1, 0)[i], w)
+    for s in range(2):
+        for t in ts:
+            t.spread(s)
+    for s in range(2):
+        for t in ts:
+            t.spread_y(s)
+    for t in ts:
+        t.finish()
+    for w in range(4):
+        g.finish(w)
+
+
+def reduce_call(po, pn, gin, gexp, gcon, gout):
+    bf = jnp.bfloat16
+    S = jax.ShapeDtypeStruct
+    ANY = pl.BlockSpec(memory_space=pl.ANY)
+    return pl.pallas_call(
+        reduce_kernel,
+        out_shape=[S((2, 256, 2048), bf), S((2, 256, 2048), bf), S((3, 256, 512), bf), S((256, 2048), bf), S((2048, 256), bf), S((512, 256), bf)],
+        in_specs=[ANY] * 6,
+        out_specs=[ANY] * 6,
+        scratch_shapes=(reduce_bufs() + reduce_sems()) * 2 + grad_bufs() + grad_sems(),
+        compiler_params=pltpu.CompilerParams(collective_id=1, has_side_effects=True, vmem_limit_bytes=56 * MB),
+        name="reduce",
+    )(po, pn, gin, gexp, gcon, gout)
+
+
+NT = (((1,), (1,)), ((), ()))
+
+
+def dot(a, b):
+    return jnp.dot(a, b, preferred_element_type=jnp.float32)
+
+
+def turn(v, tab, back=False):
+    cos, lo, hi = tab
+    if back:
+        return v * cos - pltpu.roll(v, 112, 1) * lo - pltpu.roll(v, 16, 1) * hi
+    return v * cos + pltpu.roll(v, 112, 1) * lo + pltpu.roll(v, 16, 1) * hi
+
+
+def attention_kernel(inv, proj, do, tab, mixed, pg, q, k, v, qt, kt, vt, dos, dot_, ot, dqt, dk, dv):
+    n = q.shape[1]
+    nb = n // 128
+    half = nb // 2
+
+    def source(b):
+        pair = jnp.where(b < half, b, nb - 1 - b)
+        return pl.multiple_of(inv[pair] * 256 + jnp.where(b < half, 0, 128), 128)
+
+    @pl.loop(0, nb)
+    def _(b):
+        src = pl.ds(source(b), 128)
+        here = pl.ds(pl.multiple_of(b * 128, 128), 128)
+        t = [tab[i, here] for i in range(3)]
+        rq = turn(proj[0, src], t).astype(jnp.bfloat16) * jnp.bfloat16(0.125)
+        rk = turn(proj[1, src], t).astype(jnp.bfloat16)
+        rv = proj[2, src].astype(jnp.bfloat16)
+        g = do[src]
+        qT, kT, vT, gT = (a.astype(jnp.float32).T.astype(jnp.bfloat16) for a in (rq, rk, rv, g))
+        for h in range(2):
+            at = slice(64 * h, 64 * h + 64)
+            q[h, here], k[h, here], v[h, here], dos[h, here] = rq[:, at], rk[:, at], rv[:, at], g[:, at]
+            qt[h, :, here], kt[h, :, here], vt[h, :, here], dot_[h, :, here] = qT[at], kT[at], vT[at], gT[at]
+
+    dk[...] = jnp.zeros_like(dk)
+    dv[...] = jnp.zeros_like(dv)
+
+    @pl.loop(0, 2)
+    def _(h):
+        for i in range(n // 256):
+            kr = 256 * (i + 1)
+            here = pl.ds(256 * i, 256)
+            gT = dot_[h, :, here]
+            st = dot(k[h, :kr], qt[h, :, here])
+            row = lax.broadcasted_iota(jnp.int32, (256, 256), 0)
+            column = lax.broadcasted_iota(jnp.int32, (256, 256), 1)
+            last = jnp.where(row <= column, st[kr - 256:], -1e30)
+            st = last if i == 0 else jnp.concatenate([st[:kr - 256], last], axis=0)
+            peak = jnp.max(st, axis=0, keepdims=True)
+            p = jnp.exp(st - peak)
+            p = p * (1.0 / jnp.sum(p, axis=0, keepdims=True))
+            low = p.astype(jnp.bfloat16)
+            o = dot(vt[h, :, :kr], low)
+            ot[h, :, here] = o
+            delta = jnp.sum(o * gT.astype(jnp.float32), axis=0, keepdims=True)
+            ds = (p * (dot(v[h, :kr], gT) - delta)).astype(jnp.bfloat16)
+            dv[h, :kr] += dot(low, dos[h, here])
+            dk[h, :kr] += dot(ds, q[h, here])
+            dqt[h, :, here] = dot(kt[h, :, :kr], ds) * 0.125
+
+    @pl.loop(0, nb)
+    def _(b):
+        dst = pl.ds(source(b), 128)
+        here = pl.ds(pl.multiple_of(b * 128, 128), 128)
+        t = [tab[i, here] for i in range(3)]
+        mixed[dst] = jnp.concatenate([ot[0, :, here], ot[1, :, here]], axis=0).T.astype(jnp.bfloat16)
+        gq = jnp.concatenate([dqt[0, :, here], dqt[1, :, here]], axis=0).T
+        gk = jnp.concatenate([dk[0, here], dk[1, here]], axis=1)
+        gv = jnp.concatenate([dv[0, here], dv[1, here]], axis=1)
+        pg[0, dst] = turn_back(gq, t).astype(jnp.bfloat16)
+        pg[1, dst] = turn_back(gk, t).astype(jnp.bfloat16)
+        pg[2, dst] = gv.astype(jnp.bfloat16)
+
+
+def turn_back(v, tab):
+    cos, lo, hi = tab
+    return v * cos - pltpu.roll(v, 112, 1) * lo - pltpu.roll(v, 16, 1) * hi
+
+
+def tables(n):
+    half = 16
+    frequency = 10000.0 ** (-2.0 * jnp.arange(half, dtype=jnp.float32) / 32)
+    angles = jnp.arange(n, dtype=jnp.int32).astype(jnp.float32)[:, None] * frequency
+    c, s = jnp.cos(angles), jnp.sin(angles)
+    one, zero = jnp.ones((n, 32), jnp.float32), jnp.zeros((n, 16), jnp.float32)
+    cos = jnp.concatenate([c, c, one] * 2, axis=1)
+    lo = jnp.concatenate([-s, zero, zero, zero] * 2, axis=1)
+    hi = jnp.concatenate([zero, s, zero, zero] * 2, axis=1)
+    return jnp.stack([cos, lo, hi])
+
+
+def attention_call(inv, proj, do, tab):
+    n = proj.shape[1]
+    bf, f4 = jnp.bfloat16, jnp.float32
+    S = jax.ShapeDtypeStruct
+    VM = pl.BlockSpec(memory_space=pltpu.VMEM)
+    V = pltpu.VMEM
+    return pl.pallas_call(
+        attention_kernel,
+        out_shape=[S((n, 128), bf), S((3, n, 128), bf)],
+        in_specs=[pl.BlockSpec(memory_space=pltpu.SMEM)] + [VM] * 3,
+        out_specs=[VM] * 2,
+        scratch_shapes=[V((2, n, 64), bf)] * 3 + [V((2, 64, n), bf)] * 3 + [V((2, n, 64), bf), V((2, 64, n), bf)]
+        + [V((2, 64, n), f4)] * 2 + [V((2, n, 64), f4)] * 2,
+        compiler_params=pltpu.CompilerParams(vmem_limit_bytes=56 * MB),
+        name="attention",
+    )(inv, proj, do, tab)
+
+def own_local(tokens, pair_index, norm_gain, norm_shift, w_attention_in, w_attention_out, w_expand, w_contract, cotangent):
+    f4, bf = jnp.float32, jnp.bfloat16
+    dots = functools.partial(jnp.einsum, preferred_element_type=f4)
+    x = lax.axis_index("ctx") % 2
+    pairs = lax.dynamic_index_in_dim(pair_index, x, 0, False)
+    which = jnp.arange(8, dtype=jnp.int32)
+    inverse = jnp.sum(jnp.where(pairs[None, :] == which[:, None], which[None, :], 0), axis=1).astype(jnp.int32)
+    gs = jnp.concatenate([norm_gain[None], norm_shift[None], jnp.zeros((6, 256), bf)], axis=0).astype(f4)
+    xn, ct, win, wout, wexp, wcon, gs_all = gather_call(tokens, gs, cotangent, w_attention_in, w_attention_out, w_expand, w_contract)
+    xn, ct = xn.reshape(2048, 2048), ct.reshape(2048, 2048)
+    win, wexp = win.reshape(3, 2048, 128), wexp.reshape(2048, 512)
+    proj = dots("td,kde->kte", xn, win)
+    mixed_grad = dots("td,ed->te", ct, wout).astype(bf)
+    mixed, pg = attention_call(inverse, proj, mixed_grad, tables(2048))
+    hidden = dots("td,df->tf", xn, wexp)
+    activated_full, pull = jax.vjp(gelu_tanh, hidden)
+    activated = activated_full.astype(bf)
+    out_part = (dots("te,ed->td", mixed, wout) + dots("tf,fd->td", activated, wcon)).astype(bf)
+    gcon = dots("tf,td->fd", activated, ct).astype(bf)
+    hidden_grad = pull(dots("td,fd->tf", ct, wcon))[0].astype(bf)
+    gout = dots("te,td->ed", mixed, ct).astype(bf)
+    gexp = dots("td,tf->df", xn, hidden_grad).astype(bf)
+    gin = dots("td,kte->kde", xn, pg).astype(bf)
+    ng_part = (dots("kte,kde->td", pg, win) + dots("tf,df->td", hidden_grad, wexp)).astype(bf)
+    out_sum, ng, gin, gexp, gcon, gout = reduce_call(
+        out_part.reshape(4, 2, 256, 2048), ng_part.reshape(4, 2, 256, 2048),
+        gin.reshape(3, 4, 2, 256, 128), gexp.reshape(4, 2, 256, 512), gcon, gout)
+    inputs = tokens.astype(f4)
+    output = (inputs + out_sum.astype(f4)).astype(bf)
+    gain, shift = gs_all[:, 0].reshape(2048), gs_all[:, 1].reshape(2048)
+    _, norm_pull = jax.vjp(layer_norm, inputs, gain, shift)
+    input_part, gain_grad, shift_grad = norm_pull(ng.astype(f4))
+    gain_grad, shift_grad = (
+        lax.psum_scatter(g, "ctx", scatter_dimension=0, tiled=True) for g in (gain_grad, shift_grad)
+    )
+    return (output, input_part + cotangent.astype(f4), gain_grad, shift_grad,
+            gin.astype(f4), gout.astype(f4), gexp.astype(f4), gcon.astype(f4))
+
+
+def local(tokens, pair_index, norm_gain, norm_shift, w_attention_in, w_attention_out, w_expand, w_contract, cotangent):
+    args = (tokens, pair_index, norm_gain, norm_shift, w_attention_in, w_attention_out, w_expand, w_contract, cotangent)
+    sizes = (lax.axis_size("ctx"), lax.axis_size("tp")) + tokens.shape + w_attention_in.shape[2:] + w_expand.shape[1:]
+    if sizes == (8, 4, 2, 256, 2048, 512, 2048):
+        return own_local(*args)
+    return general_local(*args)
+
+
 def solution(mesh):
     in_specs = (
         P(None, "ctx", None),

time: 1350 us -> 544 us (0.40)
  waiting for transfers between devices: 953 us -> 0 us
  Pallas kernels: 0 us -> 324 us
  matrix products: 199 us -> 104 us
  local copies, waits for them, and re-layouts: 59.1 us -> 16 us
  other arithmetic: 53.4 us -> 30.6 us
  between operations: 15.6 us -> 1.95 us
    reduce_scatter x6 -> x0, waiting for transfers between devices: 555 us -> none  [the longest x1 149 us: local(): lax.psum_scatter(contract_grad.astype(jnp.bfloat16), 'ctx', scatter_dimen...]
    pallas_call x0 -> x3, Pallas kernels: none -> 324 us  [the longest x1 154 us: gather_call(): pl.pallas_call(gather_kernel, out_shape=[S((4, 2, 256, 2048), bf), S((4,...]
    all_gather x6 -> x0, waiting for transfers between devices: 309 us -> none  [the longest x1 114 us: local(): lax.all_gather(w_expand, 'ctx', axis=0, tiled=True)]
    dot_general x26 -> x12, matrix products: 199 us -> 104 us  [the longest x1 12.6 us: own_local(): dots('tf,df->td', hidden_grad, wexp)]
    psum x1 -> x0, waiting for transfers between devices: 85.8 us -> none  [local(): branch = lax.psum(branch.astype(jnp.bfloat16), 'tp').astype(jnp.float32)]
    all_gather x2 -> x0, blocking collectives: 38.9 us -> none  [the longest x1 22.4 us: local(): lax.all_gather(norm_gain, 'ctx', axis=0, tiled=True)]
    unnamed x1, blocking collectives: 22.7 us -> 57.9 us
    reduce_sum x4 -> x1, other arithmetic: 19.3 us -> 0.63 us  [own_local(): jnp.sum(jnp.where(pairs[None, :] == which[:, None], which[None, :], 0), a...]
  transfers between devices with their start and end apart: 13 -> 0, of which waited for: 12 -> 0; matrix products, arithmetic and copies ran while one was open for 23% -> 0% of each run, Pallas kernels for 0% -> 0%
where the time goes in v1:
time: 544 us; the launch traced here: 535 us
  Pallas kernels  324 us (60%)
  matrix products  104 us (19%)
  blocking collectives  57.9 us (11%)
  other arithmetic  30.6 us (6%)
  local copies, waits for them, and re-layouts  16 us (3%)
    pallas_call x1, Pallas kernels, gather_call(): pl.pallas_call(gather_kernel, out_shape=[S((4, 2, 256, 2048), bf), S((4,...  154 us
    pallas_call x1, Pallas kernels, reduce_call(): pl.pallas_call(reduce_kernel, out_shape=[S((2, 256, 2048), bf), S((2, 256...  134 us
    unnamed x1, blocking collectives  57.9 us
    pallas_call x1, Pallas kernels, attention_call(): pl.pallas_call(attention_kernel, out_shape=[S((n, 128), bf), S((3, n, 128...  36.6 us
    dot_general x1, matrix products, own_local(): dots('tf,df->td', hidden_grad, wexp)  12.6 us
    dot_general x1, matrix products, own_local(): dots('te,ed->td', mixed, wout) + dots('tf,fd->td', activated, wcon)  11.4 us
    dot_general x1, matrix products, own_local(): gcon = dots('tf,td->fd', activated, ct).astype(bf)  11.1 us
    dot_general x1, matrix products, own_local(): dots('tf,fd->td', activated, wcon)  11 us

profile of v1, /device:TPU:0, one launch (start us, length us, event | category | flops | bytes accessed | tf_op | source)
XLA Modules:
  0.0 534.6 jit_solution(7684833955317651555)
XLA Ops:
  0.6 0.0 copy-start
  0.7 1.2 dynamic-slice
  2.6 0.0 copy-done
  2.6 0.6 select_reduce_fusion.inv
  3.2 0.1 pad.9.clone
  3.3 0.7 broadcast_in_dim.42
  4.0 0.7 broadcast_in_dim.43
  4.6 1.9 convert_reduce_fusion.1
  6.6 0.1 maximum_convert_fusion.gs
  6.7 5.3 multiply_cosine_fusion
  12.0 0.1 broadcast.68
  12.1 1.0 concatenate.18
  13.1 1.0 broadcast_in_dim.46
  14.2 4.2 concatenate.19
  18.3 0.1 broadcast_in_dim.45
  18.4 3.0 concatenate.16
  21.4 2.6 maximum_bitcast_fusion
  24.0 3.5 pad_maximum_fusion.tab
  27.5 0.0 copy-done.2
  27.5 0.0 copy-done.3
  27.5 0.0 copy-done.4
  27.5 0.0 copy-done.5
  27.5 153.7 %gather.1 = (bf16[4,2,256,2048]{3,2,1,0:T(8,128)(2,1)}, bf16[4,2,256,2048]{3,2,1,0:T(8,128)(2,1)}, bf16[3,4,2,256,128]{4,3,2,1,0:T(8,128)(2,1)S(1)}, bf16[128,20...) custom-call(bf16[2,256,2048]{2,1,0:T(8,128)(2,1)} %tok.1, ...), custom_call_target="tpu_custom_call" | custom-call | tf_op jit(solution)/shard_map/gather/pallas_call | solution.py:629
  181.2 0.0 copy-start.16
  181.2 6.7 %convolution_convert_fusion.4.do = bf16[2048,128]{1,0:T(8,128)(2,1)} fusion(bf16[2048,2048]{1,0:T(8,128)(2,1)} %bitcast.50, bf16[128,2048]{1,0:T(8,128)(2,1)S(1)} %get-tuple-element.26), kind=kOutput, calls=%fused_computation.39 | convolution fusion | flops 1074003968 | bytes 9437184 | tf_op jit(solution)/shard_map/td,ed->te/dot_general | solution.py:1062
  187.9 6.3 %convolution_bitcast_fusion.proj = f32[3,2048,128]{2,1,0:T(8,128)} fusion(bf16[2048,2048,1]{1,0,2:T(8,128)(2,1)S(1)} %bitcast.64, bf16[3,2048,128]{2,1,0:T(8,128)(2,1)S(1)} %bitcast.46), kind=kOutput, calls=%fused_computation.32 | convolution fusion | flops 3221225472 | bytes 13107200 | tf_op jit(solution)/shard_map/td,kde->kte/dot_general | solution.py:1061
  194.3 36.6 %attention.1 = (bf16[2048,128]{1,0:T(8,128)(2,1)}, bf16[3,2048,128]{2,1,0:T(8,128)(2,1)}) custom-call(s32[8]{0:T(128)} %select_reduce_fusion.inv, f32[3,2048,128]{2,1,0:T(8,128)} %convolution_bitcast_fusion.proj, bf16[2048,128]{1,0:T(8,128)(2,1)} %convolution_convert_fusion.4.do, f32[3,2048,128]{2,1,0:T(8,128)} %pad_maximum_fusion.tab), custom_call_target="tpu_custom_call" | custom-call | tf_op jit(solution)/shard_map/attention/pallas_call | solution.py:1039
  230.9 5.8 %convolution_convert_fusion.3.gout = bf16[128,2048]{1,0:T(8,128)(2,1)} fusion(bf16[2048,128]{1,0:T(8,128)(2,1)} %get-tuple-element.27, bf16[2048,2048]{1,0:T(8,128)(2,1)} %bitcast.51), kind=kOutput, calls=%fused_computation.38 | convolution fusion | flops 1074003968 | bytes 9437184 | tf_op jit(solution)/shard_map/te,td->ed/dot_general | solution.py:1070
  236.7 0.0 slice-done.3
  236.7 4.9 fusion.17
  241.6 2.6 copy.33
  244.2 7.7 %fusion.24 = f32[2048,512]{1,0:T(8,128)S(1)} fusion(bf16[2048,2048]{1,0:T(8,128)(2,1)} %bitcast.63, bf16[2048,512]{1,0:T(8,128)(2,1)} %bitcast.71), kind=kOutput, calls=%fused_computation.57 | convolution fusion | flops 4294967296 | bytes 14680064 | tf_op jit(solution)/shard_map/td,df->tf/dot_general | solution.py:1064
  251.9 0.0 copy-start.19
  251.9 0.0 slice-start.1
  251.9 0.0 copy-start.17
  251.9 0.0 slice-start.5
  251.9 11.1 %convolution_convert_fusion.gcon = bf16[512,2048]{1,0:T(8,128)(2,1)} fusion(bf16[2048,2048]{1,0:T(8,128)(2,1)} %bitcast.52, f32[2048,512]{1,0:T(8,128)S(1)} %fusion.24), kind=kOutput, calls=%fused_computation.33 | convolution fusion | flops 4305453056 | bytes 14680064 | tf_op jit(solution)/shard_map/tf,td->fd/dot_general | solution.py:1068
  263.0 6.6 %fusion.25 = f32[2048,512]{1,0:T(8,128)} fusion(bf16[2048,2048]{1,0:T(8,128)(2,1)S(1)} %bitcast.55, bf16[512,2048]{1,0:T(8,128)(2,1)S(1)} %copy-done.17), kind=kOutput, calls=%fused_computation.58 | convolution fusion | flops 4294967296 | bytes 14680064 | tf_op jit(solution)/shard_map/td,fd->tf/dot_general | solution.py:1069
  269.6 0.0 slice-done.4
  269.6 0.0 slice-done.5
  269.6 0.0 copy-start.18
  269.6 9.8 %convolution_convert_fusion.1 = bf16[2048,512]{1,0:T(8,128)(2,1)} fusion(bf16[2048,2048]{1,0:T(8,128)(2,1)S(1)} %bitcast.70, f32[2048,512]{1,0:T(8,128)S(1)} %fusion.24, f32[2048,512]{1,0:T(8,128)} %fusion.25), kind=kOutput, calls=%fused_computation.34 | convolution fusion | flops 4321181696 | bytes 18874368 | tf_op jit(solution)/shard_map/td,tf->df/dot_general | solution.py:1071
  279.4 0.0 copy-done.18
  279.4 12.6 %fusion.22 = f32[2048,2048]{1,0:T(8,128)} fusion(bf16[2048,512]{1,0:T(8,128)(2,1)S(1)} %bitcast.72, f32[2048,512]{1,0:T(8,128)S(1)} %fusion.24, f32[2048,512]{1,0:T(8,128)} %fusion.25), kind=kOutput, calls=%fused_computation.56 | convolution fusion | flops 4320133120 | bytes 27262976 | tf_op jit(solution)/shard_map/tf,df->td/dot_general | solution.py:1073
  292.0 10.3 %fusion = bf16[2048,2048]{1,0:T(8,128)(2,1)} fusion(f32[2048,2048]{1,0:T(8,128)} %fusion.22, bf16[3,2048,128]{2,1,0:T(8,128)(2,1)S(1)} %copy-done.11, bf16[3,2048,128]{2,1,0:T(8,128)(2,1)S(1)} %bitcast.47), kind=kOutput, calls=%fused_computation.1 | convolution fusion | flops 3229614080 | bytes 28311552 | tf_op jit(solution)/shard_map/kte,kde->td/dot_general | solution.py:1073
  302.3 11.0 %fusion.20 = f32[2048,2048]{1,0:T(8,128)} fusion(bf16[512,2048]{1,0:T(8,128)(2,1)S(1)} %copy-done.17, f32[2048,512]{1,0:T(8,128)} %copy-done.19), kind=kOutput, calls=%fused_computation.55 | convolution fusion | flops 4304404480 | bytes 23068672 | tf_op jit(solution)/shard_map/tf,fd->td/dot_general | solution.py:1067
  313.3 0.0 copy-done.9
  313.3 11.4 %add_convert_fusion = bf16[2048,2048]{1,0:T(8,128)(2,1)} fusion(f32[2048,2048]{1,0:T(8,128)} %fusion.20, bf16[2048,128]{1,0:T(8,128)(2,1)S(1)} %copy-done.9, bf16[128,2048]{1,0:T(8,128)(2,1)S(1)} %get-tuple-element.26), kind=kOutput, calls=%fused_computation.2 | convolution fusion | flops 1082130432 | bytes 26214400 | tf_op jit(solution)/shard_map/te,ed->td/dot_general | solution.py:1067
  324.7 133.8 %reduce.1 = (bf16[2,256,2048]{2,1,0:T(8,128)(2,1)}, bf16[2,256,2048]{2,1,0:T(8,128)(2,1)}, bf16[3,256,512]{2,1,0:T(8,128)(2,1)}, bf16[256,2048]{1,0:T(8,128)(2,1...) custom-call(bf16[4,2,256,2048]{3,2,1,0:T(8,128)(2,1)} %bitcast.49, bf16[4,2,256,2048]{3,2,1,0:T(8,128)(2,1)} %bitcast.48, ...), custom_call_target="tpu_custom_call" | custom-call | tf_op jit(solution)/shard_map/reduce/pallas_call | solution.py:927
  458.5 0.0 copy-start.7
  458.5 0.0 copy-done.6
  458.5 0.0 copy-start.15
  458.5 0.0 copy-start.14
  458.5 3.5 fusion.10
  462.0 0.0 copy-done.7
  462.0 2.1 fusion.15
  464.1 57.9 %all-reduce.2 = (f32[2048]{0:T(1024)S(1)}, f32[2048]{0:T(1024)S(1)}) all-reduce(f32[2048]{0:T(1024)S(1)} %get-tuple-element.38, f32[2048]{0:T(1024)S(1)} %get-tuple-element.42), channel_id=2, replica_groups=mesh['ctx'=8,'tp'=4] {'ctx'}, use_global_device_ids=true, to_apply=%region_6.7.clone | all-reduce | flops 4096 | bytes 32768
  522.0 0.6 dynamic-slice.1
  522.7 0.6 dynamic-slice.3
  523.3 0.8 convert_element_type.99
  524.1 1.4 convert_element_type.98
  525.5 5.7 %convert_add_fusion.1 = (f32[2,256,2048]{2,1,0:T(8,128)}, bf16[2,256,2048]{2,1,0:T(8,128)(2,1)}) fusion(bf16[2,256,2048]{2,1,0:T(8,128)(2,1)} %cot.1, bf16[2,256,2048]{2,1,0:T(8,128)(2,1)S(1)} %copy-done.6, bf16[2,256,2048]{2,1,0:T(8,128)(2,1)S(1)} %copy-done.8, f32[2,256]{1,0:T(2,128)S(1)} %negate_multiply_fusion, f32[2,256]{1,0:T(2,128)S(1)} %get-tuple-element.50, ...), kind=kLoop, calls=%fused_computation.29 | loop fusion | flops 14680064 | bytes 14696448 | tf_op jit(solution)/shard_map/add | solution.py:1085
  531.2 1.6 convert_element_type.100
  532.8 1.5 convert_element_type.101
  (41 shorter events, 0.1 us)
Async XLA Ops:
  0.6 1.9 copy-start
  21.4 6.1 %copy-start.2 = (bf16[256,2048]{1,0:T(8,128)(2,1)S(1)}, bf16[256,2048]{1,0:T(8,128)(2,1)}, u32[]{:S(2)}) copy-start(bf16[256,2048]{1,0:T(8,128)(2,1)} %wexp.1) | copy-start | bytes 3145732
  21.4 6.1 %copy-start.3 = (bf16[2048,256]{1,0:T(8,128)(2,1)S(1)}, bf16[2048,256]{1,0:T(8,128)(2,1)}, u32[]{:S(2)}) copy-start(bf16[2048,256]{1,0:T(8,128)(2,1)} %wcon.1) | copy-start | bytes 3145732
  21.4 6.1 %copy-start.4 = (bf16[3,256,512]{2,1,0:T(8,128)(2,1)S(1)}, bf16[3,256,512]{2,1,0:T(8,128)(2,1)}, u32[]{:S(2)}) copy-start(bf16[3,256,512]{2,1,0:T(8,128)(2,1)} %win.1) | copy-start | bytes 2359300
  21.4 6.1 %copy-start.5 = (bf16[512,256]{1,0:T(8,128)(2,1)S(1)}, bf16[512,256]{1,0:T(8,128)(2,1)}, u32[]{:S(2)}) copy-start(bf16[512,256]{1,0:T(8,128)(2,1)} %wout.1) | copy-start | bytes 786436
  181.2 6.7 %copy-start.16 = (bf16[4,2,256,2048]{3,2,1,0:T(8,128)(2,1)S(1)}, bf16[4,2,256,2048]{3,2,1,0:T(8,128)(2,1)}, u32[]{:S(2)}) copy-start(bf16[4,2,256,2048]{3,2,1,0:T(8,128)(2,1)} %get-tuple-element.24) | copy-start | bytes 25165828
  194.3 42.4 %slice-start.2 = ((s8[8388608]{0:T(1024)(128)(4,1)}), s8[4194304]{0:T(1024)(128)(4,1)S(1)}, s32[]{:S(2)}) async-start(s8[8388608]{0:T(1024)(128)(4,1)} %bitcast.65), calls=%async_computation.2 | async-start | bytes 8388608
  230.9 5.8 %copy-start.10 = (bf16[3,2048,128]{2,1,0:T(8,128)(2,1)S(1)}, bf16[3,2048,128]{2,1,0:T(8,128)(2,1)}, u32[]{:S(2)}) copy-start(bf16[3,2048,128]{2,1,0:T(8,128)(2,1)} %get-tuple-element.30) | copy-start | bytes 4718596
  230.9 5.8 %slice-start.3 = ((s8[8388608]{0:T(1024)(128)(4,1)}), s8[4194304]{0:T(1024)(128)(4,1)S(1)}, s32[]{:S(2)}) async-start(s8[8388608]{0:T(1024)(128)(4,1)} %bitcast.65), calls=%async_computation.3 | async-start | bytes 8388608
  244.2 18.8 %slice-start = ((s8[8388608]{0:T(1024)(128)(4,1)}), s8[4194304]{0:T(1024)(128)(4,1)S(1)}, s32[]{:S(2)}) async-start(s8[8388608]{0:T(1024)(128)(4,1)} %bitcast.53), calls=%async_computation | async-start | bytes 8388608
  244.2 25.4 %slice-start.4 = ((s8[8388608]{0:T(1024)(128)(4,1)}), s8[4194304]{0:T(1024)(128)(4,1)S(1)}, s32[]{:S(2)}) async-start(s8[8388608]{0:T(1024)(128)(4,1)} %bitcast.68), calls=%async_computation.4 | async-start | bytes 8388608
  251.9 27.5 %copy-start.19 = (f32[2048,512]{1,0:T(8,128)}, f32[2048,512]{1,0:T(8,128)S(1)}, u32[]{:S(2)}) copy-start(f32[2048,512]{1,0:T(8,128)S(1)} %fusion.24) | copy-start | bytes 12582916
  251.9 11.1 %slice-start.1 = ((s8[8388608]{0:T(1024)(128)(4,1)}), s8[4194304]{0:T(1024)(128)(4,1)S(1)}, s32[]{:S(2)}) async-start(s8[8388608]{0:T(1024)(128)(4,1)} %bitcast.53), calls=%async_computation.1 | async-start | bytes 8388608
  251.9 11.1 %copy-start.17 = (bf16[512,2048]{1,0:T(8,128)(2,1)S(1)}, bf16[512,2048]{1,0:T(8,128)(2,1)}, u32[]{:S(2)}) copy-start(bf16[512,2048]{1,0:T(8,128)(2,1)} %get-tuple-element.29) | copy-start | bytes 6291460
  251.9 17.7 %slice-start.5 = ((s8[8388608]{0:T(1024)(128)(4,1)}), s8[4194304]{0:T(1024)(128)(4,1)S(1)}, s32[]{:S(2)}) async-start(s8[8388608]{0:T(1024)(128)(4,1)} %bitcast.68), calls=%async_computation.5 | async-start | bytes 8388608
  269.6 9.8 %copy-start.18 = (bf16[4,2,256,512]{3,2,1,0:T(8,128)(2,1)S(1)}, bf16[4,2,256,512]{3,2,1,0:T(8,128)(2,1)}, u32[]{:S(2)}) copy-start(bf16[4,2,256,512]{3,2,1,0:T(8,128)(2,1)} %get-tuple-element.28) | copy-start | bytes 6291460
  279.4 12.6 %copy-start.11 = (bf16[3,2048,128]{2,1,0:T(8,128)(2,1)S(1)}, bf16[3,2048,128]{2,1,0:T(8,128)(2,1)}, u32[]{:S(2)}) copy-start(bf16[3,2048,128]{2,1,0:T(8,128)(2,1)} %get-tuple-element.30) | copy-start | bytes 4718596
  302.3 11.0 %copy-start.9 = (bf16[2048,128]{1,0:T(8,128)(2,1)S(1)}, bf16[2048,128]{1,0:T(8,128)(2,1)}, u32[]{:S(2)}) copy-start(bf16[2048,128]{1,0:T(8,128)(2,1)} %get-tuple-element.27) | copy-start | bytes 1572868
  324.7 133.8 %copy-start.6 = (bf16[2,256,2048]{2,1,0:T(8,128)(2,1)S(1)}, bf16[2,256,2048]{2,1,0:T(8,128)(2,1)}, u32[]{:S(2)}) copy-start(bf16[2,256,2048]{2,1,0:T(8,128)(2,1)} %tok.1) | copy-start | bytes 6291460
  458.5 3.5 copy-start.7
  458.5 64.8 %copy-start.15 = (bf16[512,256]{1,0:T(8,128)(2,1)S(1)}, bf16[512,256]{1,0:T(8,128)(2,1)}, u32[]{:S(2)}) copy-start(bf16[512,256]{1,0:T(8,128)(2,1)} %get-tuple-element.35) | copy-start | bytes 786436
  458.5 65.6 %copy-start.14 = (bf16[3,256,512]{2,1,0:T(8,128)(2,1)S(1)}, bf16[3,256,512]{2,1,0:T(8,128)(2,1)}, u32[]{:S(2)}) copy-start(bf16[3,256,512]{2,1,0:T(8,128)(2,1)} %get-tuple-element.34) | copy-start | bytes 2359300
  522.0 3.5 copy-start.8
  525.5 5.7 %copy-start.13 = (bf16[256,2048]{1,0:T(8,128)(2,1)S(1)}, bf16[256,2048]{1,0:T(8,128)(2,1)}, u32[]{:S(2)}) copy-start(bf16[256,2048]{1,0:T(8,128)(2,1)} %get-tuple-element.36) | copy-start | bytes 3145732
  525.5 7.3 %copy-start.12 = (bf16[2048,256]{1,0:T(8,128)(2,1)S(1)}, bf16[2048,256]{1,0:T(8,128)(2,1)}, u32[]{:S(2)}) copy-start(bf16[2048,256]{1,0:T(8,128)(2,1)} %get-tuple-element.37) | copy-start | bytes 3145732
  525.5 8.8 %copy-start.1 = (s32[2,8]{1,0:T(2,128)S(1)}, s32[2,8]{1,0:T(2,128)}, u32[]{:S(2)}) copy-start(s32[2,8]{1,0:T(2,128)} %param.10) | copy-start | bytes 196

commit v2 on v1

--- a/solution.py
+++ b/solution.py
@@ -3,6 +3,7 @@
 
 import jax
 import jax.numpy as jnp
+import numpy as np
 from jax import lax
 from jax.experimental import pallas as pl
 from jax.experimental.pallas import tpu as pltpu
@@ -874,9 +875,32 @@
     return [D((4, 4)) for _ in range(5)]
 
 
-def reduce_kernel(po, pn, gin, gexp, gcon, gout, o_out, o_ng, o_gin, o_gexp, o_gcon, o_gout, *scratch):
+def norm_backward(tok, cot, ng, gains, out, sums):
+    gain = jnp.concatenate([gains[i, 0:1, :] for i in range(8)], axis=1)
+    sums[...] = jnp.zeros_like(sums)
+
+    @pl.loop(0, 32)
+    def _(i):
+        s, at = i // 16, pl.ds(pl.multiple_of(16 * (i % 16), 16), 16)
+        v = tok[s, at].astype(jnp.float32)
+        centred = v - jnp.mean(v, axis=-1, keepdims=True)
+        scale = lax.rsqrt(jnp.mean(centred * centred, axis=-1, keepdims=True) + EPS)
+        xhat = centred * scale
+        n = ng[s, at].astype(jnp.float32)
+        g = n * gain
+        along = jnp.mean(g * xhat, axis=-1, keepdims=True)
+        out[s, at] = cot[s, at].astype(jnp.float32) + (g - jnp.mean(g, axis=-1, keepdims=True) - xhat * along) * scale
+        both = n * xhat
+        sums[0] += both[:8] + both[8:]
+        sums[1] += n[:8] + n[8:]
+
+
+def reduce_kernel(po, pn, gin, gexp, gcon, gout, tok, cot, gains, o_out, o_ig, o_gs, o_gin, o_gexp, o_gcon, o_gout, *scratch):
     z, x, y, k = place()
+    c = z * 2 + x
+    others = [((c + i) % 8, lax.axis_index("tp")) for i in range(1, 8)]
     scratch = list(scratch)
+    o_ng, sums, vec, vecs, vs, vr = (scratch.pop(0) for _ in range(6))
     take = lambda n: [scratch.pop(0) for _ in range(n)]
     nb, ns = len(reduce_bufs()), len(reduce_sems())
     to = TokenReduce(po, o_out, take(nb), take(ns))
@@ -889,7 +913,7 @@
         (lambda zz, xx: gout.at[:, col(256, zz * 2 + xx)], lambda zz: o_gout.at[col(128, zz), :]),
     ]
     g = GradReduce(pairs, take(4), take(4), take(5))
-    meet([device((z + d) % 4, x, y, k) for d in (1, 2, 3)] + [device(z, 1 - x, y, k), device(z, x, 1 - y, k), device(z, x, y, 1 - k)])
+    meet(others + [device(z, x, 1 - y, k), device(z, x, y, 1 - k)])
     ts = (to, tn)
     for i in range(4):
         for t in ts:
@@ -914,25 +938,46 @@
     for s in range(2):
         for t in ts:
             t.spread_y(s)
-    for t in ts:
-        t.finish()
+    tn.finish()
+    norm_backward(tok, cot, o_ng, gains, o_ig, sums)
+    for i in range(8):
+        at = slice(256 * i, 256 * i + 256)
+        for j in range(2):
+            vec[i, j:j + 1, :] = jnp.sum(sums[j, :, at], axis=0, keepdims=True)
+    vecs[c] = vec[c]
+    copies = [remote(vec.at[(c + i + 1) % 8], vecs.at[c], vs.at[i], vr.at[i], others[i]) for i in range(7)]
+    for cp in copies:
+        cp.start()
+    to.finish()
     for w in range(4):
         g.finish(w)
-
-
-def reduce_call(po, pn, gin, gexp, gcon, gout):
-    bf = jnp.bfloat16
+    for i in range(7):
+        frm = vecs.at[(c - i - 1 + 8) % 8]
+        remote(frm, frm, vs.at[i], vr.at[i], others[i]).wait_recv()
+    total = vecs[0]
+    for i in range(1, 8):
+        total = total + vecs[i]
+    o_gs[...] = total
+    for cp in copies:
+        cp.wait_send()
+
+
+def reduce_call(po, pn, gin, gexp, gcon, gout, tok, cot, gains):
+    bf, f4 = jnp.bfloat16, jnp.float32
+    VM = pl.BlockSpec(memory_space=pltpu.VMEM)
+    V = pltpu.VMEM
+    D = pltpu.SemaphoreType.DMA
     S = jax.ShapeDtypeStruct
     ANY = pl.BlockSpec(memory_space=pl.ANY)
     return pl.pallas_call(
         reduce_kernel,
-        out_shape=[S((2, 256, 2048), bf), S((2, 256, 2048), bf), S((3, 256, 512), bf), S((256, 2048), bf), S((2048, 256), bf), S((512, 256), bf)],
-        in_specs=[ANY] * 6,
-        out_specs=[ANY] * 6,
-        scratch_shapes=(reduce_bufs() + reduce_sems()) * 2 + grad_bufs() + grad_sems(),
+        out_shape=[S((2, 256, 2048), bf), S((2, 256, 2048), f4), S((8, 256), f4), S((3, 256, 512), bf), S((256, 2048), bf), S((2048, 256), bf), S((512, 256), bf)],
+        in_specs=[ANY] * 6 + [VM] * 3,
+        out_specs=[ANY, VM, VM] + [ANY] * 4,
+        scratch_shapes=[V((2, 256, 2048), bf), V((2, 8, 2048), f4), V((8, 8, 256), f4), V((8, 8, 256), f4), D((7,)), D((7,))] + (reduce_bufs() + reduce_sems()) * 2 + grad_bufs() + grad_sems(),
         compiler_params=pltpu.CompilerParams(collective_id=1, has_side_effects=True, vmem_limit_bytes=56 * MB),
         name="reduce",
-    )(po, pn, gin, gexp, gcon, gout)
+    )(po, pn, gin, gexp, gcon, gout, tok, cot, gains)
 
 
 NT = (((1,), (1,)), ((), ()))
@@ -942,14 +987,32 @@
     return jnp.dot(a, b, preferred_element_type=jnp.float32)
 
 
-def turn(v, tab, back=False):
+def turn(v, tab):
     cos, lo, hi = tab
-    if back:
-        return v * cos - pltpu.roll(v, 112, 1) * lo - pltpu.roll(v, 16, 1) * hi
     return v * cos + pltpu.roll(v, 112, 1) * lo + pltpu.roll(v, 16, 1) * hi
 
 
-def attention_kernel(inv, proj, do, tab, mixed, pg, q, k, v, qt, kt, vt, dos, dot_, ot, dqt, dk, dv):
+def turn_back(v, tab):
+    cos, lo, hi = tab
+    return v * cos - pltpu.roll(v, 112, 1) * lo - pltpu.roll(v, 16, 1) * hi
+
+
+def angle_table(within, block, b):
+    cr, sr = within[0], within[1]
+    cb, sb = block[0, pl.ds(b, 1)], block[1, pl.ds(b, 1)]
+    cos, sin = cb * cr - sb * sr, sb * cr + cb * sr
+    entry = lax.broadcasted_iota(jnp.int32, cos.shape, 1) % 64
+    return cos, jnp.where(entry < 16, -sin, 0.0), jnp.where(entry < 16, 0.0, sin)
+
+
+def angles(rows, step):
+    frequency = (10000.0 ** (-2.0 * np.arange(16) / 32)).astype(np.float32).astype(np.float64)
+    lanes = np.concatenate([frequency, frequency, np.zeros(32)] * 2)
+    angle = step * np.arange(rows)[:, None] * lanes
+    return np.stack([np.cos(angle), np.sin(angle)]).astype(np.float32)
+
+
+def attention_kernel(inv, proj, do, within, block, mixed, pg, q, k, v, qt, kt, vt, dos, dot_, ot, dqt, dk, dv):
     n = q.shape[1]
     nb = n // 128
     half = nb // 2
@@ -962,7 +1025,7 @@
     def _(b):
         src = pl.ds(source(b), 128)
         here = pl.ds(pl.multiple_of(b * 128, 128), 128)
-        t = [tab[i, here] for i in range(3)]
+        t = angle_table(within, block, b)
         rq = turn(proj[0, src], t).astype(jnp.bfloat16) * jnp.bfloat16(0.125)
         rk = turn(proj[1, src], t).astype(jnp.bfloat16)
         rv = proj[2, src].astype(jnp.bfloat16)
@@ -1003,7 +1066,7 @@
     def _(b):
         dst = pl.ds(source(b), 128)
         here = pl.ds(pl.multiple_of(b * 128, 128), 128)
-        t = [tab[i, here] for i in range(3)]
+        t = angle_table(within, block, b)
         mixed[dst] = jnp.concatenate([ot[0, :, here], ot[1, :, here]], axis=0).T.astype(jnp.bfloat16)
         gq = jnp.concatenate([dqt[0, :, here], dqt[1, :, here]], axis=0).T
         gk = jnp.concatenate([dk[0, here], dk[1, here]], axis=1)
@@ -1013,24 +1076,7 @@
         pg[2, dst] = gv.astype(jnp.bfloat16)
 
 
-def turn_back(v, tab):
-    cos, lo, hi = tab
-    return v * cos - pltpu.roll(v, 112, 1) * lo - pltpu.roll(v, 16, 1) * hi
-
-
-def tables(n):
-    half = 16
-    frequency = 10000.0 ** (-2.0 * jnp.arange(half, dtype=jnp.float32) / 32)
-    angles = jnp.arange(n, dtype=jnp.int32).astype(jnp.float32)[:, None] * frequency
-    c, s = jnp.cos(angles), jnp.sin(angles)
-    one, zero = jnp.ones((n, 32), jnp.float32), jnp.zeros((n, 16), jnp.float32)
-    cos = jnp.concatenate([c, c, one] * 2, axis=1)
-    lo = jnp.concatenate([-s, zero, zero, zero] * 2, axis=1)
-    hi = jnp.concatenate([zero, s, zero, zero] * 2, axis=1)
-    return jnp.stack([cos, lo, hi])
-
-
-def attention_call(inv, proj, do, tab):
+def attention_call(inv, proj, do):
     n = proj.shape[1]
     bf, f4 = jnp.bfloat16, jnp.float32
     S = jax.ShapeDtypeStruct
@@ -1039,13 +1085,13 @@
     return pl.pallas_call(
         attention_kernel,
         out_shape=[S((n, 128), bf), S((3, n, 128), bf)],
-        in_specs=[pl.BlockSpec(memory_space=pltpu.SMEM)] + [VM] * 3,
+        in_specs=[pl.BlockSpec(memory_space=pltpu.SMEM)] + [VM] * 4,
         out_specs=[VM] * 2,
         scratch_shapes=[V((2, n, 64), bf)] * 3 + [V((2, 64, n), bf)] * 3 + [V((2, n, 64), bf), V((2, 64, n), bf)]
         + [V((2, 64, n), f4)] * 2 + [V((2, n, 64), f4)] * 2,
         compiler_params=pltpu.CompilerParams(vmem_limit_bytes=56 * MB),
         name="attention",
-    )(inv, proj, do, tab)
+    )(inv, proj, do, jnp.asarray(angles(128, 1)), jnp.asarray(angles(n // 128, 128)))
 
 def own_local(tokens, pair_index, norm_gain, norm_shift, w_attention_in, w_attention_out, w_expand, w_contract, cotangent):
     f4, bf = jnp.float32, jnp.bfloat16
@@ -1060,7 +1106,7 @@
     win, wexp = win.reshape(3, 2048, 128), wexp.reshape(2048, 512)
     proj = dots("td,kde->kte", xn, win)
     mixed_grad = dots("td,ed->te", ct, wout).astype(bf)
-    mixed, pg = attention_call(inverse, proj, mixed_grad, tables(2048))
+    mixed, pg = attention_call(inverse, proj, mixed_grad)
     hidden = dots("td,df->tf", xn, wexp)
     activated_full, pull = jax.vjp(gelu_tanh, hidden)
     activated = activated_full.astype(bf)
@@ -1071,18 +1117,11 @@
     gexp = dots("td,tf->df", xn, hidden_grad).astype(bf)
     gin = dots("td,kte->kde", xn, pg).astype(bf)
     ng_part = (dots("kte,kde->td", pg, win) + dots("tf,df->td", hidden_grad, wexp)).astype(bf)
-    out_sum, ng, gin, gexp, gcon, gout = reduce_call(
+    out_sum, input_grad, vectors, gin, gexp, gcon, gout = reduce_call(
         out_part.reshape(4, 2, 256, 2048), ng_part.reshape(4, 2, 256, 2048),
-        gin.reshape(3, 4, 2, 256, 128), gexp.reshape(4, 2, 256, 512), gcon, gout)
-    inputs = tokens.astype(f4)
-    output = (inputs + out_sum.astype(f4)).astype(bf)
-    gain, shift = gs_all[:, 0].reshape(2048), gs_all[:, 1].reshape(2048)
-    _, norm_pull = jax.vjp(layer_norm, inputs, gain, shift)
-    input_part, gain_grad, shift_grad = norm_pull(ng.astype(f4))
-    gain_grad, shift_grad = (
-        lax.psum_scatter(g, "ctx", scatter_dimension=0, tiled=True) for g in (gain_grad, shift_grad)
-    )
-    return (output, input_part + cotangent.astype(f4), gain_grad, shift_grad,
+        gin.reshape(3, 4, 2, 256, 128), gexp.reshape(4, 2, 256, 512), gcon, gout, tokens, cotangent, gs_all)
+    output = (tokens.astype(f4) + out_sum.astype(f4)).astype(bf)
+    return (output, input_grad, vectors[0], vectors[1],
             gin.astype(f4), gout.astype(f4), gexp.astype(f4), gcon.astype(f4))
 
 

time: 544 us -> 502 us (0.923)
  blocking collectives: 57.9 us -> 0 us
  Pallas kernels: 324 us -> 368 us
  other arithmetic: 30.6 us -> 9.9 us
    unnamed x1 -> x0, blocking collectives: 57.9 us -> none
    pallas_call x1, Pallas kernels: 134 us -> 178 us  [reduce_call(): pl.pallas_call(reduce_kernel, out_shape=[S((2, 256, 2048), bf), S((2, 256...]
    concatenate x3 -> x0, local copies, waits for them, and re-layouts: 8.18 us -> none  [the longest x2 5.23 us: tables(): hi = jnp.concatenate([zero, s, zero, zero] * 2, axis=1)]
    reduce_sum x3 -> x0, other arithmetic: 7.46 us -> none  [the longest x1 3.46 us: layer_norm(): spread = jnp.mean(centred * centred, axis=-1, keepdims=True)]
    another operation x2 -> x0, other arithmetic: 6.1 us -> none  [tables(): return jnp.stack([cos, lo, hi])]
    add x1 -> x0, other arithmetic: 5.7 us -> none  [own_local(): input_part + cotangent.astype(f4)]
where the time goes in v2:
time: 502 us; the launch traced here: 495 us
  Pallas kernels  368 us (73%)
  matrix products  104 us (21%)
  local copies, waits for them, and re-layouts  12.6 us (3%)
  other arithmetic  9.9 us (2%)
    pallas_call x1, Pallas kernels, reduce_call(): pl.pallas_call(reduce_kernel, out_shape=[S((2, 256, 2048), bf), S((2, 256...  178 us
    pallas_call x1, Pallas kernels, gather_call(): pl.pallas_call(gather_kernel, out_shape=[S((4, 2, 256, 2048), bf), S((4,...  154 us
    pallas_call x1, Pallas kernels, attention_call(): pl.pallas_call(attention_kernel, out_shape=[S((n, 128), bf), S((3, n, 128...  36.1 us
    dot_general x1, matrix products, own_local(): dots('tf,df->td', hidden_grad, wexp)  12.6 us
    dot_general x1, matrix products, own_local(): dots('te,ed->td', mixed, wout) + dots('tf,fd->td', activated, wcon)  11.4 us
    dot_general x1, matrix products, own_local(): dots('tf,fd->td', activated, wcon)  11.1 us
    dot_general x1, matrix products, own_local(): gcon = dots('tf,td->fd', activated, ct).astype(bf)  11.1 us
    dot_general x1, matrix products, own_local(): dots('kte,kde->td', pg, win) + dots('tf,df->td', hidden_grad, wexp)  10.3 us

profile of v2, /device:TPU:0, one launch (start us, length us, event | category | flops | bytes accessed | tf_op | source)
XLA Modules:
  0.0 495.4 jit_solution(11133652597304545199)
XLA Ops:
  0.6 0.0 copy-start
  0.7 0.7 copy-done
  1.3 0.6 select_reduce_fusion.inv
  2.0 0.1 pad.2.clone
  2.0 0.7 broadcast_in_dim.26
  2.7 0.7 broadcast_in_dim.27
  3.4 0.1 maximum_convert_fusion.gs
  3.4 1.2 copy-done.2
  4.7 1.2 copy-done.3
  5.9 1.1 copy-done.4
  7.0 0.9 copy-done.5
  8.0 153.7 %gather.1 = (bf16[4,2,256,2048]{3,2,1,0:T(8,128)(2,1)}, bf16[4,2,256,2048]{3,2,1,0:T(8,128)(2,1)}, bf16[3,4,2,256,128]{4,3,2,1,0:T(8,128)(2,1)S(1)}, bf16[128,20...) custom-call(bf16[2,256,2048]{2,1,0:T(8,128)(2,1)} %tok.3, ...), custom_call_target="tpu_custom_call" | custom-call | tf_op jit(solution)/shard_map/gather/pallas_call | solution.py:630
  161.6 0.0 copy-start.6
  161.6 0.0 copy-start.16
  161.6 6.7 %convolution_convert_fusion.4.do = bf16[2048,128]{1,0:T(8,128)(2,1)} fusion(bf16[2048,2048]{1,0:T(8,128)(2,1)} %bitcast.46, bf16[128,2048]{1,0:T(8,128)(2,1)S(1)} %get-tuple-element.27), kind=kOutput, calls=%fused_computation.21 | convolution fusion | flops 1074003968 | bytes 9437184 | tf_op jit(solution)/shard_map/td,ed->te/dot_general | solution.py:1108
  168.3 0.0 copy-done.6
  168.3 0.0 copy-done.16
  168.4 6.3 %convolution_bitcast_fusion.proj = f32[3,2048,128]{2,1,0:T(8,128)} fusion(bf16[2048,2048,1]{1,0,2:T(8,128)(2,1)S(1)} %bitcast.57, bf16[3,2048,128]{2,1,0:T(8,128)(2,1)S(1)} %bitcast.42), kind=kOutput, calls=%fused_computation.15 | convolution fusion | flops 3221225472 | bytes 13107200 | tf_op jit(solution)/shard_map/td,kde->kte/dot_general | solution.py:1107
  174.7 36.1 %attention.1 = (bf16[2048,128]{1,0:T(8,128)(2,1)}, bf16[3,2048,128]{2,1,0:T(8,128)(2,1)}) custom-call(s32[8]{0:T(128)} %select_reduce_fusion.inv, f32[3,2048,128]{2,1,0:T(8,128)} %convolution_bitcast_fusion.proj, bf16[2048,128]{1,0:T(8,128)(2,1)} %convolution_convert_fusion.4.do, f32[2,128,128]{2,1,0:T(8,128)} %constant.38.clone.within, ...), custom_call_target="tpu_custom_call" | custom-call | tf_op jit(solution)/shard_map/attention/pallas_call | solution.py:1085
  210.8 5.8 %convolution_convert_fusion.3.gout = bf16[128,2048]{1,0:T(8,128)(2,1)} fusion(bf16[2048,128]{1,0:T(8,128)(2,1)} %get-tuple-element.28, bf16[2048,2048]{1,0:T(8,128)(2,1)} %bitcast.47), kind=kOutput, calls=%fused_computation.20 | convolution fusion | flops 1074003968 | bytes 9437184 | tf_op jit(solution)/shard_map/te,td->ed/dot_general | solution.py:1116
  216.6 0.0 slice-done.2
  216.6 0.0 copy-done.10
  216.6 0.0 slice-done.3
  216.6 4.7 fusion.7
  221.3 2.6 copy.26
  223.8 7.7 %fusion.13 = f32[2048,512]{1,0:T(8,128)S(1)} fusion(bf16[2048,2048]{1,0:T(8,128)(2,1)} %bitcast.56, bf16[2048,512]{1,0:T(8,128)(2,1)} %bitcast.64), kind=kOutput, calls=%fused_computation.29 | convolution fusion | flops 4294967296 | bytes 14680064 | tf_op jit(solution)/shard_map/td,df->tf/dot_general | solution.py:1110
  231.5 0.0 copy-start.19
  231.5 0.0 slice-start.1
  231.6 0.0 copy-start.17
  231.6 0.0 slice-start.5
  231.6 11.1 %convolution_convert_fusion.gcon = bf16[512,2048]{1,0:T(8,128)(2,1)} fusion(bf16[2048,2048]{1,0:T(8,128)(2,1)} %bitcast.48, f32[2048,512]{1,0:T(8,128)S(1)} %fusion.13), kind=kOutput, calls=%fused_computation.16 | convolution fusion | flops 4305453056 | bytes 14680064 | tf_op jit(solution)/shard_map/tf,td->fd/dot_general | solution.py:1114
  242.6 0.0 slice-done
  242.6 0.0 slice-done.1
  242.6 0.0 copy-done.17
  242.7 6.6 %fusion.14 = f32[2048,512]{1,0:T(8,128)} fusion(bf16[2048,2048]{1,0:T(8,128)(2,1)S(1)} %bitcast.51, bf16[512,2048]{1,0:T(8,128)(2,1)S(1)} %copy-done.17), kind=kOutput, calls=%fused_computation.30 | convolution fusion | flops 4294967296 | bytes 14680064 | tf_op jit(solution)/shard_map/td,fd->tf/dot_general | solution.py:1115
  249.3 0.0 slice-done.4
  249.3 0.0 slice-done.5
  249.3 0.0 copy-start.18
  249.3 9.8 %convolution_convert_fusion.1 = bf16[2048,512]{1,0:T(8,128)(2,1)} fusion(bf16[2048,2048]{1,0:T(8,128)(2,1)S(1)} %bitcast.63, f32[2048,512]{1,0:T(8,128)S(1)} %fusion.13, f32[2048,512]{1,0:T(8,128)} %fusion.14), kind=kOutput, calls=%fused_computation.17 | convolution fusion | flops 4321181696 | bytes 18874368 | tf_op jit(solution)/shard_map/td,tf->df/dot_general | solution.py:1117
  259.1 0.0 copy-done.19
  259.1 0.0 copy-done.18
  259.1 12.6 %fusion.10 = f32[2048,2048]{1,0:T(8,128)} fusion(bf16[2048,512]{1,0:T(8,128)(2,1)S(1)} %bitcast.65, f32[2048,512]{1,0:T(8,128)S(1)} %fusion.13, f32[2048,512]{1,0:T(8,128)} %fusion.14), kind=kOutput, calls=%fused_computation.27 | convolution fusion | flops 4320133120 | bytes 27262976 | tf_op jit(solution)/shard_map/tf,df->td/dot_general | solution.py:1119
  271.7 0.0 copy-done.11
  271.7 10.3 %fusion = bf16[2048,2048]{1,0:T(8,128)(2,1)} fusion(f32[2048,2048]{1,0:T(8,128)} %fusion.10, bf16[3,2048,128]{2,1,0:T(8,128)(2,1)S(1)} %copy-done.11, bf16[3,2048,128]{2,1,0:T(8,128)(2,1)S(1)} %bitcast.43), kind=kOutput, calls=%fused_computation.1 | convolution fusion | flops 3229614080 | bytes 28311552 | tf_op jit(solution)/shard_map/kte,kde->td/dot_general | solution.py:1119
  282.0 11.1 %fusion.8 = f32[2048,2048]{1,0:T(8,128)} fusion(bf16[512,2048]{1,0:T(8,128)(2,1)S(1)} %copy-done.17, f32[2048,512]{1,0:T(8,128)} %copy-done.19), kind=kOutput, calls=%fused_computation.26 | convolution fusion | flops 4304404480 | bytes 23068672 | tf_op jit(solution)/shard_map/tf,fd->td/dot_general | solution.py:1113
  293.1 0.0 copy-done.8
  293.1 11.4 %add_convert_fusion = bf16[2048,2048]{1,0:T(8,128)(2,1)} fusion(f32[2048,2048]{1,0:T(8,128)} %fusion.8, bf16[2048,128]{1,0:T(8,128)(2,1)S(1)} %copy-done.8, bf16[128,2048]{1,0:T(8,128)(2,1)S(1)} %get-tuple-element.27), kind=kOutput, calls=%fused_computation.2 | convolution fusion | flops 1082130432 | bytes 26214400 | tf_op jit(solution)/shard_map/te,ed->td/dot_general | solution.py:1113
  304.5 177.9 %reduce.1 = (bf16[2,256,2048]{2,1,0:T(8,128)(2,1)}, f32[2,256,2048]{2,1,0:T(8,128)}, f32[8,256]{1,0:T(8,128)}, bf16[3,256,512]{2,1,0:T(8,128)(2,1)}, bf16[256,20...) custom-call(bf16[4,2,256,2048]{3,2,1,0:T(8,128)(2,1)} %bitcast.45, ...), custom_call_target="tpu_custom_call" | custom-call | tf_op jit(solution)/shard_map/reduce/pallas_call | solution.py:972
  482.3 0.0 copy-start.15
  482.4 0.0 copy-start.14
  482.4 0.0 copy-done.7
  482.4 0.0 copy-start.13
  482.4 4.0 add_convert_fusion.1
  486.4 1.4 fusion.12
  487.7 0.0 copy-done.15
  487.7 0.8 convert_element_type.69
  488.6 0.0 copy-done.14
  488.6 1.4 convert_element_type.68
  489.9 0.0 copy-done.13
  489.9 1.6 convert_element_type.70
  491.5 0.0 copy-done.12
  491.5 1.5 convert_element_type.71
  493.0 0.0 copy-done.9
  493.0 2.0 copy.31
  (21 shorter events, 0.0 us)
Async XLA Ops:
  0.6 0.7 copy-start
  3.4 1.2 copy-start.2
  4.7 1.2 copy-start.3
  5.9 1.1 copy-start.4
  7.0 0.9 copy-start.5
  161.6 6.7 %copy-start.6 = (f32[8,8,256]{2,1,0:T(8,128)}, f32[8,8,256]{2,1,0:T(8,128)S(1)}, u32[]{:S(2)}) copy-start(f32[8,8,256]{2,1,0:T(8,128)S(1)} %get-tuple-element.32.gains) | copy-start | bytes 196612
  161.6 6.7 %copy-start.16 = (bf16[4,2,256,2048]{3,2,1,0:T(8,128)(2,1)S(1)}, bf16[4,2,256,2048]{3,2,1,0:T(8,128)(2,1)}, u32[]{:S(2)}) copy-start(bf16[4,2,256,2048]{3,2,1,0:T(8,128)(2,1)} %get-tuple-element.25) | copy-start | bytes 25165828
  174.7 41.9 %slice-start.2 = ((s8[8388608]{0:T(1024)(128)(4,1)}), s8[4194304]{0:T(1024)(128)(4,1)S(1)}, s32[]{:S(2)}) async-start(s8[8388608]{0:T(1024)(128)(4,1)} %bitcast.58), calls=%async_computation.2 | async-start | bytes 8388608
  210.8 5.8 %copy-start.10 = (bf16[3,2048,128]{2,1,0:T(8,128)(2,1)S(1)}, bf16[3,2048,128]{2,1,0:T(8,128)(2,1)}, u32[]{:S(2)}) copy-start(bf16[3,2048,128]{2,1,0:T(8,128)(2,1)} %get-tuple-element.31) | copy-start | bytes 4718596
  210.8 5.8 %slice-start.3 = ((s8[8388608]{0:T(1024)(128)(4,1)}), s8[4194304]{0:T(1024)(128)(4,1)S(1)}, s32[]{:S(2)}) async-start(s8[8388608]{0:T(1024)(128)(4,1)} %bitcast.58), calls=%async_computation.3 | async-start | bytes 8388608
  223.8 18.8 %slice-start = ((s8[8388608]{0:T(1024)(128)(4,1)}), s8[4194304]{0:T(1024)(128)(4,1)S(1)}, s32[]{:S(2)}) async-start(s8[8388608]{0:T(1024)(128)(4,1)} %bitcast.49), calls=%async_computation | async-start | bytes 8388608
  223.8 25.4 %slice-start.4 = ((s8[8388608]{0:T(1024)(128)(4,1)}), s8[4194304]{0:T(1024)(128)(4,1)S(1)}, s32[]{:S(2)}) async-start(s8[8388608]{0:T(1024)(128)(4,1)} %bitcast.61), calls=%async_computation.4 | async-start | bytes 8388608
  231.5 27.5 %copy-start.19 = (f32[2048,512]{1,0:T(8,128)}, f32[2048,512]{1,0:T(8,128)S(1)}, u32[]{:S(2)}) copy-start(f32[2048,512]{1,0:T(8,128)S(1)} %fusion.13) | copy-start | bytes 12582916
  231.5 11.1 %slice-start.1 = ((s8[8388608]{0:T(1024)(128)(4,1)}), s8[4194304]{0:T(1024)(128)(4,1)S(1)}, s32[]{:S(2)}) async-start(s8[8388608]{0:T(1024)(128)(4,1)} %bitcast.49), calls=%async_computation.1 | async-start | bytes 8388608
  231.6 11.1 %copy-start.17 = (bf16[512,2048]{1,0:T(8,128)(2,1)S(1)}, bf16[512,2048]{1,0:T(8,128)(2,1)}, u32[]{:S(2)}) copy-start(bf16[512,2048]{1,0:T(8,128)(2,1)} %get-tuple-element.30) | copy-start | bytes 6291460
  231.6 17.7 %slice-start.5 = ((s8[8388608]{0:T(1024)(128)(4,1)}), s8[4194304]{0:T(1024)(128)(4,1)S(1)}, s32[]{:S(2)}) async-start(s8[8388608]{0:T(1024)(128)(4,1)} %bitcast.61), calls=%async_computation.5 | async-start | bytes 8388608
  249.3 9.8 %copy-start.18 = (bf16[4,2,256,512]{3,2,1,0:T(8,128)(2,1)S(1)}, bf16[4,2,256,512]{3,2,1,0:T(8,128)(2,1)}, u32[]{:S(2)}) copy-start(bf16[4,2,256,512]{3,2,1,0:T(8,128)(2,1)} %get-tuple-element.29) | copy-start | bytes 6291460
  259.1 12.6 %copy-start.11 = (bf16[3,2048,128]{2,1,0:T(8,128)(2,1)S(1)}, bf16[3,2048,128]{2,1,0:T(8,128)(2,1)}, u32[]{:S(2)}) copy-start(bf16[3,2048,128]{2,1,0:T(8,128)(2,1)} %get-tuple-element.31) | copy-start | bytes 4718596
  282.0 11.1 %copy-start.8 = (bf16[2048,128]{1,0:T(8,128)(2,1)S(1)}, bf16[2048,128]{1,0:T(8,128)(2,1)}, u32[]{:S(2)}) copy-start(bf16[2048,128]{1,0:T(8,128)(2,1)} %get-tuple-element.28) | copy-start | bytes 1572868
  304.5 177.9 %copy-start.7 = (bf16[2,256,2048]{2,1,0:T(8,128)(2,1)S(1)}, bf16[2,256,2048]{2,1,0:T(8,128)(2,1)}, u32[]{:S(2)}) copy-start(bf16[2,256,2048]{2,1,0:T(8,128)(2,1)} %tok.3) | copy-start | bytes 6291460
  482.3 5.4 %copy-start.15 = (bf16[512,256]{1,0:T(8,128)(2,1)S(1)}, bf16[512,256]{1,0:T(8,128)(2,1)}, u32[]{:S(2)}) copy-start(bf16[512,256]{1,0:T(8,128)(2,1)} %get-tuple-element.37) | copy-start | bytes 786436
  482.4 6.2 %copy-start.14 = (bf16[3,256,512]{2,1,0:T(8,128)(2,1)S(1)}, bf16[3,256,512]{2,1,0:T(8,128)(2,1)}, u32[]{:S(2)}) copy-start(bf16[3,256,512]{2,1,0:T(8,128)(2,1)} %get-tuple-element.36) | copy-start | bytes 2359300
  482.4 7.6 %copy-start.13 = (bf16[256,2048]{1,0:T(8,128)(2,1)S(1)}, bf16[256,2048]{1,0:T(8,128)(2,1)}, u32[]{:S(2)}) copy-start(bf16[256,2048]{1,0:T(8,128)(2,1)} %get-tuple-element.38) | copy-start | bytes 3145732
  486.4 5.1 %copy-start.12 = (bf16[2048,256]{1,0:T(8,128)(2,1)S(1)}, bf16[2048,256]{1,0:T(8,128)(2,1)}, u32[]{:S(2)}) copy-start(bf16[2048,256]{1,0:T(8,128)(2,1)} %get-tuple-element.39) | copy-start | bytes 3145732
  488.6 4.4 copy-start.9
  491.5 3.5 copy-start.1

commit v3 on v0

--- a/solution.py
+++ b/solution.py
@@ -1,6 +1,11 @@
+import itertools
+
 import jax
 import jax.numpy as jnp
+import numpy as np
 from jax import lax
+from jax.experimental import pallas as pl
+from jax.experimental.pallas import tpu as pltpu
 from jax.sharding import PartitionSpec as P
 
 HEAD_DIM = 64
@@ -172,7 +177,7 @@
     return lax.fori_loop(0, turn_count, full_one_turn, initial)
 
 
-def local(
+def general_local(
     tokens,
     pair_index,
     norm_gain,
@@ -309,6 +314,1014 @@
     )
 
 
+MESH = pl.DeviceIdType.MESH
+MB = 1 << 20
+EPS = 1e-05
+BF = jnp.bfloat16
+F4 = jnp.float32
+NT = (((1,), (1,)), ((), ()))
+FAR = (2, 3, 1, 0)
+
+
+def place():
+    c = lax.axis_index("ctx")
+    t = lax.axis_index("tp")
+    return c // 2, c % 2, t // 2, t % 2
+
+
+def device(z, x, y, k):
+    return (z * 2 + x, y * 2 + k)
+
+
+def remote(src, dst, send_sem, recv_sem, target):
+    return pltpu.make_async_remote_copy(
+        src_ref=src, dst_ref=dst, send_sem=send_sem, recv_sem=recv_sem,
+        device_id=target, device_id_type=MESH,
+    )
+
+
+def meet(peers):
+    barrier = pltpu.get_barrier_semaphore()
+    for peer in peers:
+        pl.semaphore_signal(barrier, inc=1, device_id=peer, device_id_type=MESH)
+    pl.semaphore_wait(barrier, len(peers))
+
+
+def peers_of(z, x, y, k):
+    c = z * 2 + x
+    others = [((c + i) % 8, lax.axis_index("tp")) for i in range(1, 8)]
+    return others, others + [device(z, x, 1 - y, k), device(z, x, y, 1 - k)]
+
+
+def columns(n, i):
+    return pl.ds(pl.multiple_of(n * i, n), n)
+
+
+def dot(a, b):
+    return jnp.dot(a, b, preferred_element_type=F4)
+
+
+def dot_t(a, b):
+    return lax.dot_general(a, b, NT, preferred_element_type=F4)
+
+
+def far_first(z, i):
+    return (3 * (1 - z // 2), z // 2 + 2 * (1 - z % 2), 1 + z % 2, z)[i]
+
+
+def add_into(dst, src):
+    lead, rows = dst.shape[:-2], dst.shape[-2]
+    for idx in itertools.product(*(range(n) for n in lead)):
+        @pl.loop(0, rows // 16)
+        def _(i):
+            at = idx + (pl.ds(pl.multiple_of(16 * i, 16), 16), slice(None))
+            dst[at] = (dst[at].astype(F4) + src[at].astype(F4)).astype(BF)
+
+
+class TokenGather:
+    def __init__(self, whole, sems):
+        self.whole = whole
+        self.xs, self.xr, self.zs, self.zr, self.ys, self.yr, self.cs, self.cr = sems
+        self.z, self.x, self.y, self.k = place()
+        self.q = 2 * self.y + self.k
+
+    def chunk(self, zz, s, q):
+        xx = self.x if s == 0 else 1 - self.x
+        return self.whole.at[zz, xx, pl.ds(64 * q, 64), :]
+
+    def send_x(self, src):
+        z, x, y, k = self.z, self.x, self.y, self.k
+        return remote(src, self.whole.at[z, x, pl.ds(64 * self.q, 64), :], self.xs, self.xr, device(z, 1 - x, y, k))
+
+    def send_up(self, zz, s, src):
+        return remote(src, self.chunk(zz, s, self.q), self.zs.at[zz, s, 0], self.zr.at[zz, s],
+                      device(jnp.minimum(self.z + 1, 3), self.x, self.y, self.k))
+
+    def send_down(self, zz, s, src):
+        return remote(src, self.chunk(zz, s, self.q), self.zs.at[zz, s, 1], self.zr.at[zz, s],
+                      device(jnp.maximum(self.z - 1, 0), self.x, self.y, self.k))
+
+    def send_y(self, zz, s):
+        c = self.chunk(zz, s, self.q)
+        return remote(c, c, self.ys.at[zz, s], self.yr.at[zz, s], device(self.z, self.x, 1 - self.y, self.k))
+
+    def send_core(self, zz, s, j):
+        yy = self.y if j == 0 else 1 - self.y
+        c = self.chunk(zz, s, 2 * yy + self.k)
+        return remote(c, c, self.cs.at[zz, s, j], self.cr.at[zz, s, j], device(self.z, self.x, self.y, 1 - self.k))
+
+    def both_ways(self, s, src):
+        z = self.z
+
+        @pl.when(z < 3)
+        def _():
+            self.send_up(z, s, src).start()
+
+        @pl.when(z > 0)
+        def _():
+            self.send_down(z, s, src).start()
+
+    def start(self, own_quarter, other_quarter):
+        self.send_x(other_quarter).start()
+        self.both_ways(0, own_quarter)
+
+    def after_x(self):
+        c = self.chunk(self.z, 1, self.q)
+        remote(c, c, self.xs, self.xr, device(self.z, 1 - self.x, self.y, self.k)).wait_recv()
+        self.both_ways(1, c)
+        self.send_y(self.z, 1).start()
+        self.send_core(self.z, 1, 0).start()
+
+    def hop(self, d, s):
+        z = self.z
+
+        @pl.when(z >= d)
+        def _():
+            zz = z - d
+            c = self.chunk(zz, s, self.q)
+            self.send_down(zz, s, c).wait_recv()
+
+            @pl.when(z < 3)
+            def _():
+                self.send_up(zz, s, c).start()
+
+            self.send_y(zz, s).start()
+            self.send_core(zz, s, 0).start()
+
+        @pl.when(z + d <= 3)
+        def _():
+            zz = z + d
+            c = self.chunk(zz, s, self.q)
+            self.send_up(zz, s, c).wait_recv()
+
+            @pl.when(z > 0)
+            def _():
+                self.send_down(zz, s, c).start()
+
+            self.send_y(zz, s).start()
+            self.send_core(zz, s, 0).start()
+
+    def y_in(self, zz, s):
+        c = self.chunk(zz, s, 2 * (1 - self.y) + self.k)
+        remote(c, c, self.ys.at[zz, s], self.yr.at[zz, s], device(self.z, self.x, 1 - self.y, self.k)).wait_recv()
+        self.send_core(zz, s, 1).start()
+
+    def y_hop(self, d, s):
+        z = self.z
+        if d == 0:
+            self.y_in(z, s)
+            return
+
+        @pl.when(z >= d)
+        def _():
+            self.y_in(z - d, s)
+
+        @pl.when(z + d <= 3)
+        def _():
+            self.y_in(z + d, s)
+
+    def landed(self, zz):
+        def rest(s):
+            for j in range(2):
+                yy = self.y if j == 0 else 1 - self.y
+                c = self.chunk(zz, s, 2 * yy + 1 - self.k)
+                remote(c, c, self.cs.at[zz, s, j], self.cr.at[zz, s, j], device(self.z, self.x, self.y, 1 - self.k)).wait_recv()
+
+        pl.when(self.z != zz)(lambda: rest(0))
+        rest(1)
+
+    def finish(self, other_quarter):
+        z = self.z
+        self.send_x(other_quarter).wait_send()
+        for zz in range(4):
+            for s in range(2):
+                def rest():
+                    self.send_y(zz, s).wait_send()
+                    for j in range(2):
+                        self.send_core(zz, s, j).wait_send()
+                if s == 0:
+                    pl.when(z != zz)(rest)
+                else:
+                    rest()
+                c = self.chunk(zz, s, self.q)
+
+                @pl.when((z < 3) & (zz <= z))
+                def _():
+                    self.send_up(zz, s, c).wait_send()
+
+                @pl.when((z > 0) & (zz >= z))
+                def _():
+                    self.send_down(zz, s, c).wait_send()
+
+
+def token_sems():
+    D = pltpu.SemaphoreType.DMA
+    return [D, D, D((4, 2, 2)), D((4, 2)), D((4, 2)), D((4, 2)), D((4, 2, 2)), D((4, 2, 2))]
+
+
+class WeightGather:
+    def __init__(self, pairs, sems):
+        self.pairs = pairs
+        self.zs, self.zr, self.xs, self.xr, self.loc = sems
+        self.z, self.x, self.y, self.k = place()
+
+    def z_send(self, d, w):
+        src, dst = self.pairs[w]
+        to = (self.z + d) % 4
+        return remote(src(to), dst(self.z, self.x), self.zs.at[d, w], self.zr.at[d, w], device(to, self.x, self.y, self.k))
+
+    def z_recv(self, d, w):
+        dst = self.pairs[w][1]
+        frm = (self.z - d + 4) % 4
+        return remote(dst(frm, self.x), dst(frm, self.x), self.zs.at[d, w], self.zr.at[d, w], device(frm, self.x, self.y, self.k))
+
+    def x_send(self, d, w):
+        src, dst = self.pairs[w]
+        frm = (self.z - d + 4) % 4
+        s = src(self.z) if d == 0 else dst(frm, self.x)
+        return remote(s, dst(frm, self.x), self.xs.at[d, w], self.xr.at[d, w], device(self.z, 1 - self.x, self.y, self.k))
+
+    def x_recv(self, d, w):
+        frm = (self.z - d + 4) % 4
+        r = self.pairs[w][1](frm, 1 - self.x)
+        return remote(r, r, self.xs.at[d, w], self.xr.at[d, w], device(self.z, 1 - self.x, self.y, self.k))
+
+    def local(self, w):
+        src, dst = self.pairs[w]
+        return pltpu.make_async_copy(src(self.z), dst(self.z, self.x), self.loc.at[w])
+
+    def start(self, *ws):
+        for w in ws:
+            for d in (2, 3, 1):
+                self.z_send(d, w).start()
+            self.x_send(0, w).start()
+            self.local(w).start()
+
+    def forward(self, w, d):
+        self.z_recv(d, w).wait_recv()
+        self.x_send(d, w).start()
+
+    def landed(self, w):
+        self.local(w).wait()
+        for d in range(4):
+            self.x_recv(d, w).wait_recv()
+
+    def finish(self, w):
+        for d in range(4):
+            if d:
+                self.z_send(d, w).wait_send()
+            self.x_send(d, w).wait_send()
+
+
+def weight_sems(n):
+    D = pltpu.SemaphoreType.DMA
+    return [D((4, n)), D((4, n)), D((4, n)), D((4, n)), D((n,))]
+
+
+class TokenReduce:
+    def __init__(self, out, bufs, sems):
+        self.out = out
+        self.A, self.S, self.r1, self.r2, self.rz, self.rf = bufs
+        (self.cs, self.cr, self.ys, self.yr, self.zs, self.zr, self.xs, self.xr,
+         self.fl, self.fys, self.fyr, self.fcs, self.fcr) = sems
+        self.z, self.x, self.y, self.k = place()
+        self.q = 2 * self.y + self.k
+
+    def core(self, i):
+        zz = far_first(self.z, i)
+        return remote(self.S.at[i % 2], self.r1.at[zz], self.cs.at[zz], self.cr.at[zz], device(self.z, self.x, self.y, 1 - self.k))
+
+    def yex(self, zz):
+        return remote(self.r1.at[zz, 1 - self.y], self.r2.at[zz], self.ys.at[zz], self.yr.at[zz],
+                      device(self.z, self.x, 1 - self.y, self.k))
+
+    def up(self, zz):
+        return remote(self.r1.at[zz, self.y], self.rz.at[zz], self.zs.at[zz], self.zr.at[zz],
+                      device(jnp.minimum(self.z + 1, 3), self.x, self.y, self.k))
+
+    def down(self, zz):
+        slot = jnp.where(zz == self.z - 1, 4, zz)
+        return remote(self.r1.at[zz, self.y], self.rz.at[slot], self.zs.at[zz], self.zr.at[slot],
+                      device(jnp.maximum(self.z - 1, 0), self.x, self.y, self.k))
+
+    def arrived(self, slot):
+        remote(self.rz.at[slot], self.rz.at[slot], self.zs.at[0], self.zr.at[slot],
+               device(self.z, self.x, self.y, 1 - self.k)).wait_recv()
+
+    def xex(self):
+        return remote(self.r1.at[self.z, self.y, 1 - self.x], self.rf, self.xs, self.xr,
+                      device(self.z, 1 - self.x, self.y, self.k))
+
+    def fill(self, i, lhs, rhs, free):
+        zz = far_first(self.z, i)
+        free()
+
+        def rows(kk):
+            return jnp.concatenate([lhs(zz, xx, 64 * (2 * yy + kk)) for yy in range(2) for xx in range(2)], axis=0)
+
+        for kk, dst in ((1 - self.k, self.S.at[i % 2]), (self.k, self.A.at[i % 2])):
+            a = rows(kk)
+
+            @pl.loop(0, 4)
+            def _(j):
+                at = columns(512, j)
+                dst[:, :, :, at] = rhs(a, at).astype(BF).reshape(2, 2, 64, 512)
+            if kk is not self.k:
+                self.core(i).start()
+
+    def after_core(self, i):
+        zz = far_first(self.z, i)
+        self.core(i).wait_recv()
+        add_into(self.r1.at[zz], self.A.at[i % 2])
+        self.yex(zz).start()
+
+    def after_y(self, i):
+        zz = far_first(self.z, i)
+        self.yex(zz).wait_recv()
+        add_into(self.r1.at[zz, self.y], self.r2.at[zz])
+
+    def line(self, i):
+        z = self.z
+        zz = far_first(z, i)
+        mine = self.r1.at[zz, self.y]
+        if i < 3:
+            @pl.when(zz > z)
+            def _():
+                @pl.when(z > 0)
+                def _():
+                    self.arrived(zz)
+                    add_into(mine, self.rz.at[zz])
+                self.up(zz).start()
+
+            @pl.when(zz < z)
+            def _():
+                @pl.when(z < 3)
+                def _():
+                    self.arrived(zz)
+                    add_into(mine, self.rz.at[zz])
+                self.down(zz).start()
+        else:
+            @pl.when(z > 0)
+            def _():
+                self.arrived(z)
+                add_into(mine, self.rz.at[z])
+
+            @pl.when(z < 3)
+            def _():
+                self.arrived(4)
+                add_into(mine, self.rz.at[4])
+            self.xex().start()
+
+    def spot(self, s, q):
+        return self.out.at[s, pl.ds(64 * q, 64), :]
+
+    def fin(self, s):
+        return (self.r1.at[self.z, self.y, self.x], self.x) if s == 0 else (self.rf, 1 - self.x)
+
+    def fin_copies(self, s):
+        src, seq = self.fin(s)
+        here = self.spot(seq, self.q)
+        return (pltpu.make_async_copy(src, here, self.fl.at[s]),
+                remote(src, here, self.fys.at[s], self.fyr.at[s], device(self.z, self.x, 1 - self.y, self.k)),
+                remote(src, here, self.fcs.at[s, 0], self.fcr.at[s, 0], device(self.z, self.x, self.y, 1 - self.k)))
+
+    def relay(self, s):
+        seq = self.x if s == 0 else 1 - self.x
+        r = self.spot(seq, 2 * (1 - self.y) + self.k)
+        return remote(r, r, self.fcs.at[s, 1], self.fcr.at[s, 1], device(self.z, self.x, self.y, 1 - self.k))
+
+    def spread(self, s):
+        if s == 1:
+            self.xex().wait_recv()
+        for cp in self.fin_copies(s):
+            cp.start()
+
+    def spread_y(self, s):
+        seq = self.x if s == 0 else 1 - self.x
+        r = self.spot(seq, 2 * (1 - self.y) + self.k)
+        remote(r, r, self.fys.at[s], self.fyr.at[s], device(self.z, self.x, 1 - self.y, self.k)).wait_recv()
+        self.relay(s).start()
+
+    def finish(self):
+        z = self.z
+        for zz in range(4):
+            self.yex(zz).wait_send()
+
+            @pl.when(z != zz)
+            def _():
+                self.up(zz).wait_send()
+        self.xex().wait_send()
+        for s in range(2):
+            seq = self.x if s == 0 else 1 - self.x
+            a, b, c = self.fin_copies(s)
+            a.wait()
+            b.wait_send()
+            c.wait_send()
+            self.relay(s).wait_send()
+            for j, yy in ((0, self.y), (1, 1 - self.y)):
+                r = self.spot(seq, 2 * yy + 1 - self.k)
+                remote(r, r, self.fcs.at[s, j], self.fcr.at[s, j], device(self.z, self.x, self.y, 1 - self.k)).wait_recv()
+
+
+def reduce_sems():
+    D = pltpu.SemaphoreType.DMA
+    return [D((4,)), D((4,)), D((4,)), D((4,)), D((4,)), D((5,)), D, D,
+            D((2,)), D((2,)), D((2,)), D((2, 2)), D((2, 2))]
+
+
+def reduce_bufs():
+    V = lambda *s: pltpu.VMEM(s, BF)
+    return [V(4, 2, 2, 64, 2048), V(4, 2, 64, 2048), V(5, 2, 64, 2048), V(64, 2048)]
+
+
+def ring_bufs():
+    return [pltpu.VMEM((2, 2, 2, 64, 2048), BF)] * 2
+
+
+class GradReduce:
+    def __init__(self, out, own, away, got, sems):
+        self.out, self.own, self.away, self.got = out, own, away, got
+        self.xs, self.xr, self.zs, self.zr = sems
+        self.z, self.x, self.y, self.k = place()
+
+    def x_send(self, d):
+        return remote(self.away.at[FAR.index(d) % 2], self.got.at[d], self.xs.at[d], self.xr.at[d], device(self.z, 1 - self.x, self.y, self.k))
+
+    def z_send(self, d):
+        here = self.out.at[self.z]
+        if d == 0:
+            return pltpu.make_async_copy(self.own.at[0], here, self.zs.at[0])
+        return remote(self.own.at[d], here, self.zs.at[d], self.zr.at[d], device((self.z + d) % 4, self.x, self.y, self.k))
+
+    def give(self, d, terms):
+        i = FAR.index(d)
+        if i >= 2:
+            self.x_send(FAR[i - 2]).wait_send()
+        self.away[i % 2] = terms.astype(BF)
+        self.x_send(d).start()
+
+    def keep(self, d, terms):
+        self.x_send(d).wait_recv()
+        self.own[d] = (terms + self.got[d].astype(F4)).astype(BF)
+        self.z_send(d).start()
+
+    def finish(self):
+        self.z_send(0).wait()
+        for d in FAR[2:]:
+            self.x_send(d).wait_send()
+        for d in range(4):
+            if d:
+                self.z_send(d).wait_send()
+                frm = (self.z - d + 4) % 4
+                r = self.out.at[frm]
+                remote(r, r, self.zs.at[d], self.zr.at[d], device(frm, self.x, self.y, self.k)).wait_recv()
+
+
+def grad_scratch(block):
+    D = pltpu.SemaphoreType.DMA
+    V = pltpu.VMEM
+    return [V((4,) + block, BF), V((2,) + block, BF), V((4,) + block, BF)] + [D((4,))] * 4
+
+
+def norm_rows(rows, gain, shift):
+    v = rows.astype(F4)
+    centred = v - jnp.mean(v, axis=-1, keepdims=True)
+    spread = jnp.mean(centred * centred, axis=-1, keepdims=True)
+    return (centred * lax.rsqrt(spread + EPS) * gain + shift).astype(BF)
+
+
+def turn(v, tab):
+    cos, lo, hi = tab
+    return v * cos + pltpu.roll(v, 112, 1) * lo + pltpu.roll(v, 16, 1) * hi
+
+
+def turn_back(v, tab):
+    cos, lo, hi = tab
+    return v * cos - pltpu.roll(v, 112, 1) * lo - pltpu.roll(v, 16, 1) * hi
+
+
+def angle_table(within, block, b):
+    cr, sr = within[0], within[1]
+    cb, sb = block[0, pl.ds(b, 1)], block[1, pl.ds(b, 1)]
+    cos, sin = cb * cr - sb * sr, sb * cr + cb * sr
+    entry = lax.broadcasted_iota(jnp.int32, cos.shape, 1) % 64
+    return cos, jnp.where(entry < 16, -sin, 0.0), jnp.where(entry < 16, 0.0, sin)
+
+
+def angles(rows, step):
+    frequency = (10000.0 ** (-2.0 * np.arange(16) / 32)).astype(np.float32).astype(np.float64)
+    lanes = np.concatenate([frequency, frequency, np.zeros(32)] * 2)
+    angle = step * np.arange(rows)[:, None] * lanes
+    return np.stack([np.cos(angle), np.sin(angle)]).astype(np.float32)
+
+
+def pick(index, parts):
+    chosen = parts(0)
+    for j in range(1, 8):
+        chosen = jnp.where(index == j, parts(j), chosen)
+    return chosen
+
+
+def one_head(v, h, axis):
+    entry = lax.broadcasted_iota(jnp.int32, v.shape, axis)
+    return jnp.where((entry < 64) == (h == 0), v, jnp.zeros_like(v))
+
+
+def masked(st, kr):
+    row = lax.broadcasted_iota(jnp.int32, (256, 256), 0)
+    column = lax.broadcasted_iota(jnp.int32, (256, 256), 1)
+    last = jnp.where(row <= column, st[kr - 256:], -1e30)
+    return last if kr == 256 else jnp.concatenate([st[:kr - 256], last], axis=0)
+
+
+def flip(v):
+    return v.astype(F4).T.astype(BF)
+
+
+def front_kernel(order, tok, gs, within, block, cot, win, wout, wexp, wcon,
+                 xn_out, ct_out, wx_out, wco, am_out, amt_out, dgelu_out, pg_out, gs_all,
+                 xn, ct, xo, wx, wo, proj, am, amt, dgelu, pg, qkv, qt, kt, vt, ot, logs, gt, gpos, dqt, dk, dv,
+                 osem, csem, gsem_s, gsem_r, *sems):
+    z, x, y, k = place()
+    c, q = z * 2 + x, 2 * y + k
+    nt = len(token_sems())
+    tx = TokenGather(xn, sems[:nt])
+    tc = TokenGather(ct, sems[nt:2 * nt])
+    pairs = [
+        (lambda zz, j=j: win.at[j, :, columns(128, zz)], lambda zz, xx, j=j: wx.at[zz, xx, :, pl.ds(512 + 128 * j, 128)])
+        for j in range(3)
+    ] + [
+        (lambda zz: wexp.at[:, columns(512, zz)], lambda zz, xx: wx.at[zz, xx, :, pl.ds(0, 512)]),
+        (lambda zz: wcon.at[columns(512, zz), :], lambda zz, xx: wco.at[pl.ds(0, 512), columns(256, zz * 2 + xx)]),
+        (lambda zz: wout.at[columns(128, zz), :], lambda zz, xx: wo.at[:, columns(256, zz * 2 + xx)]),
+    ]
+    wg = WeightGather(pairs, sems[2 * nt:])
+    others, everyone = peers_of(z, x, y, k)
+    meet(everyone)
+    gcopies = [remote(gs, gs_all.at[c], gsem_s.at[i], gsem_r.at[i], others[i]) for i in range(7)]
+    for g in gcopies:
+        g.start()
+    gs_all[c] = gs[...]
+    wg.start(0, 1, 2)
+    own_slot = pltpu.make_async_copy(cot.at[x], ct.at[z, x], csem)
+    own_slot.start()
+    for i in range(7):
+        frm = gs_all.at[(c - i - 1 + 8) % 8]
+        remote(frm, frm, gsem_s.at[i], gsem_r.at[i], others[i]).wait_recv()
+    gain = jnp.concatenate([gs_all[i, 0:1, :] for i in range(8)], axis=1)
+    shift = jnp.concatenate([gs_all[i, 1:2, :] for i in range(8)], axis=1)
+
+    @pl.loop(0, 2)
+    def _(i):
+        xo[pl.ds(32 * i, 32)] = norm_rows(tok[1 - x, pl.ds(64 * q + 32 * i, 32)], gain, shift)
+
+    @pl.loop(0, 8)
+    def _(i):
+        xn[z, x, pl.ds(32 * i, 32)] = norm_rows(tok[x, pl.ds(32 * i, 32)], gain, shift)
+
+    cot_other = cot.at[1 - x, pl.ds(64 * q, 64)]
+    tx.start(tx.chunk(z, 0, q), xo)
+    tx.after_x()
+    tc.start(cot.at[x, pl.ds(64 * q, 64)], cot_other)
+    wg.start(5, 3)
+
+    def project(i):
+        zz = far_first(z, 3 - i)
+        tx.landed(zz)
+
+        @pl.loop(0, 2)
+        def _(xx):
+            row = pl.multiple_of(512 * zz + 256 * xx, 256)
+            proj[pl.ds(row, 256)] = dot(xn[zz, xx], wx[:, :, :, pl.ds(512, 384)].reshape(2048, 384))
+
+    tx.hop(1, 0)
+    tx.hop(1, 1)
+    for w in range(3):
+        for d in (1, 2, 3):
+            wg.forward(w, d)
+    tx.y_hop(0, 1)
+    tx.hop(2, 0)
+    tx.hop(2, 1)
+    tc.after_x()
+    for s in range(2):
+        tx.y_hop(1, s)
+    for s in range(2):
+        tx.hop(3, s)
+    for s in range(2):
+        tx.y_hop(2, s)
+    wg.start(4)
+    for s in range(2):
+        tc.hop(1, s)
+    for s in range(2):
+        tx.y_hop(3, s)
+    tc.y_hop(0, 1)
+    for d in (1, 2, 3):
+        wg.forward(5, d)
+    for w in range(3):
+        wg.landed(w)
+    project(0)
+    project(1)
+    for s in range(2):
+        tc.hop(2, s)
+    for s in range(2):
+        tc.y_hop(1, s)
+    project(2)
+    project(3)
+    out_xn = pltpu.make_async_copy(xn, xn_out, osem.at[0])
+    out_xn.start()
+    for s in range(2):
+        tc.hop(3, s)
+    for s in range(2):
+        tc.y_hop(2, s)
+
+    @pl.loop(0, 16)
+    def _(b):
+        half = b // 8
+        pair = b + half * (15 - 2 * b)
+        here = pl.ds(pl.multiple_of(b * 128, 128), 128)
+        t = angle_table(within, block, b)
+        three = pick(order[0, pair], lambda j: proj[pl.ds(pl.multiple_of(256 * j + 128 * half, 128), 128)])
+        rq = turn(three[:, 0:128], t).astype(BF) * BF(0.125)
+        rk = turn(three[:, 128:256], t).astype(BF)
+        rv = three[:, 256:384].astype(BF)
+        qkv[0, here], qkv[1, here], qkv[2, here] = rq, rk, rv
+        qt[:, here], kt[:, here], vt[:, here] = flip(rq), flip(rk), flip(rv)
+
+    for i in range(8):
+        kr, here = 256 * (i + 1), pl.ds(256 * i, 256)
+        for h in range(2):
+            st = masked(dot(qkv[1, :kr], one_head(qt[:, here], h, 0)), kr)
+            peak = jnp.max(st, axis=0, keepdims=True)
+            p = jnp.exp(st - peak)
+            total = jnp.sum(p, axis=0, keepdims=True)
+            o = dot(vt[:, :kr], p.astype(BF)) * (1.0 / total)
+            ot[pl.ds(64 * h, 64), here] = o[64 * h:64 * h + 64]
+            logs[pl.ds(h, 1), here] = peak + jnp.log(total)
+        if i in (3, 5, 6):
+            wg.forward(3, {3: 1, 5: 2, 6: 3}[i])
+    for s in range(2):
+        tc.y_hop(3, s)
+
+    @pl.loop(0, 16)
+    def _(b):
+        here = pl.ds(pl.multiple_of(b * 128, 128), 128)
+        gpos[here] = ot[:, here].T
+
+    def by_rows(c2, half):
+        p = order[1, c2]
+        return lambda ref: pick(p, lambda j: ref[pl.ds(128 * (j if half == 0 else 15 - j), 128)])
+
+    for half in range(2):
+        @pl.loop(0, 8)
+        def _(c2):
+            row = pl.ds(pl.multiple_of(256 * c2 + 128 * half, 128), 128)
+            am[row, pl.ds(512, 128)] = by_rows(c2, half)(gpos).astype(BF)
+
+    own_slot.wait()
+    wg.landed(5)
+
+    @pl.loop(0, 4)
+    def _(zz):
+        tc.landed(zz)
+        for xx in range(2):
+            row = pl.multiple_of(512 * zz + 256 * xx, 256)
+            proj[pl.ds(row, 256), pl.ds(0, 128)] = dot_t(ct[zz, xx], wo[...])
+
+    out_ct = pltpu.make_async_copy(ct, ct_out, osem.at[1])
+    out_ct.start()
+
+    @pl.loop(0, 16)
+    def _(b):
+        half = b // 8
+        pair = b + half * (15 - 2 * b)
+        here = pl.ds(pl.multiple_of(b * 128, 128), 128)
+        g = pick(order[0, pair], lambda j: proj[pl.ds(pl.multiple_of(256 * j + 128 * half, 128), 128), pl.ds(0, 128)])
+        gpos[here] = g
+        gt[:, here] = flip(g)
+
+    dk[...] = jnp.zeros_like(dk)
+    dv[...] = jnp.zeros_like(dv)
+    for i in range(8):
+        kr, here = 256 * (i + 1), pl.ds(256 * i, 256)
+        for h in range(2):
+            gT = gt[:, here]
+            st = masked(dot(qkv[1, :kr], one_head(qt[:, here], h, 0)), kr)
+            p = jnp.exp(st - logs[pl.ds(h, 1), here])
+            low = p.astype(BF)
+            at = pl.ds(64 * h, 64)
+            delta = jnp.sum(ot[at, here] * gt[at, here].astype(F4), axis=0, keepdims=True)
+            ds = (p * (dot(qkv[2, :kr], one_head(gT, h, 0)) - delta)).astype(BF)
+            dv[:kr] += dot(low, one_head(gpos[here].astype(BF), h, 1))
+            dk[:kr] += dot(ds, one_head(qkv[0, here], h, 1))
+            dqt[at, here] = dot(kt[:, :kr], ds)[64 * h:64 * h + 64] * 0.125
+        if i in (3, 5, 6):
+            wg.forward(4, {3: 1, 5: 2, 6: 3}[i])
+
+    @pl.loop(0, 16)
+    def _(b):
+        here = pl.ds(pl.multiple_of(b * 128, 128), 128)
+        t = angle_table(within, block, b)
+        gpos[here] = turn_back(dqt[:, here].T, t)
+        dk[here] = turn_back(dk[here], t)
+
+    for half in range(2):
+        @pl.loop(0, 8)
+        def _(c2):
+            row = pl.ds(pl.multiple_of(256 * c2 + 128 * half, 128), 128)
+            for j, ref in enumerate((gpos, dk, dv)):
+                pg[row, pl.ds(128 * j, 128)] = by_rows(c2, half)(ref).astype(BF)
+
+    outs = [pltpu.make_async_copy(pg, pg_out, osem.at[2])]
+    outs[0].start()
+    wg.landed(3)
+    outs.append(pltpu.make_async_copy(wx, wx_out, osem.at[3]))
+    outs[1].start()
+    outs.append(pltpu.make_async_copy(wo, wco.at[pl.ds(512, 128)], osem.at[4]))
+    outs[2].start()
+
+    @pl.loop(0, 8)
+    def _(i):
+        at = pl.ds(pl.multiple_of(256 * i, 256), 256)
+        u = dot(xn[i // 2, i % 2], wx[:, :, :, pl.ds(0, 512)].reshape(2048, 512))
+        square = u * u
+        t = jnp.tanh(0.7978845608028654 * (u + 0.044715 * u * square))
+        half = 0.5 * (1.0 + t)
+        am[at, pl.ds(0, 512)] = (u * half).astype(BF)
+        dgelu[at] = half + 0.5 * u * (1.0 - t * t) * (0.7978845608028654 * (1.0 + 3 * 0.044715 * square))
+        amt[:, at] = flip(am[at])
+
+    for j, (src, dst) in enumerate(((am, am_out), (amt, amt_out), (dgelu, dgelu_out))):
+        outs.append(pltpu.make_async_copy(src, dst, osem.at[5 + j]))
+        outs[-1].start()
+    wg.landed(4)
+    tx.finish(xo)
+    tc.finish(cot_other)
+    for w in range(6):
+        wg.finish(w)
+    for g in gcopies:
+        g.wait_send()
+    for o in [out_xn, out_ct] + outs:
+        o.wait()
+
+
+def front_call(order, tokens, gs, cot, win, wout, wexp, wcon):
+    S = jax.ShapeDtypeStruct
+    ANY = pl.BlockSpec(memory_space=pl.ANY)
+    VM = pl.BlockSpec(memory_space=pltpu.VMEM)
+    D = pltpu.SemaphoreType.DMA
+    V = pltpu.VMEM
+    rows = (4, 2, 256, 2048)
+    return pl.pallas_call(
+        front_kernel,
+        out_shape=[S(rows, BF), S(rows, BF), S((4, 2, 256, 896), BF), S((640, 2048), BF), S((2048, 640), BF), S((640, 2048), BF),
+                   S((2048, 512), F4), S((2048, 384), BF), S((8, 8, 256), F4)],
+        in_specs=[pl.BlockSpec(memory_space=pltpu.SMEM)] + [VM] * 4 + [ANY] * 5,
+        out_specs=[ANY] * 8 + [VM],
+        scratch_shapes=[V(rows, BF), V(rows, BF), V((64, 2048), BF), V((4, 2, 256, 896), BF), V((128, 2048), BF), V((2048, 384), F4),
+                        V((2048, 640), BF), V((640, 2048), BF), V((2048, 512), F4), V((2048, 384), BF),
+                        V((3, 2048, 128), BF), V((128, 2048), BF), V((128, 2048), BF), V((128, 2048), BF),
+                        V((128, 2048), F4), V((8, 2048), F4), V((128, 2048), BF), V((2048, 128), F4), V((128, 2048), F4),
+                        V((2048, 128), F4), V((2048, 128), F4), D((8,)), D, D((7,)), D((7,))]
+        + token_sems() * 2 + weight_sems(6),
+        compiler_params=pltpu.CompilerParams(collective_id=0, has_side_effects=True, vmem_limit_bytes=60 * MB),
+        name="front",
+    )(order, tokens, gs, jnp.asarray(angles(128, 1)), jnp.asarray(angles(16, 128)), cot, win, wout, wexp, wcon)
+
+
+def norm_backward(tok, cot, ng, gains, out, stage, ssem, sums):
+    gain = jnp.concatenate([gains[i, 0:1, :] for i in range(8)], axis=1)
+    sums[...] = jnp.zeros_like(sums)
+
+    def store(i):
+        return pltpu.make_async_copy(stage.at[i % 2], out.at[i // 8, pl.ds(pl.multiple_of(32 * (i % 8), 32), 32)], ssem.at[i % 2])
+
+    @pl.loop(0, 16)
+    def _(i):
+        s, at = i // 8, pl.ds(pl.multiple_of(32 * (i % 8), 32), 32)
+        v = tok[s, at].astype(F4)
+        centred = v - jnp.mean(v, axis=-1, keepdims=True)
+        scale = lax.rsqrt(jnp.mean(centred * centred, axis=-1, keepdims=True) + EPS)
+        xhat = centred * scale
+        n = ng[s, at].astype(F4)
+        g = n * gain
+        along = jnp.mean(g * xhat, axis=-1, keepdims=True)
+
+        @pl.when(i >= 2)
+        def _():
+            store(i - 2).wait()
+        stage[i % 2] = cot[s, at].astype(F4) + (g - jnp.mean(g, axis=-1, keepdims=True) - xhat * along) * scale
+        store(i).start()
+        both = n * xhat
+        sums[0] += both[:8] + both[8:16] + both[16:24] + both[24:]
+        sums[1] += n[:8] + n[8:16] + n[16:24] + n[24:]
+
+    store(14).wait()
+    store(15).wait()
+
+
+def back_kernel(am, amt, wco, wx, gains, ct, xn, dgelu, pg, tok, cot,
+                out, ig, vectors, o1, o2,
+                hp, ctr, col, dg, ng, stage, sums, vec, vecs, psem, rsem, csem, dsem, tsem, ssem, vs, vr, *rest):
+    z, x, y, k = place()
+    c = z * 2 + x
+    rest = list(rest)
+    take = lambda n: [rest.pop(0) for _ in range(n)]
+    ring = take(2)
+    nb, ns = len(reduce_bufs()), len(reduce_sems())
+    tn = TokenReduce(ng, ring + take(nb), take(ns))
+    to = TokenReduce(out, ring + take(nb), take(ns))
+    g1 = GradReduce(o1, *take(3), take(4))
+    g2 = GradReduce(o2, *take(3), take(4))
+    others, everyone = peers_of(z, x, y, k)
+    load_pg = pltpu.make_async_copy(pg, hp.at[:, pl.ds(512, 384)], psem)
+    load_pg.start()
+
+    def chunk_loads(i):
+        zz = far_first(z, i)
+        return (pltpu.make_async_copy(ct.at[zz], ctr.at[i % 2], rsem.at[i % 2]),
+                pltpu.make_async_copy(dgelu.at[pl.ds(pl.multiple_of(512 * zz, 512), 512)], dg.at[i % 2], dsem.at[i % 2]))
+
+    blocks = [(src, d, xx) for xx in (1 - x, x) for src in (ct, xn) for d in FAR]
+
+    def block_load(n):
+        src, d, xx = blocks[n]
+        return pltpu.make_async_copy(src.at[:, :, :, columns(256, 2 * ((z + d) % 4) + xx)], col.at[n % 3], csem.at[n % 3])
+
+    for i in range(2):
+        for cp in chunk_loads(i):
+            cp.start()
+    for n in range(3):
+        block_load(n).start()
+    meet(everyone)
+
+    def pull(i):
+        zz = far_first(z, i)
+        for cp in chunk_loads(i):
+            cp.wait()
+        for xx in range(2):
+            row = pl.multiple_of(512 * zz + 256 * xx, 256)
+            g = dot_t(ctr[i % 2, xx], wco[pl.ds(0, 512)])
+            hp[pl.ds(row, 256), pl.ds(0, 512)] = (g * dg[i % 2, pl.ds(256 * xx, 256)]).astype(BF)
+        if i < 2:
+            for cp in chunk_loads(i + 2):
+                cp.start()
+
+    def fill_n(i):
+        tn.fill(i, lambda zz, xx, r: hp[pl.ds(pl.multiple_of(512 * zz + 256 * xx + r, 64), 64)], lambda a, at: dot_t(a, wx[at]),
+                lambda: tn.core(i - 2).wait_send() if i >= 2 else None)
+
+    def fill_o(i):
+        to.fill(i, lambda zz, xx, r: am[pl.ds(pl.multiple_of(512 * zz + 256 * xx + r, 64), 64)], lambda a, at: dot(a, wco[:, at]),
+                lambda: (to.core(i - 2) if i >= 2 else tn.core(i + 2)).wait_send())
+
+    def grad(n):
+        block_load(n).wait()
+        v = col[n % 3].reshape(2048, 256)
+        terms = dot(amt[...], v) if n // 4 % 2 == 0 else dot(flip(v), hp[...])
+        g = (g1, g2)[n // 4 % 2]
+        (g.give if n < 8 else g.keep)(blocks[n][1], terms)
+        if n + 3 < 16:
+            block_load(n + 3).start()
+
+    pull(0)
+    load_pg.wait()
+    fill_n(0)
+    pull(1)
+    fill_n(1)
+    tn.after_core(0)
+    pull(2)
+    fill_n(2)
+    tn.after_core(1)
+    pull(3)
+    fill_n(3)
+    tn.after_core(2)
+    grad(0)
+    tn.after_core(3)
+    tn.after_y(0)
+    tn.line(0)
+    fill_o(0)
+    grad(1)
+    fill_o(1)
+    tn.after_y(1)
+    tn.line(1)
+    to.after_core(0)
+    grad(2)
+    grad(3)
+    fill_o(2)
+    to.after_core(1)
+    grad(4)
+    tn.after_y(2)
+    tn.line(2)
+    grad(5)
+    fill_o(3)
+    to.after_core(2)
+    grad(6)
+    grad(7)
+    to.after_core(3)
+    grad(8)
+    tn.after_y(3)
+    tn.line(3)
+    loads = [pltpu.make_async_copy(tok, ctr.at[0], tsem.at[0]), pltpu.make_async_copy(cot, ctr.at[1], tsem.at[1])]
+    for cp in loads:
+        cp.start()
+    grad(9)
+    grad(10)
+    grad(11)
+    to.after_y(0)
+    to.line(0)
+    tn.spread(0)
+    tn.spread(1)
+    grad(12)
+    grad(13)
+    tn.spread_y(0)
+    tn.spread_y(1)
+    to.after_y(1)
+    to.line(1)
+    grad(14)
+    grad(15)
+    tn.finish()
+    for cp in loads:
+        cp.wait()
+    to.after_y(2)
+    to.line(2)
+    norm_backward(ctr.at[0], ctr.at[1], ng, gains, ig, stage, ssem, sums)
+    for i in range(8):
+        at = slice(256 * i, 256 * i + 256)
+        for j in range(2):
+            vec[i, j:j + 1, :] = jnp.sum(sums[j, :, at], axis=0, keepdims=True)
+        vec[i, 2:8, :] = jnp.zeros((6, 256), F4)
+    vecs[c] = vec[c]
+    copies = [remote(vec.at[(c + i + 1) % 8], vecs.at[c], vs.at[i], vr.at[i], others[i]) for i in range(7)]
+    for cp in copies:
+        cp.start()
+    to.after_y(3)
+    to.line(3)
+    to.spread(0)
+    to.spread(1)
+    to.spread_y(0)
+    to.spread_y(1)
+    for i in range(7):
+        frm = vecs.at[(c - i - 1 + 8) % 8]
+        remote(frm, frm, vs.at[i], vr.at[i], others[i]).wait_recv()
+    total = vecs[0]
+    for i in range(1, 8):
+        total = total + vecs[i]
+    vectors[...] = total
+    to.core(2).wait_send()
+    to.core(3).wait_send()
+    to.finish()
+    g1.finish()
+    g2.finish()
+    for cp in copies:
+        cp.wait_send()
+
+
+def back_call(am, amt, wco, wx, gains, ct, xn, dgelu, pg, tok, cot):
+    S = jax.ShapeDtypeStruct
+    ANY = pl.BlockSpec(memory_space=pl.ANY)
+    VM = pl.BlockSpec(memory_space=pltpu.VMEM)
+    D = pltpu.SemaphoreType.DMA
+    V = pltpu.VMEM
+    b1, b2 = (640, 256), (256, 896)
+    return pl.pallas_call(
+        back_kernel,
+        out_shape=[S((2, 256, 2048), BF), S((2, 256, 2048), F4), S((8, 256), F4), S((4,) + b1, BF), S((4,) + b2, BF)],
+        in_specs=[VM] * 5 + [ANY] * 6,
+        out_specs=[ANY, ANY, VM, ANY, ANY],
+        scratch_shapes=[V((2048, 896), BF), V((2, 2, 256, 2048), BF), V((3, 4, 2, 256, 256), BF), V((2, 512, 512), F4),
+                        V((2, 256, 2048), BF), V((2, 32, 2048), F4), V((2, 8, 2048), F4), V((8, 8, 256), F4), V((8, 8, 256), F4),
+                        D, D((2,)), D((3,)), D((2,)), D((2,)), D((2,)), D((7,)), D((7,))]
+        + ring_bufs() + (reduce_bufs() + reduce_sems()) * 2 + grad_scratch(b1) + grad_scratch(b2),
+        compiler_params=pltpu.CompilerParams(collective_id=1, has_side_effects=True, vmem_limit_bytes=62 * MB),
+        name="back",
+    )(am, amt, wco, wx.reshape(2048, 896), gains, ct, xn, dgelu, pg, tok, cot)
+
+
+def own_local(tokens, pair_index, norm_gain, norm_shift, w_attention_in, w_attention_out, w_expand, w_contract, cotangent):
+    x = lax.axis_index("ctx") % 2
+    pairs = lax.dynamic_index_in_dim(pair_index, x, 0, False)
+    which = jnp.arange(8, dtype=jnp.int32)
+    inverse = jnp.sum(jnp.where(pairs[None, :] == which[:, None], which[None, :], 0), axis=1).astype(jnp.int32)
+    gs = jnp.concatenate([norm_gain[None], norm_shift[None], jnp.zeros((6, 256), BF)], axis=0).astype(F4)
+    xn, ct, wx, wco, am, amt, dgelu, pg, gains = front_call(
+        jnp.stack([inverse, pairs]), tokens, gs, cotangent, w_attention_in, w_attention_out, w_expand, w_contract)
+    out_sum, input_grad, vectors, o1, o2 = back_call(am, amt, wco, wx, gains, ct, xn, dgelu, pg, tokens, cotangent)
+    output = (tokens.astype(F4) + out_sum.astype(F4)).astype(BF)
+    gcon = o1[:, :512].reshape(2048, 256).astype(F4)
+    gout = o1[:, 512:].reshape(512, 256).astype(F4)
+    gexp = o2[:, :, :512].transpose(1, 0, 2).reshape(256, 2048).astype(F4)
+    gin = o2[:, :, 512:].reshape(4, 256, 3, 128).transpose(2, 1, 0, 3).reshape(3, 256, 512).astype(F4)
+    return (output, input_grad, vectors[0], vectors[1], gin, gout, gexp, gcon)
+
+
+def local(tokens, pair_index, norm_gain, norm_shift, w_attention_in, w_attention_out, w_expand, w_contract, cotangent):
+    args = (tokens, pair_index, norm_gain, norm_shift, w_attention_in, w_attention_out, w_expand, w_contract, cotangent)
+    sizes = (lax.axis_size("ctx"), lax.axis_size("tp")) + tokens.shape + w_attention_in.shape[2:] + w_expand.shape[1:]
+    if sizes == (8, 4, 2, 256, 2048, 512, 2048):
+        return own_local(*args)
+    return general_local(*args)
+
+
 def solution(mesh):
     in_specs = (
         P(None, "ctx", None),

time: 1350 us -> 408 us (0.30)
  the two profiles are of different devices: /device:TPU:0 before, /device:TPU:9 now
where the time goes in v3:
time: 408 us; the launch traced here: 404 us
  Pallas kernels  377 us (92%)
  local copies, waits for them, and re-layouts  15.1 us (4%)
  other arithmetic  11 us (3%)
    pallas_call x1, Pallas kernels, back_call(): pl.pallas_call(back_kernel, out_shape=[S((2, 256, 2048), BF), S((2, 256,...  194 us
    pallas_call x1, Pallas kernels, front_call(): pl.pallas_call(front_kernel, out_shape=[S(rows, BF), S(rows, BF), S((4, 2...  183 us
    unnamed x9, local copies, waits for them, and re-layouts  9.88 us

profile of v3, /device:TPU:9, one launch (start us, length us, event | category | flops | bytes accessed | tf_op | source)
XLA Modules:
  0.0 403.8 jit_solution(17639110517763332254)
XLA Ops:
  0.6 0.0 copy-start
  0.7 0.7 copy-done
  1.3 0.1 select_reduce_fusion
  1.4 0.6 pad_add_fusion.order
  2.0 0.1 pad.2.clone
  2.1 0.7 broadcast_in_dim.26
  2.8 0.7 broadcast_in_dim.27
  3.4 0.7 maximum_convert_fusion.gs
  4.1 182.9 %front.1 = (bf16[4,2,256,2048]{3,2,1,0:T(8,128)(2,1)}, bf16[4,2,256,2048]{3,2,1,0:T(8,128)(2,1)}, bf16[4,2,256,896]{3,2,1,0:T(8,128)(2,1)}, bf16[640,2048]{1,0:T...) custom-call(s32[2,8]{1,0:T(2,128)} %pad_add_fusion.order, ...), custom_call_target="tpu_custom_call" | custom-call | tf_op jit(solution)/shard_map/front/pallas_call | solution.py:1074
  187.0 193.7 %back.1 = (bf16[2,256,2048]{2,1,0:T(8,128)(2,1)}, f32[2,256,2048]{2,1,0:T(8,128)}, f32[8,256]{1,0:T(8,128)}, bf16[4,640,256]{2,1,0:T(8,128)(2,1)}, bf16[4,256,896]{2,1,0:T(8,128)(2,1)}) custom-call(bf16[2048,640]{1,0:T(8,128)(2,1)} %get-tuple-element.22.am, bf16[640,2048]{1,0:T(8,128)(2,1)} %get-tuple-element.23.amt, ...), custom_call_target="tpu_custom_call" | custom-call | tf_op jit(solution)/shard_map/back/pallas_call | solution.py:1286
  380.6 0.0 copy-start.2
  380.7 4.5 %add_convert_fusion = bf16[2,256,2048]{2,1,0:T(8,128)(2,1)} fusion(bf16[2,256,2048]{2,1,0:T(8,128)(2,1)} %get-tuple-element.31, bf16[2,256,2048]{2,1,0:T(8,128)(2,1)} %tok.3), kind=kLoop, calls=%fused_computation | loop fusion | flops 4194304 | bytes 6291456 | tf_op jit(solution)/shard_map/convert_element_type | solution.py:1309
  385.2 1.3 fusion
  386.5 0.0 copy-done.2
  386.6 0.1 slice.23
  386.6 0.8 bitcast_convert_fusion.1
  387.5 1.5 bitcast_convert_fusion
  389.0 1.2 slice_convert_fusion
  390.3 0.5 copy.28
  390.8 0.1 copy.29
  390.9 1.6 copy.31
  392.5 1.5 convert_bitcast_fusion
  394.0 1.8 copy.30
  395.8 2.9 copy.32
  398.7 0.0 copy-start.1
  398.7 4.7 %copy.34 = f32[2,256,2048]{2,1,0:T(8,128)} copy(f32[2,256,2048]{2,1,0:T(8,128)} %get-tuple-element.71) | data formatting | bytes 8388608
  403.4 0.0 copy-done.1
  (4 shorter events, 0.0 us)
Async XLA Ops:
  0.6 0.7 copy-start
  380.6 5.9 %copy-start.2 = (bf16[4,640,256]{2,1,0:T(8,128)(2,1)S(1)}, bf16[4,640,256]{2,1,0:T(8,128)(2,1)}, u32[]{:S(2)}) copy-start(bf16[4,640,256]{2,1,0:T(8,128)(2,1)} %get-tuple-element.35) | copy-start | bytes 3932164
  398.7 4.7 %copy-start.1 = (s32[2,8]{1,0:T(2,128)S(1)}, s32[2,8]{1,0:T(2,128)}, u32[]{:S(2)}) copy-start(s32[2,8]{1,0:T(2,128)} %param.12) | copy-start | bytes 196

commit v4 on v0

--- a/solution.py
+++ b/solution.py
@@ -1,6 +1,12 @@
+import functools
+import itertools
+
 import jax
 import jax.numpy as jnp
+import numpy as np
 from jax import lax
+from jax.experimental import pallas as pl
+from jax.experimental.pallas import tpu as pltpu
 from jax.sharding import PartitionSpec as P
 
 HEAD_DIM = 64
@@ -172,7 +178,7 @@
     return lax.fori_loop(0, turn_count, full_one_turn, initial)
 
 
-def local(
+def general_local(
     tokens,
     pair_index,
     norm_gain,
@@ -309,6 +315,977 @@
     )
 
 
+MESH = pl.DeviceIdType.MESH
+MB = 1 << 20
+EPS = 1e-05
+BF = jnp.bfloat16
+F4 = jnp.float32
+NT = (((1,), (1,)), ((), ()))
+FAR = (1, 2, 3, 0)
+
+
+def place():
+    c = lax.axis_index("ctx")
+    t = lax.axis_index("tp")
+    return c // 2, c % 2, t // 2, t % 2
+
+
+def device(z, x, y, k):
+    return (z * 2 + x, y * 2 + k)
+
+
+def remote(src, dst, send_sem, recv_sem, target):
+    return pltpu.make_async_remote_copy(
+        src_ref=src, dst_ref=dst, send_sem=send_sem, recv_sem=recv_sem,
+        device_id=target, device_id_type=MESH,
+    )
+
+
+def meet(peers):
+    barrier = pltpu.get_barrier_semaphore()
+    for peer in peers:
+        pl.semaphore_signal(barrier, inc=1, device_id=peer, device_id_type=MESH)
+    pl.semaphore_wait(barrier, len(peers))
+
+
+def peers_of(z, x, y, k):
+    c = z * 2 + x
+    others = [((c + i) % 8, lax.axis_index("tp")) for i in range(1, 8)]
+    return others, others + [device(z, x, 1 - y, k), device(z, x, y, 1 - k)]
+
+
+def columns(n, i):
+    return pl.ds(pl.multiple_of(n * i, n), n)
+
+
+def dot(a, b):
+    return jnp.dot(a, b, preferred_element_type=F4)
+
+
+def dot_t(a, b):
+    return lax.dot_general(a, b, NT, preferred_element_type=F4)
+
+
+def mirrored(z, e):
+    return jnp.where(z < 2, 4 - e, e) if e in (1, 3) else e
+
+
+def far_first(z, i):
+    return (3 * (1 - z // 2), z // 2 + 2 * (1 - z % 2), 1 + z % 2, z)[i]
+
+
+def add_into(dst, src):
+    lead, rows = dst.shape[:-2], dst.shape[-2]
+    for idx in itertools.product(*(range(n) for n in lead)):
+        @pl.loop(0, rows // 16)
+        def _(i):
+            at = idx + (pl.ds(pl.multiple_of(16 * i, 16), 16), slice(None))
+            dst[at] = (dst[at].astype(F4) + src[at].astype(F4)).astype(BF)
+
+
+class TokenGather:
+    def __init__(self, whole, sems):
+        self.whole = whole
+        self.xs, self.xr, self.zs, self.zr, self.ys, self.yr, self.cs, self.cr = sems
+        self.z, self.x, self.y, self.k = place()
+        self.q = 2 * self.y + self.k
+
+    def chunk(self, zz, s, q):
+        xx = self.x if s == 0 else 1 - self.x
+        return self.whole.at[zz, xx, pl.ds(64 * q, 64), :]
+
+    def send_x(self, src):
+        z, x, y, k = self.z, self.x, self.y, self.k
+        return remote(src, self.whole.at[z, x, pl.ds(64 * self.q, 64), :], self.xs, self.xr, device(z, 1 - x, y, k))
+
+    def send_up(self, zz, s, src):
+        return remote(src, self.chunk(zz, s, self.q), self.zs.at[zz, s, 0], self.zr.at[zz, s],
+                      device(jnp.minimum(self.z + 1, 3), self.x, self.y, self.k))
+
+    def send_down(self, zz, s, src):
+        return remote(src, self.chunk(zz, s, self.q), self.zs.at[zz, s, 1], self.zr.at[zz, s],
+                      device(jnp.maximum(self.z - 1, 0), self.x, self.y, self.k))
+
+    def send_y(self, zz, s):
+        c = self.chunk(zz, s, self.q)
+        return remote(c, c, self.ys.at[zz, s], self.yr.at[zz, s], device(self.z, self.x, 1 - self.y, self.k))
+
+    def send_core(self, zz, s, j):
+        yy = self.y if j == 0 else 1 - self.y
+        c = self.chunk(zz, s, 2 * yy + self.k)
+        return remote(c, c, self.cs.at[zz, s, j], self.cr.at[zz, s, j], device(self.z, self.x, self.y, 1 - self.k))
+
+    def both_ways(self, s, src):
+        z = self.z
+
+        @pl.when(z < 3)
+        def _():
+            self.send_up(z, s, src).start()
+
+        @pl.when(z > 0)
+        def _():
+            self.send_down(z, s, src).start()
+
+    def start(self, own_quarter, other_quarter):
+        self.send_x(other_quarter).start()
+        self.both_ways(0, own_quarter)
+
+    def after_x(self):
+        c = self.chunk(self.z, 1, self.q)
+        remote(c, c, self.xs, self.xr, device(self.z, 1 - self.x, self.y, self.k)).wait_recv()
+        self.both_ways(1, c)
+        self.send_y(self.z, 1).start()
+        self.send_core(self.z, 1, 0).start()
+
+    def hop(self, d, s):
+        z = self.z
+
+        @pl.when(z >= d)
+        def _():
+            zz = z - d
+            c = self.chunk(zz, s, self.q)
+            self.send_down(zz, s, c).wait_recv()
+
+            @pl.when(z < 3)
+            def _():
+                self.send_up(zz, s, c).start()
+
+            self.send_y(zz, s).start()
+            self.send_core(zz, s, 0).start()
+
+        @pl.when(z + d <= 3)
+        def _():
+            zz = z + d
+            c = self.chunk(zz, s, self.q)
+            self.send_up(zz, s, c).wait_recv()
+
+            @pl.when(z > 0)
+            def _():
+                self.send_down(zz, s, c).start()
+
+            self.send_y(zz, s).start()
+            self.send_core(zz, s, 0).start()
+
+    def y_in(self, zz, s):
+        c = self.chunk(zz, s, 2 * (1 - self.y) + self.k)
+        remote(c, c, self.ys.at[zz, s], self.yr.at[zz, s], device(self.z, self.x, 1 - self.y, self.k)).wait_recv()
+        self.send_core(zz, s, 1).start()
+
+    def y_hop(self, d):
+        z = self.z
+        if d == 0:
+            self.y_in(z, 1)
+            return
+        for s in range(2):
+            pl.when(z >= d)(lambda: self.y_in(z - d, s))
+            pl.when(z + d <= 3)(lambda: self.y_in(z + d, s))
+
+    def landed(self, zz):
+        def rest(s):
+            for j in range(2):
+                yy = self.y if j == 0 else 1 - self.y
+                c = self.chunk(zz, s, 2 * yy + 1 - self.k)
+                remote(c, c, self.cs.at[zz, s, j], self.cr.at[zz, s, j], device(self.z, self.x, self.y, 1 - self.k)).wait_recv()
+
+        pl.when(self.z != zz)(lambda: rest(0))
+        rest(1)
+
+    def sent_own(self, own_quarter, other_quarter):
+        z = self.z
+        self.send_x(other_quarter).wait_send()
+        pl.when(z < 3)(lambda: self.send_up(z, 0, own_quarter).wait_send())
+        pl.when(z > 0)(lambda: self.send_down(z, 0, own_quarter).wait_send())
+
+    def finish(self):
+        z = self.z
+        for zz in range(4):
+            for s in range(2):
+                def rest():
+                    self.send_y(zz, s).wait_send()
+                    for j in range(2):
+                        self.send_core(zz, s, j).wait_send()
+                if s == 0:
+                    pl.when(z != zz)(rest)
+                else:
+                    rest()
+                c = self.chunk(zz, s, self.q)
+
+                pl.when((z < 3) & (zz < z + s))(lambda: self.send_up(zz, s, c).wait_send())
+                pl.when((z > 0) & (zz > z - s))(lambda: self.send_down(zz, s, c).wait_send())
+
+
+def token_sems():
+    D = pltpu.SemaphoreType.DMA
+    return [D, D, D((4, 2, 2)), D((4, 2)), D((4, 2)), D((4, 2)), D((4, 2, 2)), D((4, 2, 2))]
+
+
+class WeightGather:
+    def __init__(self, pairs, sems):
+        self.pairs = pairs
+        self.zs, self.zr, self.xs, self.xr, self.loc = sems
+        self.z, self.x, self.y, self.k = place()
+
+    def z_send(self, d, w):
+        src, dst = self.pairs[w]
+        to = (self.z + d) % 4
+        return remote(src(to), dst(self.z, self.x), self.zs.at[d, w], self.zr.at[d, w], device(to, self.x, self.y, self.k))
+
+    def z_recv(self, d, w):
+        dst = self.pairs[w][1]
+        frm = (self.z - d + 4) % 4
+        return remote(dst(frm, self.x), dst(frm, self.x), self.zs.at[d, w], self.zr.at[d, w], device(frm, self.x, self.y, self.k))
+
+    def x_send(self, d, w):
+        src, dst = self.pairs[w]
+        frm = (self.z - d + 4) % 4
+        s = src(self.z) if isinstance(d, int) and d == 0 else dst(frm, self.x)
+        return remote(s, dst(frm, self.x), self.xs.at[d, w], self.xr.at[d, w], device(self.z, 1 - self.x, self.y, self.k))
+
+    def x_recv(self, d, w):
+        frm = (self.z - d + 4) % 4
+        r = self.pairs[w][1](frm, 1 - self.x)
+        return remote(r, r, self.xs.at[d, w], self.xr.at[d, w], device(self.z, 1 - self.x, self.y, self.k))
+
+    def local(self, w):
+        src, dst = self.pairs[w]
+        return pltpu.make_async_copy(src(self.z), dst(self.z, self.x), self.loc.at[w])
+
+    def send(self, ws, e):
+        d = mirrored(self.z, e)
+        for w in ws:
+            if e:
+                self.z_send(d, w).start()
+            else:
+                self.x_send(0, w).start()
+                self.local(w).start()
+
+    def forward(self, ws, e):
+        d = mirrored(self.z, e)
+        for w in ws:
+            self.z_recv(d, w).wait_recv()
+            self.x_send(d, w).start()
+
+    def landed(self, w):
+        self.local(w).wait()
+        for d in range(4):
+            self.x_recv(d, w).wait_recv()
+
+    def finish(self, w):
+        for d in range(4):
+            if d:
+                self.z_send(d, w).wait_send()
+            self.x_send(d, w).wait_send()
+
+
+def weight_sems(n):
+    D = pltpu.SemaphoreType.DMA
+    return [D((4, n)), D((4, n)), D((4, n)), D((4, n)), D((n,))]
+
+
+class TokenReduce:
+    def __init__(self, out, bufs, sems):
+        self.out = out
+        self.S, self.r1, self.r2, self.rz, self.rf = bufs
+        (self.cs, self.cr, self.ys, self.yr, self.zs, self.zr, self.xs, self.xr,
+         self.fl, self.fys, self.fyr, self.fcs, self.fcr) = sems
+        self.z, self.x, self.y, self.k = place()
+        self.q = 2 * self.y + self.k
+
+    def slot(self, s):
+        return self.x if s == 0 else 1 - self.x
+
+    def core(self, i, slot=0):
+        zz = far_first(self.z, i)
+        return remote(self.S.at[slot], self.r1.at[zz], self.cs.at[zz], self.cr.at[zz], device(self.z, self.x, self.y, 1 - self.k))
+
+    def yex(self, zz, s):
+        xx = self.slot(s)
+        return remote(self.r1.at[zz, 1 - self.y, xx], self.r2.at[zz, xx], self.ys.at[zz, s], self.yr.at[zz, s],
+                      device(self.z, self.x, 1 - self.y, self.k))
+
+    def mine(self, zz, s):
+        return self.r1.at[zz, self.y, self.slot(s)]
+
+    def up(self, zz, s):
+        return remote(self.mine(zz, s), self.rz.at[zz, s], self.zs.at[zz, s], self.zr.at[zz, s],
+                      device(jnp.minimum(self.z + 1, 3), self.x, self.y, self.k))
+
+    def down(self, zz, s):
+        slot = jnp.where(zz == self.z - 1, 4, zz)
+        return remote(self.mine(zz, s), self.rz.at[slot, s], self.zs.at[zz, s], self.zr.at[slot, s],
+                      device(jnp.maximum(self.z - 1, 0), self.x, self.y, self.k))
+
+    def arrive(self, zz, s, slot):
+        r = self.rz.at[slot, s]
+        remote(r, r, self.zs.at[0, s], self.zr.at[slot, s], device(self.z, self.x, self.y, 1 - self.k)).wait_recv()
+        add_into(self.mine(zz, s), r)
+
+    def xex(self):
+        return remote(self.mine(self.z, 1), self.rf, self.xs, self.xr, device(self.z, 1 - self.x, self.y, self.k))
+
+    def rows(self, i, kk, lhs):
+        zz = far_first(self.z, i)
+        return jnp.concatenate([lhs(zz, xx, 64 * (2 * yy + kk)) for yy in range(2) for xx in range(2)], axis=0)
+
+    def fill(self, i, slot, lhs, rhs):
+        a = self.rows(i, 1 - self.k, lhs)
+
+        @pl.loop(0, 4)
+        def _(j):
+            at = columns(512, j)
+            self.S[slot, :, :, :, at] = rhs(a, j).astype(BF).reshape(2, 2, 64, 512)
+        self.core(i, slot).start()
+
+    def after_core(self, i, lhs, rhs):
+        zz = far_first(self.z, i)
+        a = self.rows(i, self.k, lhs)
+        self.core(i).wait_recv()
+
+        @pl.loop(0, 4)
+        def _(j):
+            at = columns(512, j)
+            got = self.r1[zz, :, :, :, at].reshape(256, 512).astype(F4)
+            self.r1[zz, :, :, :, at] = (rhs(a, j) + got).astype(BF).reshape(2, 2, 64, 512)
+        for s in (1, 0):
+            self.yex(zz, s).start()
+
+    def line(self, i, s):
+        z = self.z
+        zz = far_first(z, i)
+        self.yex(zz, s).wait_recv()
+        add_into(self.mine(zz, s), self.r2.at[zz, self.slot(s)])
+        if i < 3:
+            @pl.when(zz > z)
+            def _():
+                pl.when(z > 0)(lambda: self.arrive(zz, s, zz))
+                self.up(zz, s).start()
+
+            @pl.when(zz < z)
+            def _():
+                pl.when(z < 3)(lambda: self.arrive(zz, s, zz))
+                self.down(zz, s).start()
+        else:
+            pl.when(z > 0)(lambda: self.arrive(z, s, z))
+            pl.when(z < 3)(lambda: self.arrive(z, s, 4))
+            if s == 1:
+                self.xex().start()
+
+    def spot(self, s, q):
+        return self.out.at[self.slot(s), pl.ds(64 * q, 64), :]
+
+    def fin_copies(self, s):
+        src = self.mine(self.z, 0) if s == 0 else self.rf
+        here = self.spot(s, self.q)
+        return (pltpu.make_async_copy(src, here, self.fl.at[s]),
+                remote(src, here, self.fys.at[s], self.fyr.at[s], device(self.z, self.x, 1 - self.y, self.k)),
+                remote(src, here, self.fcs.at[s, 0], self.fcr.at[s, 0], device(self.z, self.x, self.y, 1 - self.k)))
+
+    def relay(self, s):
+        r = self.spot(s, 2 * (1 - self.y) + self.k)
+        return remote(r, r, self.fcs.at[s, 1], self.fcr.at[s, 1], device(self.z, self.x, self.y, 1 - self.k))
+
+    def spread(self, s, base=None):
+        if s == 1:
+            self.xex().wait_recv()
+        if base is not None:
+            add_into(self.mine(self.z, 0) if s == 0 else self.rf, base(self.slot(s), pl.ds(64 * self.q, 64)))
+        for cp in self.fin_copies(s):
+            cp.start()
+
+    def spread_y(self, s):
+        r = self.spot(s, 2 * (1 - self.y) + self.k)
+        remote(r, r, self.fys.at[s], self.fyr.at[s], device(self.z, self.x, 1 - self.y, self.k)).wait_recv()
+        self.relay(s).start()
+
+    def finish(self):
+        z = self.z
+        for zz in range(4):
+            for s in range(2):
+                self.yex(zz, s).wait_send()
+                pl.when(z != zz)(lambda: self.up(zz, s).wait_send())
+        self.xex().wait_send()
+        for s in range(2):
+            a, b, c = self.fin_copies(s)
+            a.wait()
+            b.wait_send()
+            c.wait_send()
+            self.relay(s).wait_send()
+            for j, yy in ((0, self.y), (1, 1 - self.y)):
+                r = self.spot(s, 2 * yy + 1 - self.k)
+                remote(r, r, self.fcs.at[s, j], self.fcr.at[s, j], device(self.z, self.x, self.y, 1 - self.k)).wait_recv()
+
+
+def reduce_sems():
+    D = pltpu.SemaphoreType.DMA
+    return [D((4,)), D((4,)), D((4, 2)), D((4, 2)), D((4, 2)), D((5, 2)), D, D,
+            D((2,)), D((2,)), D((2,)), D((2, 2)), D((2, 2))]
+
+
+def reduce_bufs():
+    V = lambda *s: pltpu.VMEM(s, BF)
+    return [V(4, 2, 2, 64, 2048), V(4, 2, 64, 2048), V(5, 2, 64, 2048), V(64, 2048)]
+
+
+class GradReduce:
+    def __init__(self, parts, away, got, sems):
+        self.parts, self.away, self.got = parts, away, got
+        self.xs, self.xr, self.zs, self.zr = sems
+        self.z, self.x, self.y, self.k = place()
+
+    def x_send(self, e):
+        i = FAR.index(e)
+        return remote(self.away.at[i % 2], self.got.at[i], self.xs.at[i], self.xr.at[i], device(self.z, 1 - self.x, self.y, self.k))
+
+    def z_sends(self, e):
+        d = mirrored(self.z, e)
+        for i, (part, there) in enumerate(self.parts):
+            src, dst = self.got.at[(FAR.index(e),) + part], there(self.z)
+            if e == 0:
+                yield pltpu.make_async_copy(src, dst, self.zs.at[0, i])
+            else:
+                yield remote(src, dst, self.zs.at[d, i], self.zr.at[d, i], device((self.z + d) % 4, self.x, self.y, self.k))
+
+    def give(self, e, terms):
+        i = FAR.index(e)
+        if i >= 2:
+            self.x_send(FAR[i - 2]).wait_send()
+        self.away[i % 2] = terms.astype(BF)
+        self.x_send(e).start()
+
+    def keep(self, e, terms):
+        i = FAR.index(e)
+        self.x_send(e).wait_recv()
+        self.got[i] = (terms + self.got[i].astype(F4)).astype(BF)
+        for cp in self.z_sends(e):
+            cp.start()
+
+    def finish(self):
+        for cp in self.z_sends(0):
+            cp.wait()
+        for e in FAR[2:]:
+            self.x_send(e).wait_send()
+        for d in range(1, 4):
+            frm = (self.z - d + 4) % 4
+            for cp in self.z_sends(d):
+                cp.wait_send()
+            for i, (part, there) in enumerate(self.parts):
+                r = there(frm)
+                remote(r, r, self.zs.at[d, i], self.zr.at[d, i], device(frm, self.x, self.y, self.k)).wait_recv()
+
+
+def grad_scratch(block, parts):
+    D = pltpu.SemaphoreType.DMA
+    V = pltpu.VMEM
+    return [V((2,) + block, BF), V((4,) + block, BF)] + [D((4,))] * 2 + [D((4, parts))] * 2
+
+
+def norm_rows(rows, gain, shift):
+    v = rows.astype(F4)
+    centred = v - jnp.mean(v, axis=-1, keepdims=True)
+    spread = jnp.mean(centred * centred, axis=-1, keepdims=True)
+    return (centred * lax.rsqrt(spread + EPS) * gain + shift).astype(BF)
+
+
+def turn(v, tab):
+    cos, lo, hi = tab
+    return v * cos + pltpu.roll(v, 112, 1) * lo + pltpu.roll(v, 16, 1) * hi
+
+
+def turn_back(v, tab):
+    cos, lo, hi = tab
+    return v * cos - pltpu.roll(v, 112, 1) * lo - pltpu.roll(v, 16, 1) * hi
+
+
+def angle_table(within, cb, sb):
+    cr, sr = within[0], within[1]
+    cos, sin = cb * cr - sb * sr, sb * cr + cb * sr
+    entry = lax.broadcasted_iota(jnp.int32, cos.shape, 1) % 64
+    return cos, jnp.where(entry < 16, -sin, 0.0), jnp.where(entry < 16, 0.0, sin)
+
+
+def angles(rows, step):
+    frequency = (10000.0 ** (-2.0 * np.arange(16) / 32)).astype(np.float32).astype(np.float64)
+    lanes = np.concatenate([frequency, frequency, np.zeros(32)] * 2)
+    angle = step * np.arange(rows)[:, None] * lanes
+    return np.stack([np.cos(angle), np.sin(angle)]).astype(np.float32)
+
+
+def pick(index, parts):
+    chosen = parts(0)
+    for j in range(1, 8):
+        chosen = jnp.where(index == j, parts(j), chosen)
+    return chosen
+
+
+def one_head(v, h, axis):
+    entry = lax.broadcasted_iota(jnp.int32, v.shape, axis)
+    return jnp.where((entry < 64) == (h == 0), v, jnp.zeros_like(v))
+
+
+def masked(st, kr):
+    row = lax.broadcasted_iota(jnp.int32, (256, 256), 0)
+    column = lax.broadcasted_iota(jnp.int32, (256, 256), 1)
+    last = jnp.where(row <= column, st[kr - 256:], -1e30)
+    return last if kr == 256 else jnp.concatenate([st[:kr - 256], last], axis=0)
+
+
+def flip(v):
+    return v.astype(F4).T.astype(BF)
+
+
+def norm_backward(tok, cot, ng, gains, out, stage, ssem, sums):
+    gain = jnp.concatenate([gains[i, 0:1, :] for i in range(8)], axis=1)
+    sums[...] = jnp.zeros_like(sums)
+
+    def store(i):
+        return pltpu.make_async_copy(stage.at[i % 2], out.at[i // 8, pl.ds(pl.multiple_of(32 * (i % 8), 32), 32)], ssem.at[i % 2])
+
+    @pl.loop(0, 16)
+    def _(i):
+        s, at = i // 8, pl.ds(pl.multiple_of(32 * (i % 8), 32), 32)
+        v = tok[s, at].astype(F4)
+        centred = v - jnp.mean(v, axis=-1, keepdims=True)
+        scale = lax.rsqrt(jnp.mean(centred * centred, axis=-1, keepdims=True) + EPS)
+        xhat = centred * scale
+        n = ng[s, at].astype(F4)
+        g = n * gain
+        along = jnp.mean(g * xhat, axis=-1, keepdims=True)
+
+        @pl.when(i >= 2)
+        def _():
+            store(i - 2).wait()
+        stage[i % 2] = cot[s, at].astype(F4) + (g - jnp.mean(g, axis=-1, keepdims=True) - xhat * along) * scale
+        store(i).start()
+        both = n * xhat
+        sums[0] += both[:8] + both[8:16] + both[16:24] + both[24:]
+        sums[1] += n[:8] + n[8:16] + n[16:24] + n[24:]
+
+    store(14).wait()
+    store(15).wait()
+
+
+ORDER = (
+    "start", "WB1", "WB2", "ln", "sx", "WB3", "WB0", "hx10", "FB3", "ax", "WA1", "hx20", "WA0", "FB1", "hx11", "WC0", "WA2", "WA3",
+    "hx21", "FA1", "WC3", "yx0", "WC1", "FA2", "yx1", "sc", "hx31", "yx2", "FA3", "hx30", "ac", "FB2", "yx3", "WC2", "hc10", "lwin",
+    "P0", "FC1", "P1", "P2", "P3", "FC3", "rope", "hc11", "f0", "f1", "f2", "lwexp", "hid0", "hid1", "hc20", "hid2", "f3", "yc0", "FC2",
+    "yc1", "f4", "hc21", "f5", "f6", "f7", "hc30", "lwout", "lwcon", "mix", "fillo0", "fillo1", "fillo2", "yc2", "hc31", "hid3",
+    "coreo0", "mg0", "coreo1", "yc3", "mg1", "fillo3", "mg2", "coreo2", "mg3", "gflip", "b0", "b1", "lo01", "coreo3", "b2", "b3", "b4",
+    "lo00", "b5", "b6", "lo11", "b7", "pg", "lo10", "g01", "lo21", "pull0", "lo20", "g02", "filln0", "pull1", "g03", "pull2", "k01",
+    "g00", "coren0", "filln1", "lo30", "filln2", "k02", "pull3", "g11", "coren1", "ln01", "g12", "g13", "k03", "g10", "coren2", "ln00",
+    "ln11", "ln21", "lo31", "filln3", "spo0", "ln10", "k12", "coren3", "ln20", "ln31", "k11", "k00", "ln30", "spn0", "spn1", "syn1",
+    "syn0", "syo0", "spo1", "k13", "finn", "norm", "k10", "syo1", "fino", "gf",
+)
+
+
+def block_kernel(order, gs, within, block, tok, cot, win, wout, wexp, wcon,
+                 out, ig, vectors, gin, gout, gexp, gcon, xn, ct,
+                 wx, wco, hp, am, S, ctr, ng, gs_all, vec, vecs,
+                 gsem_s, gsem_r, lsem, rsem, csem, ssem, vs, vr, *rest):
+    z, x, y, k = place()
+    c, q = z * 2 + x, 2 * y + k
+    rest = list(rest)
+    take = lambda n: [rest.pop(0) for _ in range(n)]
+    nt, nb, ns = len(token_sems()), len(reduce_bufs()), len(reduce_sems())
+    tx = TokenGather(xn, take(nt))
+    tc = TokenGather(ct, take(nt))
+    pairs = [
+        (lambda zz, j=j: win.at[j, :, columns(128, zz)], lambda zz, xx, j=j: wx.at[zz, xx, :, pl.ds(512 + 128 * j, 128)])
+        for j in range(3)
+    ] + [
+        (lambda zz: wexp.at[:, columns(512, zz)], lambda zz, xx: wx.at[zz, xx, :, pl.ds(0, 512)]),
+        (lambda zz: wcon.at[columns(512, zz), :], lambda zz, xx: wco.at[pl.ds(0, 512), columns(256, zz * 2 + xx)]),
+        (lambda zz: wout.at[columns(128, zz), :], lambda zz, xx: wco.at[pl.ds(512, 128), columns(256, zz * 2 + xx)]),
+    ]
+    wg = WeightGather(pairs, take(len(weight_sems(6))))
+    tn = TokenReduce(ng, [S] + take(nb), take(ns))
+    to = TokenReduce(out, [S] + take(nb), take(ns))
+    whole = slice(None)
+    g1 = GradReduce([((pl.ds(0, 512), whole), lambda zz: gcon.at[columns(512, zz), :]),
+                     ((pl.ds(512, 128), whole), lambda zz: gout.at[columns(128, zz), :])], *take(2), take(4))
+    g2 = GradReduce([((whole, pl.ds(0, 512)), lambda zz: gexp.at[:, columns(512, zz)])]
+                    + [((whole, pl.ds(512 + 128 * j, 128)), lambda zz, j=j: gin.at[j, :, columns(128, zz)]) for j in range(3)],
+                    *take(2), take(4))
+    others, everyone = peers_of(z, x, y, k)
+
+    V = pltpu.VMEM
+    steps = {}
+    flags = set()
+    U = {"A": (0, 1, 2, 5), "B": (3,), "C": (4,)}
+    load_tok = lambda: pltpu.make_async_copy(tok, ctr.at[0], lsem.at[0])
+    load_cot = lambda: pltpu.make_async_copy(cot, ctr.at[1], lsem.at[1])
+    own_cot = lambda: pltpu.make_async_copy(cot.at[x], ct.at[z, x], lsem.at[2])
+    xl, xo = ctr.at[1, 0], ctr.at[1, 1, pl.ds(0, 64)]
+    own_xn = lambda: pltpu.make_async_copy(xl, xn.at[z, x], lsem.at[3])
+    gcopies = lambda: [remote(gs, gs_all.at[c], gsem_s.at[i], gsem_r.at[i], others[i]) for i in range(7)]
+    mine, cot_mine = xl.at[pl.ds(64 * q, 64)], cot.at[x, pl.ds(64 * q, 64)]
+    cot_other = cot.at[1 - x, pl.ds(64 * q, 64)]
+
+    def once(name, act):
+        if name not in flags:
+            flags.add(name)
+            act()
+
+    users = [n for n in ORDER if n[:-1] in ("P", "mg", "hid", "pull")]
+
+    def rows_in(n, xx):
+        name = users[n]
+        i = int(name[-1])
+        zz = far_first(z, i if name[:-1] in ("hid", "pull") else 3 - i)
+        src = xn if name[:-1] in ("P", "hid") else ct
+        return zz, pltpu.make_async_copy(src.at[zz, xx], ctr.at[n % 2, xx], rsem.at[n % 2, xx])
+
+    def begin_rows(n):
+        flags.add(n)
+        for xx in range(2):
+            rows_in(n, xx)[1].start()
+
+    def each_half(name, act):
+        n = users.index(name)
+        if n not in flags:
+            begin_rows(n)
+        for xx in range(2):
+            zz, cp = rows_in(n, xx)
+            cp.wait()
+            act(zz, xx, ctr.at[n % 2, xx], pl.multiple_of(512 * zz + 256 * xx, 256))
+        flags.add(name)
+        for m in (n + 1, n + 2):
+            if m < len(users) and m not in flags and {"hid": "P3", "pull": "mg3"}.get(users[m][:-1]) in flags:
+                begin_rows(m)
+        if n + 1 == len(users):
+            load_tok().start()
+            load_cot().start()
+
+    def start():
+        load_tok().start()
+        meet(everyone)
+        for g in gcopies():
+            g.start()
+        gs_all[c] = gs[...]
+        own_cot().start()
+
+    def norm():
+        for i in range(7):
+            frm = gs_all.at[(c - i - 1 + 8) % 8]
+            remote(frm, frm, gsem_s.at[i], gsem_r.at[i], others[i]).wait_recv()
+        gain = jnp.concatenate([gs_all[i, 0:1, :] for i in range(8)], axis=1)
+        shift = jnp.concatenate([gs_all[i, 1:2, :] for i in range(8)], axis=1)
+        load_tok().wait()
+
+        @pl.loop(0, 2)
+        def _(i):
+            xo[pl.ds(32 * i, 32)] = norm_rows(ctr[0, 1 - x, pl.ds(64 * q + 32 * i, 32)], gain, shift)
+
+        @pl.loop(0, 8)
+        def _(i):
+            xl[pl.ds(32 * i, 32)] = norm_rows(ctr[0, x, pl.ds(32 * i, 32)], gain, shift)
+
+        own_xn().start()
+
+    steps["start"], steps["ln"] = start, norm
+    for u, ws in U.items():
+        for d in range(4):
+            steps[f"W{u}{d}"] = functools.partial(wg.send, ws, d)
+            steps[f"F{u}{d}"] = functools.partial(wg.forward, ws, d)
+    for name, ws in (("lwin", (0, 1, 2)), ("lwout", (5,)), ("lwexp", (3,)), ("lwcon", (4,))):
+        steps[name] = functools.partial(lambda ws: [wg.landed(w) for w in ws], ws)
+    steps["sx"] = lambda: tx.start(mine, xo)
+    steps["sc"] = lambda: tc.start(cot_mine, cot_other)
+    for name, t in (("x", tx), ("c", tc)):
+        steps["a" + name] = t.after_x
+        for d in range(4):
+            steps[f"y{name}{d}"] = functools.partial(t.y_hop, d)
+            for s in range(2):
+                steps[f"h{name}{d}{s}"] = functools.partial(t.hop, d, s)
+
+    def hidden(zz, xx, rows, row):
+        at = pl.ds(row, 256)
+        u = dot(rows[...], wx[:, :, :, pl.ds(0, 512)].reshape(2048, 512))
+        square = u * u
+        t = jnp.tanh(0.7978845608028654 * (u + 0.044715 * u * square))
+        half = 0.5 * (1.0 + t)
+        am[at, pl.ds(0, 512)] = (u * half).astype(BF)
+        hp[at, pl.ds(0, 512)] = (half + 0.5 * u * (1.0 - t * t) * (0.7978845608028654 * (1.0 + 3 * 0.044715 * square))).astype(BF)
+
+    def pull(zz, xx, rows, row):
+        at = (pl.ds(row, 256), pl.ds(0, 512))
+        hp[at] = (dot_t(rows[...], wco[pl.ds(0, 512)]) * hp[at].astype(F4)).astype(BF)
+
+    for i in range(4):
+        steps[f"hid{i}"] = functools.partial(each_half, f"hid{i}", hidden)
+        steps[f"pull{i}"] = functools.partial(each_half, f"pull{i}", pull)
+
+    def piece(ref):
+        return lambda zz, xx, r: ref[pl.ds(pl.multiple_of(512 * zz + 256 * xx + r, 64), 64)]
+
+    of = {"n": (piece(hp), lambda a, j: dot_t(a, wx[j].reshape(512, 896))),
+          "o": (piece(am), lambda a, j: dot(a, wco[:, columns(512, j)]))}
+    filled = []
+
+    def fill(name, t, i):
+        if len(filled) >= 2:
+            sent(filled[-2])
+        filled.append((t, i))
+        t.fill(i, (len(filled) - 1) % 2, *of[name])
+
+    def sent(one):
+        one[0].core(one[1]).wait_send()
+
+    def to_base(seq, rows):
+        once("tok", lambda: load_tok().wait())
+        return ctr.at[0, seq, rows]
+
+    for name, t in (("n", tn), ("o", to)):
+        for i in range(4):
+            steps[f"fill{name}{i}"] = functools.partial(fill, name, t, i)
+            steps[f"core{name}{i}"] = functools.partial(t.after_core, i, *of[name])
+            for s in range(2):
+                steps[f"l{name}{i}{s}"] = functools.partial(t.line, i, s)
+        for s in range(2):
+            steps[f"sp{name}{s}"] = functools.partial(t.spread, s, to_base if t is to else None)
+            steps[f"sy{name}{s}"] = functools.partial(t.spread_y, s)
+        steps["fin" + name] = t.finish
+
+    def by_block(zz, xx, half):
+        p = order[1, 2 * zz + xx]
+        return [pick(p, lambda j: block[i, pl.ds(j if half == 0 else 15 - j, 1)]) for i in range(2)]
+
+    cut = ORDER.index("pg") + 1
+
+    def attention(ps, qkv, qt, kt, vt, gt, ot, logs, gpos, dqt, dk, dv):
+        def project(zz, xx, rows, row):
+            three = dot(rows[...], wx[:, :, :, pl.ds(512, 384)].reshape(2048, 384))
+            for half in range(2):
+                v = three[128 * half:128 * half + 128]
+                t = angle_table(within, *by_block(zz, xx, half))
+                at = pl.ds(row + 128 * half, 128)
+                ps[at, pl.ds(0, 128)] = turn(v[:, 0:128], t).astype(BF) * BF(0.125)
+                ps[at, pl.ds(128, 128)] = turn(v[:, 128:256], t).astype(BF)
+                ps[at, pl.ds(256, 128)] = v[:, 256:384].astype(BF)
+
+        def slope(zz, xx, rows, row):
+            ps[pl.ds(row, 256), pl.ds(0, 128)] = dot_t(rows[...], wco[pl.ds(512, 128)]).astype(BF)
+
+        def landed(i, name, t, own, act):
+            once("own" + name, own)
+            t.landed(far_first(z, 3 - i))
+            each_half(f"{name}{i}", act)
+
+        def own_rows():
+            own_xn().wait()
+            tx.sent_own(mine, xo)
+
+        for i in range(4):
+            steps[f"P{i}"] = functools.partial(landed, i, "P", tx, own_rows, project)
+            steps[f"mg{i}"] = functools.partial(landed, i, "mg", tc, lambda: own_cot().wait(), slope)
+
+        def by_position(b, cols):
+            half = b // 8
+            pair = b + half * (15 - 2 * b)
+            return pick(order[0, pair], lambda j: ps[pl.ds(pl.multiple_of(256 * j + 128 * half, 128), 128), cols].astype(F4))
+
+        def by_rows(c2, half):
+            p = order[1, c2]
+            return lambda ref: pick(p, lambda j: ref[pl.ds(128 * (j if half == 0 else 15 - j), 128)])
+
+        def blocks(act):
+            @pl.loop(0, 16)
+            def _(b):
+                act(b, pl.ds(pl.multiple_of(b * 128, 128), 128))
+
+        def slots(act):
+            for half in range(2):
+                @pl.loop(0, 8)
+                def _(c2):
+                    act(by_rows(c2, half), pl.ds(pl.multiple_of(256 * c2 + 128 * half, 128), 128))
+
+        def rope():
+            def act(b, here):
+                three = by_position(b, slice(None))
+                for j, ref in enumerate((qt, kt, vt)):
+                    v = three[:, 128 * j:128 * j + 128]
+                    qkv[j, here] = v.astype(BF)
+                    ref[:, here] = v.T.astype(BF)
+            blocks(act)
+
+        def score(i, h):
+            kr = 256 * (i + 1)
+            return masked(dot(qkv[1, :kr], one_head(qt[:, pl.ds(256 * i, 256)], h, 0)), kr)
+
+        ahead = []
+
+        def forward(i):
+            kr, here = 256 * (i + 1), pl.ds(256 * i, 256)
+            for h in range(2):
+                st = ahead.pop() if ahead else score(0, 0)
+                if (i, h) != (7, 1):
+                    ahead.append(score(i + h, 1 - h))
+                peak = jnp.max(st, axis=0, keepdims=True)
+                p = jnp.exp(st - peak)
+                total = jnp.sum(p, axis=0, keepdims=True)
+                o = dot(vt[:, :kr], p.astype(BF)) * (1.0 / total)
+                ot[pl.ds(64 * h, 64), here] = o[64 * h:64 * h + 64]
+                logs[pl.ds(h, 1), here] = peak + jnp.log(total)
+
+        def mix():
+            def turned(b, here):
+                gpos[here] = ot[:, here].T
+
+            def placed(pos, row):
+                am[row, pl.ds(512, 128)] = pos(gpos).astype(BF)
+            blocks(turned)
+            slots(placed)
+
+        def gflip():
+            def act(b, here):
+                g = by_position(b, pl.ds(0, 128))
+                gpos[here] = g
+                gt[:, here] = g.T.astype(BF)
+            blocks(act)
+            dk[...] = jnp.zeros_like(dk)
+            dv[...] = jnp.zeros_like(dv)
+
+        def backward(i):
+            kr, here = 256 * (i + 1), pl.ds(256 * i, 256)
+            for h in range(2):
+                p = jnp.exp(score(i, h) - logs[pl.ds(h, 1), here])
+                low = p.astype(BF)
+                at = pl.ds(64 * h, 64)
+                delta = jnp.sum(ot[at, here] * gt[at, here].astype(F4), axis=0, keepdims=True)
+                ds = (p * (dot(qkv[2, :kr], one_head(gt[:, here], h, 0)) - delta)).astype(BF)
+                dv[:kr] += dot(low, one_head(gpos[here].astype(BF), h, 1))
+                dk[:kr] += dot(ds, one_head(qkv[0, here], h, 1))
+                dqt[at, here] = dot(kt[:, :kr], ds)[64 * h:64 * h + 64] * 0.125
+
+        def gradients():
+            def turned(b, here):
+                t = angle_table(within, block[0, pl.ds(b, 1)], block[1, pl.ds(b, 1)])
+                gpos[here] = turn_back(dqt[:, here].T, t)
+                dk[here] = turn_back(dk[here], t)
+
+            def placed(pos, row):
+                for j, ref in enumerate((gpos, dk, dv)):
+                    hp[row, pl.ds(512 + 128 * j, 128)] = pos(ref).astype(BF)
+            blocks(turned)
+            slots(placed)
+
+        steps.update(rope=rope, mix=mix, gflip=gflip, pg=gradients)
+        for i in range(8):
+            steps[f"f{i}"] = functools.partial(forward, i)
+            steps[f"b{i}"] = functools.partial(backward, i)
+        for name in ORDER[:cut]:
+            steps[name]()
+
+    pl.run_scoped(
+        attention, V((2048, 384), BF), V((3, 2048, 128), BF), V((128, 2048), BF), V((128, 2048), BF), V((128, 2048), BF),
+        V((128, 2048), BF), V((128, 2048), F4), V((8, 2048), F4), V((2048, 128), F4), V((128, 2048), F4),
+        V((2048, 128), F4), V((2048, 128), F4))
+
+    def rest_of(col, stage, sums):
+        plan = [n for n in ORDER if len(n) == 3 and n[0] in "gk" and n[1:].isdigit()]
+
+        def block_load(n):
+            xx = 1 - x if plan[n][0] == "g" else x
+            src, d = (ct, xn)[int(plan[n][1])], mirrored(z, int(plan[n][2]))
+            return pltpu.make_async_copy(src.at[:, :, :, columns(256, 2 * ((z + d) % 4) + xx)], col.at[n % 3], csem.at[n % 3])
+
+        def grad(n):
+            j, e = int(plan[n][1]), int(plan[n][2])
+            block_load(n).wait()
+            terms = dot(flip(col[n % 3].reshape(2048, 256)), (am, hp)[j][...])
+            g = (g1, g2)[j]
+            (g.give if plan[n][0] == "g" else g.keep)(e, terms if j else terms.T)
+            if n + 3 < len(plan):
+                block_load(n + 3).start()
+
+        for n in range(3):
+            block_load(n).start()
+        copies = [remote(vec.at[(c + i + 1) % 8], vecs.at[c], vs.at[i], vr.at[i], others[i]) for i in range(7)]
+
+        def normed_gradient():
+            once("tok", lambda: load_tok().wait())
+            load_cot().wait()
+            norm_backward(ctr.at[0], ctr.at[1], ng, gs_all, ig, stage, ssem, sums)
+            for i in range(8):
+                at = slice(256 * i, 256 * i + 256)
+                for j in range(2):
+                    vec[i, j:j + 1, :] = jnp.sum(sums[j, :, at], axis=0, keepdims=True)
+                vec[i, 2:8, :] = jnp.zeros((6, 256), F4)
+            vecs[c] = vec[c]
+            for cp in copies:
+                cp.start()
+
+        def gradients():
+            g1.finish()
+            g2.finish()
+
+        steps["norm"], steps["gf"] = normed_gradient, gradients
+        for n, name in enumerate(plan):
+            steps[name] = functools.partial(grad, n)
+        for name in ORDER[cut:]:
+            steps[name]()
+        for i in range(7):
+            frm = vecs.at[(c - i - 1 + 8) % 8]
+            remote(frm, frm, vs.at[i], vr.at[i], others[i]).wait_recv()
+        total = vecs[0]
+        for i in range(1, 8):
+            total = total + vecs[i]
+        vectors[...] = total
+        for cp in copies:
+            cp.wait_send()
+
+    pl.run_scoped(rest_of, V((3, 4, 2, 256, 256), BF), V((2, 32, 2048), F4), V((2, 8, 2048), F4))
+    for one in filled[-2:]:
+        sent(one)
+    tx.finish()
+    tc.sent_own(cot_mine, cot_other)
+    tc.finish()
+    for w in range(6):
+        wg.finish(w)
+    for g in gcopies():
+        g.wait_send()
+
+
+def block_call(order, gs, tok, cot, win, wout, wexp, wcon):
+    S = jax.ShapeDtypeStruct
+    ANY = pl.BlockSpec(memory_space=pl.ANY)
+    VM = pl.BlockSpec(memory_space=pltpu.VMEM)
+    D = pltpu.SemaphoreType.DMA
+    V = pltpu.VMEM
+    rows = (4, 2, 256, 2048)
+    return pl.pallas_call(
+        block_kernel,
+        out_shape=[S((2, 256, 2048), BF), S((2, 256, 2048), F4), S((8, 256), F4),
+                   S((3, 256, 512), BF), S((512, 256), BF), S((256, 2048), BF), S((2048, 256), BF), S(rows, BF), S(rows, BF)],
+        in_specs=[pl.BlockSpec(memory_space=pltpu.SMEM)] + [VM] * 3 + [ANY] * 6,
+        out_specs=[ANY, ANY, VM] + [ANY] * 6,
+        scratch_shapes=[V((4, 2, 256, 896), BF), V((640, 2048), BF), V((2048, 896), BF), V((2048, 640), BF), V((2, 2, 2, 64, 2048), BF),
+                        V((2, 2, 256, 2048), BF), V((2, 256, 2048), BF), V((8, 8, 256), F4), V((8, 8, 256), F4), V((8, 8, 256), F4),
+                        D((7,)), D((7,)), D((4,)), D((2, 2)), D((3,)), D((2,)), D((7,)), D((7,))]
+        + token_sems() * 2 + weight_sems(6) + (reduce_bufs() + reduce_sems()) * 2 + grad_scratch((640, 256), 2) + grad_scratch((256, 896), 4),
+        compiler_params=pltpu.CompilerParams(collective_id=0, has_side_effects=True, vmem_limit_bytes=63 * MB),
+        name="block",
+    )(order, gs, jnp.asarray(angles(128, 1)), jnp.asarray(angles(16, 128)), tok, cot, win, wout, wexp, wcon)
+
+
+def own_local(tokens, pair_index, norm_gain, norm_shift, w_attention_in, w_attention_out, w_expand, w_contract, cotangent):
+    x = lax.axis_index("ctx") % 2
+    pairs = lax.dynamic_index_in_dim(pair_index, x, 0, False)
+    which = jnp.arange(8, dtype=jnp.int32)
+    inverse = jnp.sum(jnp.where(pairs[None, :] == which[:, None], which[None, :], 0), axis=1).astype(jnp.int32)
+    gs = jnp.concatenate([norm_gain[None], norm_shift[None], jnp.zeros((6, 256), BF)], axis=0).astype(F4)
+    output, input_grad, vectors, *grads = block_call(
+        jnp.stack([inverse, pairs]), gs, tokens, cotangent, w_attention_in, w_attention_out, w_expand, w_contract)
+    return (output, input_grad, vectors[0], vectors[1], *(g.astype(F4) for g in grads[:4]))
+
+
+def local(tokens, pair_index, norm_gain, norm_shift, w_attention_in, w_attention_out, w_expand, w_contract, cotangent):
+    args = (tokens, pair_index, norm_gain, norm_shift, w_attention_in, w_attention_out, w_expand, w_contract, cotangent)
+    sizes = (lax.axis_size("ctx"), lax.axis_size("tp")) + tokens.shape + w_attention_in.shape[2:] + w_expand.shape[1:]
+    if sizes == (8, 4, 2, 256, 2048, 512, 2048):
+        return own_local(*args)
+    return general_local(*args)
+
+
 def solution(mesh):
     in_specs = (
         P(None, "ctx", None),

time: 1350 us -> 336 us (0.25)
  waiting for transfers between devices: 953 us -> 0 us
  Pallas kernels: 0 us -> 310 us
  matrix products: 199 us -> 0 us
  blocking collectives: 61.6 us -> 0 us
  local copies, waits for them, and re-layouts: 59.1 us -> 9.27 us
  other arithmetic: 53.4 us -> 8.66 us
  between operations: 15.6 us -> 0.87 us
    reduce_scatter x6 -> x0, waiting for transfers between devices: 555 us -> none  [the longest x1 149 us: local(): lax.psum_scatter(contract_grad.astype(jnp.bfloat16), 'ctx', scatter_dimen...]
    pallas_call x0 -> x1, Pallas kernels: none -> 310 us  [block_call(): pl.pallas_call(block_kernel, out_shape=[S((2, 256, 2048), BF), S((2, 256,...]
    all_gather x6 -> x0, waiting for transfers between devices: 309 us -> none  [the longest x1 114 us: local(): lax.all_gather(w_expand, 'ctx', axis=0, tiled=True)]
    dot_general x26 -> x0, matrix products: 199 us -> none  [the longest x2 21.6 us: full_one_turn(): jnp.einsum('shqk,sqhe->skhe', weights_low, out_grad, preferred_element_ty...]
    psum x1 -> x0, waiting for transfers between devices: 85.8 us -> none  [local(): branch = lax.psum(branch.astype(jnp.bfloat16), 'tp').astype(jnp.float32)]
    all_gather x2 -> x0, blocking collectives: 38.9 us -> none  [the longest x1 22.4 us: local(): lax.all_gather(norm_gain, 'ctx', axis=0, tiled=True)]
    reduce_sum x9 -> x1, other arithmetic: 28.7 us -> 0.12 us  [own_local(): jnp.sum(jnp.where(pairs[None, :] == which[:, None], which[None, :], 0), a...]
    unnamed x1 -> x0, blocking collectives: 22.7 us -> none
  transfers between devices with their start and end apart: 13 -> 0, of which waited for: 12 -> 0; matrix products, arithmetic and copies ran while one was open for 23% -> 0% of each run, Pallas kernels for 0% -> 0%
where the time goes in v4:
time: 336 us; the launch traced here: 329 us
  Pallas kernels  310 us (92%)
  local copies, waits for them, and re-layouts  9.27 us (3%)
  other arithmetic  8.66 us (3%)
    pallas_call x1, Pallas kernels, block_call(): pl.pallas_call(block_kernel, out_shape=[S((2, 256, 2048), BF), S((2, 256,...  310 us
    convert_element_type x4, other arithmetic, own_local(): g.astype(F4)  7.3 us

profile of v4, /device:TPU:0, one launch (start us, length us, event | category | flops | bytes accessed | tf_op | source)
XLA Modules:
  0.0 329.3 jit_solution(758957223697504318)
XLA Ops:
  0.6 0.0 copy-start
  0.7 0.7 copy-done
  1.3 0.1 select_reduce_fusion
  1.4 0.6 pad_add_fusion.order
  2.0 0.1 pad.2.clone
  2.1 0.7 broadcast_in_dim.26
  2.8 0.7 broadcast_in_dim.27
  3.4 0.7 maximum_convert_fusion.gs
  4.1 310.5 %block.2 = (bf16[2,256,2048]{2,1,0:T(8,128)(2,1)}, f32[2,256,2048]{2,1,0:T(8,128)}, f32[8,256]{1,0:T(8,128)}, bf16[3,256,512]{2,1,0:T(8,128)(2,1)}, bf16[512,256...) custom-call(s32[2,8]{1,0:T(2,128)} %pad_add_fusion.order, ...), custom_call_target="tpu_custom_call" | custom-call | tf_op jit(solution)/shard_map/block/pallas_call | solution.py:1255
  314.6 0.0 copy-start.4
  314.6 1.4 fusion
  315.9 1.8 convert_element_type.17
  317.7 2.5 convert_element_type.16
  320.2 0.0 copy-done.4
  320.2 0.0 copy-start.3
  320.2 1.6 convert_element_type.18
  321.8 0.0 copy-done.3
  321.8 0.0 copy-start.2
  321.8 1.5 convert_element_type.19
  323.3 0.9 copy-done.2
  324.1 0.0 copy-start.1
  324.1 1.3 copy.21
  325.4 1.6 copy-done.1
  327.1 2.0 copy.22
  (3 shorter events, 0.0 us)
Async XLA Ops:
  0.6 0.7 copy-start
  314.6 5.7 %copy-start.4 = (bf16[256,2048]{1,0:T(8,128)(2,1)S(1)}, bf16[256,2048]{1,0:T(8,128)(2,1)}, u32[]{:S(2)}) copy-start(bf16[256,2048]{1,0:T(8,128)(2,1)} %get-tuple-element.20) | copy-start | bytes 3145732
  320.2 1.6 copy-start.3
  321.8 2.3 copy-start.2
  324.1 2.9 copy-start.1

commit v5 on v4

--- a/solution.py
+++ b/solution.py
@@ -705,14 +705,15 @@
                 pl.when(z != zz)(lambda: self.up(zz, s).wait_send())
         self.xex().wait_send()
         for s in range(2):
-            a, b, c = self.fin_copies(s)
-            a.wait()
-            b.wait_send()
-            c.wait_send()
+            for copy in self.fin_copies(s)[1:]:
+                copy.wait_send()
             self.relay(s).wait_send()
-            for j, yy in ((0, self.y), (1, 1 - self.y)):
-                r = self.spot(s, 2 * yy + 1 - self.k)
-                remote(r, r, self.fcs.at[s, j], self.fcr.at[s, j], device(self.z, self.x, self.y, 1 - self.k)).wait_recv()
+
+    def landed(self, s):
+        self.fin_copies(s)[0].wait()
+        for j, yy in ((0, self.y), (1, 1 - self.y)):
+            r = self.spot(s, 2 * yy + 1 - self.k)
+            remote(r, r, self.fcs.at[s, j], self.fcr.at[s, j], device(self.z, self.x, self.y, 1 - self.k)).wait_recv()
 
 
 def reduce_sems():
@@ -833,16 +834,15 @@
     return v.astype(F4).T.astype(BF)
 
 
-def norm_backward(tok, cot, ng, gains, out, stage, ssem, sums):
+def norm_backward(s, tok, cot, ng, gains, out, stage, ssem, sums):
     gain = jnp.concatenate([gains[i, 0:1, :] for i in range(8)], axis=1)
-    sums[...] = jnp.zeros_like(sums)
 
     def store(i):
-        return pltpu.make_async_copy(stage.at[i % 2], out.at[i // 8, pl.ds(pl.multiple_of(32 * (i % 8), 32), 32)], ssem.at[i % 2])
-
-    @pl.loop(0, 16)
+        return pltpu.make_async_copy(stage.at[i % 2], out.at[s, pl.ds(pl.multiple_of(32 * i, 32), 32)], ssem.at[i % 2])
+
+    @pl.loop(0, 8)
     def _(i):
-        s, at = i // 8, pl.ds(pl.multiple_of(32 * (i % 8), 32), 32)
+        at = pl.ds(pl.multiple_of(32 * i, 32), 32)
         v = tok[s, at].astype(F4)
         centred = v - jnp.mean(v, axis=-1, keepdims=True)
         scale = lax.rsqrt(jnp.mean(centred * centred, axis=-1, keepdims=True) + EPS)
@@ -860,26 +860,38 @@
         sums[0] += both[:8] + both[8:16] + both[16:24] + both[24:]
         sums[1] += n[:8] + n[8:16] + n[16:24] + n[24:]
 
-    store(14).wait()
-    store(15).wait()
-
-
+    store(6).wait()
+    store(7).wait()
+
+
+(
+    START, NORM, SEND, PASS, HAVE, OPEN, CROSS, HOP, TWIN, PROJECT, ARRANGE, ATTEND, MIX, SLOPE, TURN, RETURN, PROJECTED, HIDDEN,
+    PULL, FILL, CORE, LINE, SPREAD, RELAY, DONE, GIVE, KEEP, LAST, GRADIENTS,
+) = range(29)
 ORDER = (
-    "start", "WB1", "WB2", "ln", "sx", "WB3", "WB0", "hx10", "FB3", "ax", "WA1", "hx20", "WA0", "FB1", "hx11", "WC0", "WA2", "WA3",
-    "hx21", "FA1", "WC3", "yx0", "WC1", "FA2", "yx1", "sc", "hx31", "yx2", "FA3", "hx30", "ac", "FB2", "yx3", "WC2", "hc10", "lwin",
-    "P0", "FC1", "P1", "P2", "P3", "FC3", "rope", "hc11", "f0", "f1", "f2", "lwexp", "hid0", "hid1", "hc20", "hid2", "f3", "yc0", "FC2",
-    "yc1", "f4", "hc21", "f5", "f6", "f7", "hc30", "lwout", "lwcon", "mix", "fillo0", "fillo1", "fillo2", "yc2", "hc31", "hid3",
-    "coreo0", "mg0", "coreo1", "yc3", "mg1", "fillo3", "mg2", "coreo2", "mg3", "gflip", "b0", "b1", "lo01", "coreo3", "b2", "b3", "b4",
-    "lo00", "b5", "b6", "lo11", "b7", "pg", "lo10", "g01", "lo21", "pull0", "lo20", "g02", "filln0", "pull1", "g03", "pull2", "k01",
-    "g00", "coren0", "filln1", "lo30", "filln2", "k02", "pull3", "g11", "coren1", "ln01", "g12", "g13", "k03", "g10", "coren2", "ln00",
-    "ln11", "ln21", "lo31", "filln3", "spo0", "ln10", "k12", "coren3", "ln20", "ln31", "k11", "k00", "ln30", "spn0", "spn1", "syn1",
-    "syn0", "syo0", "spo1", "k13", "finn", "norm", "k10", "syo1", "fino", "gf",
+    (START,), (SEND, 1, 1), (SEND, 0, 1), (SEND, 0, 3), (SEND, 0, 2), (PASS, 0, 1), (SEND, 1, 0), (NORM,), (OPEN, 0), (CROSS, 0),
+    (SEND, 2, 3), (HOP, 0, 1, 0), (HOP, 0, 1, 1), (PASS, 0, 3), (SEND, 1, 3), (HOP, 0, 2, 0), (HOP, 0, 2, 1), (SEND, 0, 0),
+    (HOP, 0, 3, 0), (HOP, 0, 3, 1), (TWIN, 0, 0), (TWIN, 0, 1), (SEND, 1, 2), (OPEN, 1), (PASS, 0, 2), (TWIN, 0, 3), (TWIN, 0, 2),
+    (HAVE, 0), (SEND, 2, 1), (SEND, 2, 2), (SEND, 2, 0), (CROSS, 1), (PASS, 1, 1), (HOP, 1, 1, 0), (PASS, 1, 3), (PROJECT, 0),
+    (PROJECT, 1), (PASS, 1, 2), (PROJECT, 2), (PROJECT, 3), (ARRANGE,), (ATTEND, 0), (ATTEND, 1), (ATTEND, 2), (ATTEND, 3),
+    (HOP, 1, 1, 1), (ATTEND, 4), (HAVE, 3), (PASS, 2, 1), (HAVE, 1), (HIDDEN, 0), (ATTEND, 5), (PASS, 2, 3), (ATTEND, 6),
+    (TWIN, 1, 0), (HOP, 1, 2, 0), (HIDDEN, 1), (HOP, 1, 2, 1), (TWIN, 1, 1), (PASS, 2, 2), (HIDDEN, 2), (ATTEND, 7), (MIX,),
+    (HOP, 1, 3, 0), (HOP, 1, 3, 1), (HAVE, 2), (FILL, 1, 0), (FILL, 1, 1), (TWIN, 1, 2), (SLOPE, 0), (FILL, 1, 2), (CORE, 1, 0),
+    (CORE, 1, 1), (HIDDEN, 3), (LINE, 1, 0, 1), (TWIN, 1, 3), (SLOPE, 1), (SLOPE, 2), (CORE, 1, 2), (SLOPE, 3), (TURN,), (RETURN, 0),
+    (RETURN, 1), (LINE, 1, 0, 0), (RETURN, 2), (RETURN, 3), (RETURN, 4), (LINE, 1, 1, 1), (RETURN, 5), (RETURN, 6), (LINE, 1, 1, 0),
+    (RETURN, 7), (PROJECTED,), (GIVE, 0, 1), (GIVE, 0, 2), (PULL, 0), (FILL, 0, 0), (LINE, 1, 2, 0), (GIVE, 0, 3), (FILL, 1, 3),
+    (KEEP, 0, 1), (CORE, 0, 0), (CORE, 1, 3), (GIVE, 0, 0), (LINE, 1, 2, 1), (PULL, 1), (LINE, 0, 0, 1), (PULL, 2), (PULL, 3),
+    (GIVE, 1, 1), (FILL, 0, 1), (FILL, 0, 2), (KEEP, 0, 2), (CORE, 0, 1), (FILL, 0, 3), (GIVE, 1, 2), (LINE, 0, 0, 0),
+    (LINE, 1, 3, 1), (CORE, 0, 2), (KEEP, 1, 1), (GIVE, 1, 3), (LINE, 0, 1, 1), (KEEP, 0, 3), (CORE, 0, 3), (LINE, 0, 1, 0),
+    (LINE, 0, 2, 1), (LINE, 0, 2, 0), (KEEP, 1, 3), (LINE, 0, 3, 1), (LINE, 1, 3, 0), (SPREAD, 1, 0), (LINE, 0, 3, 0), (KEEP, 1, 2),
+    (SPREAD, 1, 1), (RELAY, 1, 0), (GIVE, 1, 0), (SPREAD, 0, 0), (SPREAD, 0, 1), (RELAY, 0, 0), (RELAY, 1, 1), (DONE, 1, 1),
+    (DONE, 1, 0), (DONE, 0, 0), (LAST, 0), (RELAY, 0, 1), (KEEP, 1, 0), (DONE, 0, 1), (LAST, 1), (KEEP, 0, 0), (GRADIENTS,),
 )
 
 
-def block_kernel(order, gs, within, block, tok, cot, win, wout, wexp, wcon,
+def block_kernel(pairs_of, gains, within, block, tok, cot, win, wout, wexp, wcon,
                  out, ig, vectors, gin, gout, gexp, gcon, xn, ct,
-                 wx, wco, hp, am, S, ctr, ng, gs_all, vec, vecs,
+                 wx, wco, hp, am, S, ctr, ng, gs, gs_all, vec, vecs,
                  gsem_s, gsem_r, lsem, rsem, csem, ssem, vs, vr, *rest):
     z, x, y, k = place()
     c, q = z * 2 + x, 2 * y + k
@@ -907,14 +919,24 @@
                     *take(2), take(4))
     others, everyone = peers_of(z, x, y, k)
 
+    def pair_at(slot):
+        return pairs_of[x, slot]
+
+    def slot_of(pair):
+        found = jnp.int32(0)
+        for j in range(8):
+            found = jnp.where(pairs_of[x, j] == pair, j, found)
+        return found
+
+
     V = pltpu.VMEM
     steps = {}
     flags = set()
-    U = {"A": (0, 1, 2, 5), "B": (3,), "C": (4,)}
     load_tok = lambda: pltpu.make_async_copy(tok, ctr.at[0], lsem.at[0])
     load_cot = lambda: pltpu.make_async_copy(cot, ctr.at[1], lsem.at[1])
-    own_cot = lambda: pltpu.make_async_copy(cot.at[x], ct.at[z, x], lsem.at[2])
-    xl, xo = ctr.at[1, 0], ctr.at[1, 1, pl.ds(0, 64)]
+    xl, xo, cl = ctr.at[1, 0], S.at[0, 0, 0], ctr.at[1, 1]
+    near_cot = lambda: pltpu.make_async_copy(cot.at[x], cl, lsem.at[1])
+    own_cot = lambda: pltpu.make_async_copy(cl, ct.at[z, x], lsem.at[2])
     own_xn = lambda: pltpu.make_async_copy(xl, xn.at[z, x], lsem.at[3])
     gcopies = lambda: [remote(gs, gs_all.at[c], gsem_s.at[i], gsem_r.at[i], others[i]) for i in range(7)]
     mine, cot_mine = xl.at[pl.ds(64 * q, 64)], cot.at[x, pl.ds(64 * q, 64)]
@@ -925,13 +947,12 @@
             flags.add(name)
             act()
 
-    users = [n for n in ORDER if n[:-1] in ("P", "mg", "hid", "pull")]
+    users = [n for n in ORDER if n[0] in (PROJECT, SLOPE, HIDDEN, PULL)]
 
     def rows_in(n, xx):
-        name = users[n]
-        i = int(name[-1])
-        zz = far_first(z, i if name[:-1] in ("hid", "pull") else 3 - i)
-        src = xn if name[:-1] in ("P", "hid") else ct
+        kind, i = users[n]
+        zz = far_first(z, i if kind in (HIDDEN, PULL) else 3 - i)
+        src = xn if kind in (PROJECT, HIDDEN) else ct
         return zz, pltpu.make_async_copy(src.at[zz, xx], ctr.at[n % 2, xx], rsem.at[n % 2, xx])
 
     def begin_rows(n):
@@ -949,7 +970,7 @@
             act(zz, xx, ctr.at[n % 2, xx], pl.multiple_of(512 * zz + 256 * xx, 256))
         flags.add(name)
         for m in (n + 1, n + 2):
-            if m < len(users) and m not in flags and {"hid": "P3", "pull": "mg3"}.get(users[m][:-1]) in flags:
+            if m < len(users) and m not in flags and {HIDDEN: (PROJECT, 3), PULL: (SLOPE, 3)}.get(users[m][0]) in flags:
                 begin_rows(m)
         if n + 1 == len(users):
             load_tok().start()
@@ -957,11 +978,13 @@
 
     def start():
         load_tok().start()
+        gs[...] = jnp.zeros_like(gs)
+        gs[0:2, :] = gains[...]
         meet(everyone)
         for g in gcopies():
             g.start()
         gs_all[c] = gs[...]
-        own_cot().start()
+        near_cot().start()
 
     def norm():
         for i in range(7):
@@ -980,22 +1003,24 @@
             xl[pl.ds(32 * i, 32)] = norm_rows(ctr[0, x, pl.ds(32 * i, 32)], gain, shift)
 
         own_xn().start()
-
-    steps["start"], steps["ln"] = start, norm
-    for u, ws in U.items():
+        near_cot().wait()
+        own_cot().start()
+
+    steps[START,], steps[NORM,] = start, norm
+    for u, ws in enumerate(((0, 1, 2, 5), (3,), (4,))):
         for d in range(4):
-            steps[f"W{u}{d}"] = functools.partial(wg.send, ws, d)
-            steps[f"F{u}{d}"] = functools.partial(wg.forward, ws, d)
-    for name, ws in (("lwin", (0, 1, 2)), ("lwout", (5,)), ("lwexp", (3,)), ("lwcon", (4,))):
-        steps[name] = functools.partial(lambda ws: [wg.landed(w) for w in ws], ws)
-    steps["sx"] = lambda: tx.start(mine, xo)
-    steps["sc"] = lambda: tc.start(cot_mine, cot_other)
-    for name, t in (("x", tx), ("c", tc)):
-        steps["a" + name] = t.after_x
+            steps[SEND, u, d] = functools.partial(wg.send, ws, d)
+            steps[PASS, u, d] = functools.partial(wg.forward, ws, d)
+    for u, ws in enumerate(((0, 1, 2), (3,), (4,), (5,))):
+        steps[HAVE, u] = functools.partial(lambda ws: [wg.landed(w) for w in ws], ws)
+    steps[OPEN, 0] = lambda: tx.start(mine, xo)
+    steps[OPEN, 1] = lambda: tc.start(cot_mine, cot_other)
+    for name, t in enumerate((tx, tc)):
+        steps[CROSS, name] = t.after_x
         for d in range(4):
-            steps[f"y{name}{d}"] = functools.partial(t.y_hop, d)
+            steps[TWIN, name, d] = functools.partial(t.y_hop, d)
             for s in range(2):
-                steps[f"h{name}{d}{s}"] = functools.partial(t.hop, d, s)
+                steps[HOP, name, d, s] = functools.partial(t.hop, d, s)
 
     def hidden(zz, xx, rows, row):
         at = pl.ds(row, 256)
@@ -1011,14 +1036,13 @@
         hp[at] = (dot_t(rows[...], wco[pl.ds(0, 512)]) * hp[at].astype(F4)).astype(BF)
 
     for i in range(4):
-        steps[f"hid{i}"] = functools.partial(each_half, f"hid{i}", hidden)
-        steps[f"pull{i}"] = functools.partial(each_half, f"pull{i}", pull)
+        steps[HIDDEN, i] = functools.partial(each_half, (HIDDEN, i), hidden)
+        steps[PULL, i] = functools.partial(each_half, (PULL, i), pull)
 
     def piece(ref):
         return lambda zz, xx, r: ref[pl.ds(pl.multiple_of(512 * zz + 256 * xx + r, 64), 64)]
 
-    of = {"n": (piece(hp), lambda a, j: dot_t(a, wx[j].reshape(512, 896))),
-          "o": (piece(am), lambda a, j: dot(a, wco[:, columns(512, j)]))}
+    of = ((piece(hp), lambda a, j: dot_t(a, wx[j].reshape(512, 896))), (piece(am), lambda a, j: dot(a, wco[:, columns(512, j)])))
     filled = []
 
     def fill(name, t, i):
@@ -1031,25 +1055,25 @@
         one[0].core(one[1]).wait_send()
 
     def to_base(seq, rows):
-        once("tok", lambda: load_tok().wait())
+        once(load_tok, lambda: load_tok().wait())
         return ctr.at[0, seq, rows]
 
-    for name, t in (("n", tn), ("o", to)):
+    for name, t in enumerate((tn, to)):
         for i in range(4):
-            steps[f"fill{name}{i}"] = functools.partial(fill, name, t, i)
-            steps[f"core{name}{i}"] = functools.partial(t.after_core, i, *of[name])
+            steps[FILL, name, i] = functools.partial(fill, name, t, i)
+            steps[CORE, name, i] = functools.partial(t.after_core, i, *of[name])
             for s in range(2):
-                steps[f"l{name}{i}{s}"] = functools.partial(t.line, i, s)
+                steps[LINE, name, i, s] = functools.partial(t.line, i, s)
         for s in range(2):
-            steps[f"sp{name}{s}"] = functools.partial(t.spread, s, to_base if t is to else None)
-            steps[f"sy{name}{s}"] = functools.partial(t.spread_y, s)
-        steps["fin" + name] = t.finish
+            steps[SPREAD, name, s] = functools.partial(t.spread, s, to_base if t is to else None)
+            steps[RELAY, name, s] = functools.partial(t.spread_y, s)
+            steps[DONE, name, s] = functools.partial(t.landed, s)
 
     def by_block(zz, xx, half):
-        p = order[1, 2 * zz + xx]
+        p = pair_at(2 * zz + xx)
         return [pick(p, lambda j: block[i, pl.ds(j if half == 0 else 15 - j, 1)]) for i in range(2)]
 
-    cut = ORDER.index("pg") + 1
+    cut = ORDER.index((PROJECTED,)) + 1
 
     def attention(ps, qkv, qt, kt, vt, gt, ot, logs, gpos, dqt, dk, dv):
         def project(zz, xx, rows, row):
@@ -1065,26 +1089,27 @@
         def slope(zz, xx, rows, row):
             ps[pl.ds(row, 256), pl.ds(0, 128)] = dot_t(rows[...], wco[pl.ds(512, 128)]).astype(BF)
 
-        def landed(i, name, t, own, act):
-            once("own" + name, own)
+        def landed(i, kind, t, act):
+            once(own_rows, own_rows)
             t.landed(far_first(z, 3 - i))
-            each_half(f"{name}{i}", act)
+            each_half((kind, i), act)
 
         def own_rows():
             own_xn().wait()
+            own_cot().wait()
             tx.sent_own(mine, xo)
 
         for i in range(4):
-            steps[f"P{i}"] = functools.partial(landed, i, "P", tx, own_rows, project)
-            steps[f"mg{i}"] = functools.partial(landed, i, "mg", tc, lambda: own_cot().wait(), slope)
+            steps[PROJECT, i] = functools.partial(landed, i, PROJECT, tx, project)
+            steps[SLOPE, i] = functools.partial(landed, i, SLOPE, tc, slope)
 
         def by_position(b, cols):
             half = b // 8
             pair = b + half * (15 - 2 * b)
-            return pick(order[0, pair], lambda j: ps[pl.ds(pl.multiple_of(256 * j + 128 * half, 128), 128), cols].astype(F4))
+            return pick(slot_of(pair), lambda j: ps[pl.ds(pl.multiple_of(256 * j + 128 * half, 128), 128), cols].astype(F4))
 
         def by_rows(c2, half):
-            p = order[1, c2]
+            p = pair_at(c2)
             return lambda ref: pick(p, lambda j: ref[pl.ds(128 * (j if half == 0 else 15 - j), 128)])
 
         def blocks(act):
@@ -1168,10 +1193,10 @@
             blocks(turned)
             slots(placed)
 
-        steps.update(rope=rope, mix=mix, gflip=gflip, pg=gradients)
+        steps[ARRANGE,], steps[MIX,], steps[TURN,], steps[PROJECTED,] = rope, mix, gflip, gradients
         for i in range(8):
-            steps[f"f{i}"] = functools.partial(forward, i)
-            steps[f"b{i}"] = functools.partial(backward, i)
+            steps[ATTEND, i] = functools.partial(forward, i)
+            steps[RETURN, i] = functools.partial(backward, i)
         for name in ORDER[:cut]:
             steps[name]()
 
@@ -1181,19 +1206,19 @@
         V((2048, 128), F4), V((2048, 128), F4))
 
     def rest_of(col, stage, sums):
-        plan = [n for n in ORDER if len(n) == 3 and n[0] in "gk" and n[1:].isdigit()]
+        plan = [n for n in ORDER if n[0] in (GIVE, KEEP)]
 
         def block_load(n):
-            xx = 1 - x if plan[n][0] == "g" else x
-            src, d = (ct, xn)[int(plan[n][1])], mirrored(z, int(plan[n][2]))
+            kind, j, e = plan[n]
+            src, d, xx = (ct, xn)[j], mirrored(z, e), 1 - x if kind == GIVE else x
             return pltpu.make_async_copy(src.at[:, :, :, columns(256, 2 * ((z + d) % 4) + xx)], col.at[n % 3], csem.at[n % 3])
 
         def grad(n):
-            j, e = int(plan[n][1]), int(plan[n][2])
+            kind, j, e = plan[n]
             block_load(n).wait()
             terms = dot(flip(col[n % 3].reshape(2048, 256)), (am, hp)[j][...])
             g = (g1, g2)[j]
-            (g.give if plan[n][0] == "g" else g.keep)(e, terms if j else terms.T)
+            (g.give if kind == GIVE else g.keep)(e, terms if j else terms.T)
             if n + 3 < len(plan):
                 block_load(n + 3).start()
 
@@ -1201,10 +1226,14 @@
             block_load(n).start()
         copies = [remote(vec.at[(c + i + 1) % 8], vecs.at[c], vs.at[i], vr.at[i], others[i]) for i in range(7)]
 
-        def normed_gradient():
-            once("tok", lambda: load_tok().wait())
-            load_cot().wait()
-            norm_backward(ctr.at[0], ctr.at[1], ng, gs_all, ig, stage, ssem, sums)
+        def normed_gradient(s):
+            once(load_tok, lambda: load_tok().wait())
+            once(load_cot, lambda: load_cot().wait())
+            if s == 0:
+                sums[...] = jnp.zeros_like(sums)
+            norm_backward(x if s == 0 else 1 - x, ctr.at[0], ctr.at[1], ng, gs_all, ig, stage, ssem, sums)
+            if s == 0:
+                return
             for i in range(8):
                 at = slice(256 * i, 256 * i + 256)
                 for j in range(2):
@@ -1218,7 +1247,9 @@
             g1.finish()
             g2.finish()
 
-        steps["norm"], steps["gf"] = normed_gradient, gradients
+        steps[GRADIENTS,] = gradients
+        for s in range(2):
+            steps[LAST, s] = functools.partial(normed_gradient, s)
         for n, name in enumerate(plan):
             steps[name] = functools.partial(grad, n)
         for name in ORDER[cut:]:
@@ -1236,6 +1267,8 @@
     pl.run_scoped(rest_of, V((3, 4, 2, 256, 256), BF), V((2, 32, 2048), F4), V((2, 8, 2048), F4))
     for one in filled[-2:]:
         sent(one)
+    tn.finish()
+    to.finish()
     tx.finish()
     tc.sent_own(cot_mine, cot_other)
     tc.finish()
@@ -1245,7 +1278,7 @@
         g.wait_send()
 
 
-def block_call(order, gs, tok, cot, win, wout, wexp, wcon):
+def block_call(pairs_of, gains, tok, cot, win, wout, wexp, wcon):
     S = jax.ShapeDtypeStruct
     ANY = pl.BlockSpec(memory_space=pl.ANY)
     VM = pl.BlockSpec(memory_space=pltpu.VMEM)
@@ -1259,23 +1292,60 @@
         in_specs=[pl.BlockSpec(memory_space=pltpu.SMEM)] + [VM] * 3 + [ANY] * 6,
         out_specs=[ANY, ANY, VM] + [ANY] * 6,
         scratch_shapes=[V((4, 2, 256, 896), BF), V((640, 2048), BF), V((2048, 896), BF), V((2048, 640), BF), V((2, 2, 2, 64, 2048), BF),
-                        V((2, 2, 256, 2048), BF), V((2, 256, 2048), BF), V((8, 8, 256), F4), V((8, 8, 256), F4), V((8, 8, 256), F4),
+                        V((2, 2, 256, 2048), BF), V((2, 256, 2048), BF), V((8, 256), F4), V((8, 8, 256), F4), V((8, 8, 256), F4), V((8, 8, 256), F4),
                         D((7,)), D((7,)), D((4,)), D((2, 2)), D((3,)), D((2,)), D((7,)), D((7,))]
         + token_sems() * 2 + weight_sems(6) + (reduce_bufs() + reduce_sems()) * 2 + grad_scratch((640, 256), 2) + grad_scratch((256, 896), 4),
         compiler_params=pltpu.CompilerParams(collective_id=0, has_side_effects=True, vmem_limit_bytes=63 * MB),
         name="block",
-    )(order, gs, jnp.asarray(angles(128, 1)), jnp.asarray(angles(16, 128)), tok, cot, win, wout, wexp, wcon)
+    )(pairs_of, gains, jnp.asarray(angles(128, 1)), jnp.asarray(angles(16, 128)), tok, cot, win, wout, wexp, wcon)
+
+
+def finish_kernel(out, ig, gin, gout, gexp, gcon, out_to, ig_to, gin_to, gout_to, gexp_to, gcon_to,
+                  vin, vout, vexp, vcon, fin, fout, fexp, fcon, through, wide, isem, osem):
+    work = ((gexp, vexp, fexp, gexp_to), (gcon, vcon, fcon, gcon_to), (gin, vin, fin, gin_to), (gout, vout, fout, gout_to),
+            (ig, wide, wide, ig_to), (out, through, through, out_to))
+    loads = [pltpu.make_async_copy(w[0], w[1], isem.at[i]) for i, w in enumerate(work)]
+    stores = [pltpu.make_async_copy(w[2], w[3], osem.at[i]) for i, w in enumerate(work)]
+    for copy in loads:
+        copy.start()
+    for (_, low, full, _), load, store in zip(work, loads, stores):
+        load.wait()
+        if low is not full:
+            rows = low.shape[-2]
+            for j in range(low.shape[0] if len(low.shape) == 3 else 1):
+                @pl.loop(0, rows // 128)
+                def _(i):
+                    at = (pl.ds(pl.multiple_of(128 * i, 128), 128),)
+                    at = (j,) + at if len(low.shape) == 3 else at
+                    full[at] = low[at].astype(F4)
+        store.start()
+    for copy in stores:
+        copy.wait()
+
+
+def finish_call(out, ig, *grads):
+    S = jax.ShapeDtypeStruct
+    ANY = pl.BlockSpec(memory_space=pl.ANY)
+    D = pltpu.SemaphoreType.DMA
+    V = pltpu.VMEM
+    shapes = [g.shape for g in grads]
+    return pl.pallas_call(
+        finish_kernel,
+        out_shape=[S(out.shape, BF), S(ig.shape, F4)] + [S(s, F4) for s in shapes],
+        in_specs=[ANY] * 6,
+        out_specs=[ANY] * 6,
+        scratch_shapes=[V(s, BF) for s in shapes] + [V(s, F4) for s in shapes] + [V(out.shape, BF), V(ig.shape, F4), D((6,)), D((6,))],
+        compiler_params=pltpu.CompilerParams(vmem_limit_bytes=60 * MB),
+        name="finish",
+    )(out, ig, *grads)
 
 
 def own_local(tokens, pair_index, norm_gain, norm_shift, w_attention_in, w_attention_out, w_expand, w_contract, cotangent):
-    x = lax.axis_index("ctx") % 2
-    pairs = lax.dynamic_index_in_dim(pair_index, x, 0, False)
-    which = jnp.arange(8, dtype=jnp.int32)
-    inverse = jnp.sum(jnp.where(pairs[None, :] == which[:, None], which[None, :], 0), axis=1).astype(jnp.int32)
-    gs = jnp.concatenate([norm_gain[None], norm_shift[None], jnp.zeros((6, 256), BF)], axis=0).astype(F4)
+    gains = jnp.stack([norm_gain, norm_shift]).astype(F4)
     output, input_grad, vectors, *grads = block_call(
-        jnp.stack([inverse, pairs]), gs, tokens, cotangent, w_attention_in, w_attention_out, w_expand, w_contract)
-    return (output, input_grad, vectors[0], vectors[1], *(g.astype(F4) for g in grads[:4]))
+        pair_index, gains, tokens, cotangent, w_attention_in, w_attention_out, w_expand, w_contract)
+    output, input_grad, *grads = finish_call(output, input_grad, *grads[:4])
+    return (output, input_grad, vectors[0], vectors[1], *grads)
 
 
 def local(tokens, pair_index, norm_gain, norm_shift, w_attention_in, w_attention_out, w_expand, w_contract, cotangent):

time: 336 us -> 319 us (0.949)
  other arithmetic: 8.66 us -> 0.59 us
  local copies, waits for them, and re-layouts: 9.27 us -> 2.66 us
    pallas_call x1, Pallas kernels: 310 us -> 301 us  [block_call(): pl.pallas_call(block_kernel, out_shape=[S((2, 256, 2048), BF), S((2, 256,...]
    pallas_call x0 -> x1, Pallas kernels: none -> 7.83 us  [finish_call(): pl.pallas_call(finish_kernel, out_shape=[S(out.shape, BF), S(ig.shape, F4...]
    convert_element_type x5 -> x1, other arithmetic: 7.97 us -> 0.59 us  [own_local(): gains = jnp.stack([norm_gain, norm_shift]).astype(F4)]
    unnamed x12 -> x0, local copies, waits for them, and re-layouts: 6.49 us -> none
where the time goes in v5:
time: 319 us; the launch traced here: 313 us
  Pallas kernels  308 us (97%)
    pallas_call x1, Pallas kernels, block_call(): pl.pallas_call(block_kernel, out_shape=[S((2, 256, 2048), BF), S((2, 256,...  301 us
    pallas_call x1, Pallas kernels, finish_call(): pl.pallas_call(finish_kernel, out_shape=[S(out.shape, BF), S(ig.shape, F4...  7.83 us

profile of v5, /device:TPU:0, one launch (start us, length us, event | category | flops | bytes accessed | tf_op | source)
XLA Modules:
  0.0 312.6 jit_solution(493110631598365518)
XLA Ops:
  0.6 0.7 stack.9
  1.3 0.7 stack.10
  2.0 0.6 maximum_convert_fusion.gains
  2.5 300.7 %block.2 = (bf16[2,256,2048]{2,1,0:T(8,128)(2,1)}, f32[2,256,2048]{2,1,0:T(8,128)}, f32[8,256]{1,0:T(8,128)}, bf16[3,256,512]{2,1,0:T(8,128)(2,1)}, bf16[512,256...) custom-call(s32[2,8]{1,0:T(2,128)} %pairs_of.1, ...), custom_call_target="tpu_custom_call" | custom-call | tf_op jit(solution)/shard_map/block/pallas_call | solution.py:1288
  303.2 1.3 fusion
  304.5 7.8 %finish.1 = (bf16[2,256,2048]{2,1,0:T(8,128)(2,1)}, f32[2,256,2048]{2,1,0:T(8,128)}, f32[3,256,512]{2,1,0:T(8,128)}, f32[512,256]{1,0:T(8,128)}, f32[256,2048]{1,0:T(8,128)}, /*index=5*/f32[2048,256]{1,0:T(8,128)}) custom-call(bf16[2,256,2048]{2,1,0:T(8,128)(2,1)} %get-tuple-element.21.out, f32[2,256,2048]{2,1,0:T(8,128)} %get-tuple-element.22.ig, ...), custom_call_target="tpu_custom_call" | custom-call | tf_op jit(solution)/shard_map/finish/pallas_call | solution.py:1332
